TPU v7x, 32 devices: a whole 2x2x4 slice. The times are simulated.
32 devices in a mesh: blk: 16 (over z, y, core), head: 2 (over x).
Axes of the slice: x: 2, y: 2, z: 4, core: 2. Of those that a mesh axis runs over, the one named last changes fastest.
Arguments:
- queries: bfloat16 [512, 3072], P(('blk', 'head')), may hold values from -8 to 8
- query_tangent: bfloat16 [512, 3072], P(('blk', 'head')), may hold values from -3 to 3
- key_rows: bfloat16 [2048, 3072], P(('blk', 'head')), may hold values from -8 to 8
- key_tangent: bfloat16 [2048, 3072], P(('blk', 'head')), may hold values from -3 to 3
- value_rows: bfloat16 [2048, 3072], P(('blk', 'head')), may hold values from -24 to 24
- value_tangent: bfloat16 [2048, 3072], P(('blk', 'head')), may hold values from -3 to 3
- out_weight: bfloat16 [3072, 5120], P('head'), may hold values from -0.109375 to 0.109375
Outputs:
- projected: bfloat16 [512, 5120], P('blk', 'head')
- projected_tangent: bfloat16 [512, 5120], P('blk', 'head')
All inputs are finite; a program needn't handle non-finite values.
Results may differ from a plain program's by a relative error of at most 0.0107.
Values may be sent and summed in bfloat16 or wider, within the bound.
No kernel may reach another device: no remote copies, remote signals or barrier semaphores. Data moves between devices by JAX's collectives and lax.ppermute only.
A program may use at most 128 MiB of HBM per device.

v0:
```python
import math

import jax
import jax.numpy as jnp
from jax import lax
from jax.sharding import PartitionSpec as P

H = 24
DH = 128


def query_parts_of(queries, query_tangent):
    return (queries, query_tangent)


def tile_scores(query_parts, key_block, key_tangent):
    score_scale = DH ** (-0.5)
    scores = (
        jnp.einsum("qhd,khd->qhk", query_parts[0], key_block, preferred_element_type=jnp.float32)
        * score_scale
    )
    slopes = (
        jnp.einsum("qhd,khd->qhk", query_parts[1], key_block, preferred_element_type=jnp.float32)
        + jnp.einsum(
            "qhd,khd->qhk", query_parts[0], key_tangent, preferred_element_type=jnp.float32
        )
    ) * score_scale
    return (scores, slopes)


def weighted_sums(unnormed, slopes, value_block, value_tangent):
    tilted_full = unnormed * slopes
    weights = unnormed.astype(jnp.bfloat16)
    tilted = tilted_full.astype(jnp.bfloat16)
    value_sum = jnp.einsum("qhk,khd->qhd", weights, value_block, preferred_element_type=jnp.float32)
    tangent_sum = jnp.einsum(
        "qhk,khd->qhd", tilted, value_block, preferred_element_type=jnp.float32
    ) + jnp.einsum("qhk,khd->qhd", weights, value_tangent, preferred_element_type=jnp.float32)
    return (jnp.sum(unnormed, axis=2), jnp.sum(tilted_full, axis=2), value_sum, tangent_sum)


def local(queries, query_tangent, key_rows, key_tangent, value_rows, value_tangent, out_weight):
    head_count = H // lax.axis_size("head")
    local_width = head_count * DH
    regrouped = (
        lax.all_to_all(queries, "head", split_axis=1, concat_axis=0, tiled=True),
        lax.all_to_all(query_tangent, "head", split_axis=1, concat_axis=0, tiled=True),
        lax.all_to_all(key_rows, "head", split_axis=1, concat_axis=0, tiled=True),
        lax.all_to_all(key_tangent, "head", split_axis=1, concat_axis=0, tiled=True),
        lax.all_to_all(value_rows, "head", split_axis=1, concat_axis=0, tiled=True),
        lax.all_to_all(value_tangent, "head", split_axis=1, concat_axis=0, tiled=True),
    )
    local_query, local_qtan, local_key, local_ktan, local_value, local_vtan = regrouped
    row_count = local_query.shape[0]
    all_query, all_qtan = (
        lax.all_gather(local_query, "blk", axis=0, tiled=True),
        lax.all_gather(local_qtan, "blk", axis=0, tiled=True),
    )
    query_total = all_query.shape[0]
    block_rows = math.gcd(query_total, 512)
    block_count = query_total // block_rows
    query_blocks = all_query.reshape(block_count, block_rows, head_count, DH)
    qtan_blocks = all_qtan.reshape(block_count, block_rows, head_count, DH)
    key_count = local_key.shape[0]
    key_block = local_key.reshape(key_count, head_count, DH)
    key_tan_block = local_ktan.reshape(key_count, head_count, DH)
    value_block = local_value.reshape(key_count, head_count, DH)
    value_tan_block = local_vtan.reshape(key_count, head_count, DH)

    def block_sums(block_parts):
        query_block, qtan_block = block_parts
        query_parts = query_parts_of(query_block, qtan_block)
        scores, slopes = tile_scores(query_parts, key_block, key_tan_block)
        local_peak = jnp.max(scores, axis=2)
        unnormed = jnp.exp(scores - local_peak[..., None])
        sums = weighted_sums(unnormed, slopes, value_block, value_tan_block)
        return (local_peak,) + sums

    local_peak, part_total, part_slope, part_value, part_tangent = lax.map(
        block_sums, (query_blocks, qtan_blocks)
    )
    local_peak = local_peak.reshape(query_total, head_count)
    global_peak = lax.pmax(local_peak, "blk")
    factor = jnp.exp(local_peak - global_peak)
    summed = (
        lax.psum_scatter(
            part_value.reshape(query_total, head_count, DH) * factor[..., None],
            "blk",
            scatter_dimension=0,
            tiled=True,
        ),
        lax.psum_scatter(
            part_tangent.reshape(query_total, head_count, DH) * factor[..., None],
            "blk",
            scatter_dimension=0,
            tiled=True,
        ),
        lax.psum_scatter(
            part_total.reshape(query_total, head_count) * factor,
            "blk",
            scatter_dimension=0,
            tiled=True,
        ),
        lax.psum_scatter(
            part_slope.reshape(query_total, head_count) * factor,
            "blk",
            scatter_dimension=0,
            tiled=True,
        ),
    )
    value_sum = summed[0]
    tangent_sum = summed[1]
    row_total = summed[2]
    slope_sum = summed[3]
    normed = value_sum / row_total[..., None]
    tangent = tangent_sum / row_total[..., None] - (slope_sum / row_total)[..., None] * normed
    attended = normed.astype(jnp.bfloat16).reshape(row_count, local_width)
    attended_tangent = tangent.astype(jnp.bfloat16).reshape(row_count, local_width)
    combined = jnp.concatenate([attended, attended_tangent], axis=0)
    summed_out = lax.psum_scatter(
        lax.dot_general(
            out_weight, combined, (((0,), (1,)), ((), ())), preferred_element_type=jnp.float32
        ),
        "head",
        scatter_dimension=0,
        tiled=True,
    )
    projected = summed_out[:, :row_count].T.astype(jnp.bfloat16)
    projected_tangent = summed_out[:, row_count:].T.astype(jnp.bfloat16)
    return (projected, projected_tangent)


def solution(mesh):
    placed = (
        P(("blk", "head"), None),
        P(("blk", "head"), None),
        P(("blk", "head"), None),
        P(("blk", "head"), None),
        P(("blk", "head"), None),
        P(("blk", "head"), None),
        P("head", None),
    )
    return jax.shard_map(
        local,
        mesh=mesh,
        in_specs=placed,
        out_specs=(P("blk", "head"), P("blk", "head")),
        check_vma=False,
    )
```

profile of v0, /device:TPU:0, one launch (start us, length us, event | category | flops | bytes accessed | tf_op | source)
XLA Modules:
  0.0 428.5 jit_solution(10977241088829421368)
XLA Ops:
  8.2 8.4 %all_to_all.102 = bf16[16,2,1536]{2,0,1:T(8,128)(2,1)} all-to-all(bf16[16,2,1536]{2,0,1:T(8,128)(2,1)S(1)} %bitcast.88), channel_id=1, replica_groups=mesh['blk'=16,'head'=2] {'head'}, dimensions={1} | all-to-all | bytes 196608 | tf_op jit(solution)/shard_map/all_to_all | solution.py:46
  17.6 7.3 %all_to_all.103 = bf16[16,2,1536]{2,0,1:T(8,128)(2,1)} all-to-all(bf16[16,2,1536]{2,0,1:T(8,128)(2,1)S(1)} %bitcast.89), channel_id=1, replica_groups=mesh['blk'=16,'head'=2] {'head'}, dimensions={1} | all-to-all | bytes 196608 | tf_op jit(solution)/shard_map/all_to_all | solution.py:47
  26.7 3.5 all-to-all-start
  32.0 4.1 all-to-all-done
  36.0 3.5 all-to-all-start.4
  42.1 3.2 all-to-all-done.4
  45.4 4.2 all-to-all-start.2
  50.7 6.5 %all-gather.3.cloned.1.call-done = bf16[512,1536]{1,0:T(8,128)(2,1)} async-done(((bf16[32,1536]{1,0:T(8,128)(2,1)}), bf16[512,1536]{1,0:T(8,128)(2,1)}) %all-gather.3.cloned.1.call-update) | async-done | bytes 1572880 | tf_op jit(solution)/shard_map/all_gather | solution.py:56
  57.2 2.6 copy.56
  61.9 60.0 %pmax.7 = f32[512,12]{0,1:T(8,128)S(1)} all-reduce(f32[512,12]{0,1:T(8,128)S(1)} %get-tuple-element.32), channel_id=1, replica_groups=mesh['blk'=16,'head'=2] {'blk'}, use_global_device_ids=true, to_apply=%region_1.0 | all-reduce | flops 6144 | bytes 49152 | tf_op jit(solution)/shard_map/pmax | solution.py:83
  121.9 2.6 copy.64
  124.5 2.3 fusion.9
  126.8 2.4 fusion.23
  129.8 4.2 all-to-all-start.5
  137.1 2.9 all-to-all-done.5
  143.0 2.2 fusion.3
  145.2 3.1 bitcast_multiply_fusion
  148.4 4.0 bitcast_multiply_fusion.2
  152.4 39.0 %reduce-scatter.18.cloned.1.call-done = f32[32,12]{1,0:T(8,128)} async-done(((f32[512,12]{1,0:T(8,128)}), f32[32,12]{1,0:T(8,128)}) %reduce-scatter.18.cloned.1.call-update) | async-done | bytes 1552
  192.2 56.9 %reduce-scatter.16.cloned.1.call-done = f32[32,12]{1,0:T(8,128)} async-done(((f32[512,12]{1,0:T(8,128)}), f32[32,12]{1,0:T(8,128)}) %reduce-scatter.16.cloned.1.call-update) | async-done | bytes 1552
  250.0 68.1 %reduce-scatter.12.cloned.1.call-done = f32[32,12,128]{2,0,1:T(8,128)} async-done(((f32[512,12,128]{2,0,1:T(8,128)}), f32[32,12,128]{2,0,1:T(8,128)}) %reduce-scatter.12.cloned.1.call-update) | async-done | bytes 196624 | tf_op jit(solution)/shard_map/reduce_scatter | solution.py:92
  318.0 68.7 %reduce-scatter.10.cloned.1.call-done = f32[32,12,128]{2,0,1:T(8,128)} async-done(((f32[512,12,128]{2,0,1:T(8,128)}), f32[32,12,128]{2,0,1:T(8,128)}) %reduce-scatter.10.cloned.1.call-update) | async-done | bytes 196624 | tf_op jit(solution)/shard_map/reduce_scatter | solution.py:86
  388.0 9.5 %convolution_bitcast_fusion = f32[5120,64]{0,1:T(8,128)} fusion(bf16[1536,5120]{1,0:T(8,128)(2,1)} %param.13, bf16[32,1536]{1,0:T(8,128)(2,1)S(1)} %get-tuple-element.48, bf16[32,1536]{1,0:T(8,128)(2,1)S(1)} %get-tuple-element.49), kind=kOutput, calls=%fused_computation | convolution fusion | flops 1007026176 | bytes 17235968 | tf_op jit(solution)/shard_map/dot_general | solution.py:121
  397.5 22.3 %reduce-scatter.14.cloned.1.call-done = f32[2560,64]{0,1:T(8,128)} async-done(((f32[5120,64]{0,1:T(8,128)}), f32[2560,64]{0,1:T(8,128)}) %reduce-scatter.14.cloned.1.call-update) | async-done | bytes 655376 | tf_op jit(solution)/shard_map/reduce_scatter | solution.py:120
  (49 shorter events, 22.9 us)
Async XLA Ops:
  7.2 32.4 %copy-start.3 = (bf16[64,3072]{1,0:T(8,128)(2,1)S(1)}, bf16[64,3072]{1,0:T(8,128)(2,1)}, u32[]{:S(2)}) copy-start(bf16[64,3072]{1,0:T(8,128)(2,1)} %param.11) | copy-start | bytes 1179652
  7.2 33.1 %copy-start.4 = (bf16[64,3072]{1,0:T(8,128)(2,1)S(1)}, bf16[64,3072]{1,0:T(8,128)(2,1)}, u32[]{:S(2)}) copy-start(bf16[64,3072]{1,0:T(8,128)(2,1)} %param.12) | copy-start | bytes 1179652
  7.2 50.0 %all-gather.3.cloned.1.call-start = ((), (), s32[]{:S(2)}) async-start(), calls=%async_computation.11 | async-start | bytes 1671168 | tf_op jit(solution)/shard_map/all_gather | solution.py:56
  16.6 105.3 %all-gather.5.cloned.1.call-start = ((), (), s32[]{:S(2)}) async-start(), calls=%async_computation.13 | async-start | bytes 1671168 | tf_op jit(solution)/shard_map/all_gather | solution.py:57
  26.7 9.3 %all-to-all-start = ((bf16[64,2,1536]{2,0,1:T(8,128)(2,1)}), bf16[64,2,1536]{2,0,1:T(8,128)(2,1)S(1)}, u32[]{:S(2)}, u32[]{:S(2)}) async-start(bf16[64,2,1536]{2,0,1:T(8,128)(2,1)} %bitcast.73), calls=%async_computation | async-start | bytes 786432 | tf_op jit(solution)/shard_map/all_to_all | solution.py:48
  36.0 9.3 %all-to-all-start.4 = ((bf16[64,2,1536]{2,0,1:T(8,128)(2,1)}), bf16[64,2,1536]{2,0,1:T(8,128)(2,1)S(1)}, u32[]{:S(2)}, u32[]{:S(2)}) async-start(bf16[64,2,1536]{2,0,1:T(8,128)(2,1)} %bitcast.71), calls=%async_computation.5 | async-start | bytes 786432 | tf_op jit(solution)/shard_map/all_to_all | solution.py:49
  45.4 84.4 %all-to-all-start.2 = ((bf16[64,2,1536]{2,0,1:T(8,128)(2,1)}), bf16[64,2,1536]{2,0,1:T(8,128)(2,1)}, u32[]{:S(2)}, u32[]{:S(2)}) async-start(bf16[64,2,1536]{2,0,1:T(8,128)(2,1)} %bitcast.72), calls=%async_computation.2 | async-start | bytes 786432 | tf_op jit(solution)/shard_map/all_to_all | solution.py:50
  124.5 2.3 copy-start
  124.5 2.3 copy-start.1
  129.8 10.1 %all-to-all-start.5 = ((bf16[64,2,1536]{2,0,1:T(8,128)(2,1)}), bf16[64,2,1536]{2,0,1:T(8,128)(2,1)}, u32[]{:S(2)}, u32[]{:S(2)}) async-start(bf16[64,2,1536]{2,0,1:T(8,128)(2,1)} %bitcast.79), calls=%async_computation.6 | async-start | bytes 786432 | tf_op jit(solution)/shard_map/all_to_all | solution.py:51
  134.0 57.4 %reduce-scatter.18.cloned.1.call-start = ((), (), s32[]{:S(2)}) async-start(), calls=%async_computation.17 | async-start | bytes 278528
  134.9 114.2 %reduce-scatter.16.cloned.1.call-start = ((), (), s32[]{:S(2)}) async-start(), calls=%async_computation.16 | async-start | bytes 278528
  142.9 175.1 %reduce-scatter.12.cloned.1.call-start = ((), (), s32[]{:S(2)}) async-start(), calls=%async_computation.14 | async-start | bytes 3342336 | tf_op jit(solution)/shard_map/reduce_scatter | solution.py:92
  143.0 2.2 copy-start.2
  148.3 238.4 %reduce-scatter.10.cloned.1.call-start = ((), (), s32[]{:S(2)}) async-start(), calls=%async_computation.12 | async-start | bytes 3342336 | tf_op jit(solution)/shard_map/reduce_scatter | solution.py:86
  152.3 267.4 %reduce-scatter.14.cloned.1.call-start = ((), (), s32[]{:S(2)}) async-start(), calls=%async_computation.15 | async-start | bytes 1966080 | tf_op jit(solution)/shard_map/reduce_scatter | solution.py:120
Sparse Core Ops, SparseCore 0:
  16.7 40.3 all-gather.2
  59.4 38.5 all-gather.4
  138.3 53.0 reduce-scatter.17
  194.8 54.3 reduce-scatter.15
  252.8 65.1 reduce-scatter.11
  321.7 65.0 reduce-scatter.9
  397.6 22.0 reduce-scatter.13
where the time goes:
time: 429 us; the launch traced here: 428 us
  waiting for transfers between devices  272 us (63%)
  blocking collectives  75.8 us (18%)
  matrix products  25.6 us (6%)
  local copies, waits for them, and re-layouts  22.6 us (5%)
  starting transfers between devices  15.5 us (4%)
  between operations  14.3 us (3%)
    unnamed x9, waiting for transfers between devices  96.1 us
    reduce_scatter x1, waiting for transfers between devices, local(): lax.psum_scatter(part_value.reshape(query_total, head_count, DH) * factor...  68.7 us
    reduce_scatter x1, waiting for transfers between devices, local(): lax.psum_scatter(part_tangent.reshape(query_total, head_count, DH) * fact...  68.1 us
    pmax x1, blocking collectives, local(): global_peak = lax.pmax(local_peak, 'blk')  60 us
    reduce_scatter x1, waiting for transfers between devices, local(): lax.psum_scatter(lax.dot_general(out_weight, combined, (((0,), (1,)), (()...  22.3 us
    dot_general x1, matrix products, local(): lax.dot_general(out_weight, combined, (((0,), (1,)), ((), ())), preferred...  9.51 us
  transfers between devices with their start and end apart: 11, of which 9 were waited for; matrix products, arithmetic and copies ran while one was open for 9% of the time, Pallas kernels for 0%

commit v1 on v0

v1 whole, which is shorter than its diff:
```python
import functools
import math

import jax
import jax.numpy as jnp
from jax import lax
from jax.experimental import pallas as pl
from jax.experimental.pallas import tpu as pltpu
from jax.sharding import Mesh, PartitionSpec as P

H = 24
DH = 128
NT = (((1,), (1,)), ((), ()))
STATS = 5


def split_bf16(x, parts):
    terms = []
    for _ in range(parts):
        term = x.astype(jnp.bfloat16)
        terms.append(term)
        x = x - term.astype(jnp.float32)
    return terms


def attend_kernel(heads, planes_of, row_len, plane_ref, *refs):
    query_refs, (kv_ref, out_ref) = refs[:-2], refs[-2:]
    h = pl.program_id(0)
    group, _, key_rows, _ = kv_ref.shape
    keys = group * key_rows
    g_count, head_axis = out_ref.shape[1], out_ref.shape[2] // row_len
    key, key_tan, value, value_tan = (kv_ref[:, t].reshape(keys, DH) for t in range(4))
    key_pair = jnp.concatenate([key, key_tan], axis=1)
    value_pair = jnp.concatenate([value, value_tan], axis=1)
    scale = DH ** (-0.5)
    data = pl.ds(pl.multiple_of(h * 2 * DH, 2 * DH), 2 * DH)
    tail = pl.ds(heads * 2 * DH, DH)

    def one_plane(q_ref, j, plane):
        rows = group * row_len
        query = q_ref[j, :, 0].reshape(rows, DH)
        qtan = q_ref[j, :, 1].reshape(rows, DH)
        scores = lax.dot_general(query, key, NT, preferred_element_type=jnp.float32) * scale
        slopes = (
            lax.dot_general(
                jnp.concatenate([qtan, query], axis=1),
                key_pair,
                NT,
                preferred_element_type=jnp.float32,
            )
            * scale
        )
        peak = jnp.max(scores, axis=1, keepdims=True)
        unnormed = jnp.exp(scores - peak)
        tilted = unnormed * slopes
        total = jnp.sum(unnormed, axis=1, keepdims=True)
        slope_sum = jnp.sum(tilted, axis=1, keepdims=True)
        sums = jnp.dot(
            unnormed.astype(jnp.bfloat16), value_pair, preferred_element_type=jnp.float32
        )
        tilted_sum = jnp.dot(
            tilted.astype(jnp.bfloat16), value, preferred_element_type=jnp.float32
        )
        inv = 1.0 / total
        mean_slope = slope_sum * inv
        mean_value = sums[:, :DH] * inv
        tangent = (sums[:, DH:] + tilted_sum) * inv - mean_slope * mean_value
        both = jnp.concatenate([mean_value, tangent], axis=1).astype(jnp.bfloat16)
        lse = peak + jnp.log(total)
        stats = split_bf16(lse, 3) + split_bf16(mean_slope, 2)
        lane = lax.broadcasted_iota(jnp.int32, (rows, DH), 1)
        packed = jnp.zeros((rows, DH), jnp.float32)
        for i, stat in enumerate(stats):
            packed = jnp.where(lane == i * heads + h, stat.astype(jnp.float32), packed)
        for x in range(head_axis):
            for g in range(g_count):
                here = slice((x * g_count + g) * row_len, (x * g_count + g + 1) * row_len)
                there = pl.ds(x * row_len, row_len)
                out_ref[plane, g, there, data] = both[here]
                before = jnp.where(
                    h == 0, 0.0, out_ref[plane, g, there, tail].astype(jnp.float32)
                )
                out_ref[plane, g, there, tail] = (before + packed[here]).astype(jnp.bfloat16)

    for i, q_ref in enumerate(query_refs):
        count = q_ref.shape[0]
        if count == 1:
            one_plane(q_ref, 0, planes_of(plane_ref[0], i))
        else:
            pl.loop(0, count)(lambda j, q_ref=q_ref: one_plane(q_ref, j, j))


def attend(queries, kv, plane, planes_of, k, g_count, head_axis):
    group, _, key_rows, width = kv.shape
    heads = width // DH
    row_len = queries[0].shape[3]
    out_shape = (k, g_count, head_axis * row_len, heads * 2 * DH + DH)

    def by_head(*shape):
        return pl.BlockSpec(shape + (DH,), lambda h, _: (0,) * len(shape) + (h,))

    return pl.pallas_call(
        functools.partial(attend_kernel, heads, planes_of, row_len),
        out_shape=jax.ShapeDtypeStruct(out_shape, jnp.bfloat16),
        grid_spec=pltpu.PrefetchScalarGridSpec(
            num_scalar_prefetch=1,
            grid=(heads,),
            in_specs=[by_head(*q.shape[:-1]) for q in queries] + [by_head(*kv.shape[:-1])],
            out_specs=pl.BlockSpec(out_shape, lambda h, _: (0, 0, 0, 0)),
        ),
        compiler_params=pltpu.CompilerParams(vmem_limit_bytes=48 * 2**20),
        name="attend",
    )(plane, *queries, kv)


def merge(parts_ref, both_ref, heads):
    k, g_count, rows, _ = parts_ref.shape
    tail = heads * 2 * DH
    for g in range(g_count):
        stats = [parts_ref[j, g, :, tail : tail + DH].astype(jnp.float32) for j in range(k)]
        for h in range(heads):

            def stat(j, i):
                return stats[j][:, i * heads + h : i * heads + h + 1]

            lse = [stat(j, 0) + stat(j, 1) + stat(j, 2) for j in range(k)]
            slope = [stat(j, 3) + stat(j, 4) for j in range(k)]
            top = functools.reduce(jnp.maximum, lse)
            share = [jnp.exp(e - top) for e in lse]
            inv = 1.0 / sum(share)
            share = [e * inv for e in share]
            mean_slope = sum(e * s for e, s in zip(share, slope))
            value = jnp.zeros((rows, DH), jnp.float32)
            tangent = jnp.zeros((rows, DH), jnp.float32)
            for j in range(k):
                col = h * 2 * DH
                part = parts_ref[j, g, :, col : col + DH].astype(jnp.float32)
                part_tan = parts_ref[j, g, :, col + DH : col + 2 * DH].astype(jnp.float32)
                value += share[j] * part
                tangent += share[j] * part_tan + (share[j] * (slope[j] - mean_slope)) * part
            col = (g * heads + h) * DH
            both_ref[:rows, col : col + DH] = value.astype(jnp.bfloat16)
            both_ref[rows:, col : col + DH] = tangent.astype(jnp.bfloat16)


def first_kernel(heads, half_ref, parts_ref, weight_ref, out_ref, both_ref):
    @pl.when(pl.program_id(0) == 0)
    def _():
        merge(parts_ref, both_ref, heads)

    out_ref[...] = jnp.dot(
        both_ref[...], weight_ref[...], preferred_element_type=jnp.float32
    ).astype(out_ref.dtype)


def second_kernel(half_ref, both_ref, weight_ref, out_ref):
    out_ref[...] = jnp.dot(
        both_ref[...], weight_ref[...], preferred_element_type=jnp.float32
    ).astype(out_ref.dtype)


def project(kernel, half, left, weight, width, dtype, both, tile=512):
    depth = weight.shape[0]
    steps = width // tile
    fixed = pl.BlockSpec(left.shape, lambda n, s: (0,) * left.ndim)
    column = pl.BlockSpec((depth, tile), lambda n, s: (0, s[0] * steps + n))
    rows = both[0]
    outs = [jax.ShapeDtypeStruct((rows, width), dtype)]
    out_specs = [pl.BlockSpec((rows, tile), lambda n, s: (0, n))]
    if left.ndim > 2:
        outs.append(jax.ShapeDtypeStruct(both, jnp.bfloat16))
        out_specs.append(pl.BlockSpec(both, lambda n, s: (0, 0)))
    return pl.pallas_call(
        kernel,
        out_shape=outs,
        grid_spec=pltpu.PrefetchScalarGridSpec(
            num_scalar_prefetch=1,
            grid=(steps,),
            in_specs=[fixed, column],
            out_specs=out_specs,
        ),
        compiler_params=pltpu.CompilerParams(vmem_limit_bytes=48 * 2**20),
        cost_estimate=pl.CostEstimate(
            flops=2 * rows * depth * width, bytes_accessed=2 * depth * width, transcendentals=0
        ),
        name="project",
    )(half, left, weight)


def pack(group, *matrices):
    stacked = jnp.stack(matrices)
    count, rows, columns = stacked.shape
    return stacked.reshape(count, rows, group, columns // group).transpose(2, 0, 1, 3)


def local(queries, query_tangent, key_rows, key_tangent, value_rows, value_tangent, out_weight):
    k, g_count, head_axis = (lax.axis_size(a) for a in ("k", "g", "head"))
    plane_axes = ("head", "g")
    group = g_count * head_axis
    heads = H // group
    rows = queries.shape[0] * head_axis

    def within_plane(x):
        return lax.all_to_all(x, plane_axes, split_axis=0, concat_axis=0, tiled=True)

    plane_queries = within_plane(pack(group, queries, query_tangent))
    kv = within_plane(pack(group, key_rows, key_tangent, value_rows, value_tangent))
    if k in (2, 4, 8):
        all_queries = [plane_queries[None]] + [
            lax.ppermute(plane_queries, "k", [(i, i ^ d) for i in range(k)])[None]
            for d in range(1, k)
        ]
    else:
        all_queries = [lax.all_gather(plane_queries, "k", axis=0, tiled=False)]

    plane = lax.axis_index("k").astype(jnp.int32).reshape(1)
    parts = attend(all_queries, kv, plane, lambda z, d: z ^ d, k, g_count, head_axis)
    parts = parts.reshape((k * g_count,) + parts.shape[2:])
    parts = lax.all_to_all(parts, ("k", "g"), split_axis=0, concat_axis=0, tiled=True)
    parts = parts.reshape((k, g_count) + parts.shape[1:])

    width = out_weight.shape[1] // head_axis
    both_shape = (2 * rows, out_weight.shape[0])
    mine = lax.axis_index("head").astype(jnp.int32).reshape(1)
    merging = functools.partial(first_kernel, heads)
    if head_axis == 2:
        sent, both = project(
            merging, 1 - mine, parts, out_weight, width, jnp.bfloat16, both_shape
        )
        received = lax.ppermute(sent, "head", [(0, 1), (1, 0)])
        (own,) = project(
            second_kernel, mine, both, out_weight, width, jnp.float32, both_shape
        )
        total = own + received.astype(jnp.float32)
    else:
        partial, _ = project(
            merging, 0 * mine, parts, out_weight, width * head_axis, jnp.float32, both_shape
        )
        total = lax.psum_scatter(partial, "head", scatter_dimension=1, tiled=True)
    total = total.astype(jnp.bfloat16)
    return (total[:rows], total[rows:])


def solution(mesh):
    blk, head_axis = mesh.shape["blk"], mesh.shape["head"]
    g_count = math.gcd(H // head_axis, blk)
    fine = Mesh(mesh.devices.reshape(blk // g_count, g_count, head_axis), ("k", "g", "head"))
    rows = P(("k", "g", "head"), None)
    return jax.shard_map(
        local,
        mesh=fine,
        in_specs=(rows,) * 6 + (P("head", None),),
        out_specs=(P(("k", "g"), "head"),) * 2,
        check_vma=False,
    )
```

time: 429 us -> 89.9 us (0.21)
  waiting for transfers between devices: 272 us -> 42.4 us
  blocking collectives: 75.8 us -> 0 us
  matrix products: 25.6 us -> 0 us
  Pallas kernels: 0 us -> 19.2 us
  local copies, waits for them, and re-layouts: 22.6 us -> 3.85 us
  between operations: 14.3 us -> 0.81 us
  starting transfers between devices: 15.5 us -> 20.9 us
    reduce_scatter x3 -> x0, waiting for transfers between devices: 159 us -> none  [the longest x1 68.7 us: local(): lax.psum_scatter(part_value.reshape(query_total, head_count, DH) * factor...]
    unnamed x9 -> x0, waiting for transfers between devices: 96.1 us -> none
    pmax x1 -> x0, blocking collectives: 60 us -> none  [local(): global_peak = lax.pmax(local_peak, 'blk')]
    dot_general x7 -> x0, matrix products: 25.6 us -> none  [the longest x1 9.51 us: local(): lax.dot_general(out_weight, combined, (((0,), (1,)), ((), ())), preferred...]
    pallas_call x0 -> x3, Pallas kernels: none -> 19.2 us  [the longest x2 13 us: project(): pl.pallas_call(kernel, out_shape=outs, grid_spec=pltpu.PrefetchScalarGrid...]
    ppermute x0 -> x4, waiting for transfers between devices: none -> 17.4 us  [the longest x3 14.3 us: local(): lax.ppermute(plane_queries, 'k', [(i, i ^ d) for i in range(k)])[None]]
    all_to_all x2 -> x0, blocking collectives: 15.7 us -> none  [the longest x1 8.4 us: local(): lax.all_to_all(queries, 'head', split_axis=1, concat_axis=0, tiled=True)]
    all_to_all x4 -> x3, waiting for transfers between devices: 10.2 us -> 25 us  [the longest x1 20.8 us: local(): lax.all_to_all(parts, ('k', 'g'), split_axis=0, concat_axis=0, tiled=True)]
  transfers between devices with their start and end apart: 11 -> 7, of which waited for: 9 -> 6; matrix products, arithmetic and copies ran while one was open for 9% -> 2% of each run, Pallas kernels for 0% -> 6%
where the time goes in v1:
time: 89.9 us; the launch traced here: 89.3 us
  waiting for transfers between devices  42.4 us (47%)
  starting transfers between devices  20.9 us (23%)
  Pallas kernels  19.2 us (21%)
  local copies, waits for them, and re-layouts  3.85 us (4%)
  other arithmetic  2.16 us (2%)
    all_to_all x1, waiting for transfers between devices, local(): lax.all_to_all(parts, ('k', 'g'), split_axis=0, concat_axis=0, tiled=True)  20.8 us
    ppermute x3, waiting for transfers between devices, local(): lax.ppermute(plane_queries, 'k', [(i, i ^ d) for i in range(k)])[None]  14.3 us
    pallas_call x2, Pallas kernels, project(): pl.pallas_call(kernel, out_shape=outs, grid_spec=pltpu.PrefetchScalarGrid...  13 us
    all_to_all x2, starting transfers between devices, within_plane(): lax.all_to_all(x, plane_axes, split_axis=0, concat_axis=0, tiled=True)  8.75 us
    pallas_call x1, Pallas kernels, attend(): pl.pallas_call(functools.partial(attend_kernel, heads, planes_of, row_len...  6.17 us
    all_to_all x1, starting transfers between devices, local(): lax.all_to_all(parts, ('k', 'g'), split_axis=0, concat_axis=0, tiled=True)  6.17 us
    ppermute x3, starting transfers between devices, local(): lax.ppermute(plane_queries, 'k', [(i, i ^ d) for i in range(k)])[None]  4.45 us
    all_to_all x2, waiting for transfers between devices, within_plane(): lax.all_to_all(x, plane_axes, split_axis=0, concat_axis=0, tiled=True)  4.19 us
  transfers between devices with their start and end apart: 7, of which 6 were waited for; matrix products, arithmetic and copies ran while one was open for 2% of the time, Pallas kernels for 6%

profile of v1, /device:TPU:0, one launch (start us, length us, event | category | flops | bytes accessed | tf_op | source)
XLA Modules:
  0.0 89.3 jit_solution(5370337767079422681)
XLA Ops:
  0.7 1.0 %copy.16 = bf16[2,8,8,384]{3,2,1,0:T(8,128)(2,1)S(1)} copy(bf16[2,8,8,384]{3,1,2,0:T(8,128)(2,1)} %bitcast.45) | data formatting | bytes 196608
  1.7 0.9 %copy.15 = bf16[2,8,8,384]{3,2,1,0:T(8,128)(2,1)S(1)} copy(bf16[2,8,8,384]{3,1,2,0:T(8,128)(2,1)} %bitcast.46) | data formatting | bytes 196608
  2.6 0.7 maximum_bitcast_fusion.1
  3.3 5.2 %all-to-all-start = ((bf16[8,2,16,384]{3,2,1,0:T(8,128)(2,1)}), bf16[8,2,16,384]{3,2,1,0:T(8,128)(2,1)S(1)}, u32[]{:S(2)}, u32[]{:S(2)}) async-start(bf16[8,2,16,384]{3,2,1,0:T(8,128)(2,1)} %maximum_bitcast_fusion.1), calls=%async_computation | async-start | bytes 393216 | tf_op jit(solution)/shard_map/all_to_all | solution.py:204
  8.7 0.7 copy-done.2
  9.6 0.1 copy-done.3
  9.7 1.4 %maximum_bitcast_fusion = bf16[8,4,64,384]{3,2,1,0:T(8,128)(2,1)} fusion(bf16[1,64,8,384]{3,1,0,2:T(8,128)(2,1)S(1)} %copy.14, bf16[1,64,8,384]{3,1,0,2:T(8,128)(2,1)S(1)} %copy.13, bf16[1,64,8,384]{3,1,0,2:T(8,128)(2,1)S(1)} %copy.12, bf16[1,64,8,384]{3,1,0,2:T(8,128)(2,1)S(1)} %copy.11), kind=kLoop, calls=%fused_computation | loop fusion | flops 2359296 | bytes 3145728 | tf_op jit(solution)/shard_map/transpose | solution.py:193
  11.1 3.0 %all-to-all-done = bf16[8,2,16,384]{3,2,1,0:T(8,128)(2,1)S(1)} async-done(((bf16[8,2,16,384]{3,2,1,0:T(8,128)(2,1)}), bf16[8,2,16,384]{3,2,1,0:T(8,128)(2,1)S(1)}, u32[]{:S(2)}, u32[]{:S(2)}) %all-to-all-start) | async-done | bytes 196640 | tf_op jit(solution)/shard_map/all_to_all | solution.py:204
  14.1 3.6 %all-to-all-start.1 = ((bf16[8,4,64,384]{3,2,1,0:T(8,128)(2,1)}), bf16[8,4,64,384]{3,2,1,0:T(8,128)(2,1)S(1)}, u32[]{:S(2)}, u32[]{:S(2)}) async-start(bf16[8,4,64,384]{3,2,1,0:T(8,128)(2,1)} %maximum_bitcast_fusion), calls=%async_computation.1 | async-start | bytes 3145728 | tf_op jit(solution)/shard_map/all_to_all | solution.py:204
  17.7 1.6 %collective-permute-start = (bf16[8,2,16,384]{3,2,1,0:T(8,128)(2,1)S(1)}, bf16[8,2,16,384]{3,2,1,0:T(8,128)(2,1)S(1)}, u32[]{:S(2)}, u32[]{:S(2)}) collective-permute-start(bf16[8,2,16,384]{3,2,1,0:T(8,128)(2,1)S(1)} %all-to-all-done), channel_id=1, source_target_pairs={{0,8},{8,0},{16,24},{24,16},{1,9},{9,1},{17,25},{25,17},{2,10},{10... | collective-permute-start | bytes 589832 | tf_op jit(solution)/shard_map/ppermute | solution.py:210
  19.3 2.6 %collective-permute-start.1 = (bf16[8,2,16,384]{3,2,1,0:T(8,128)(2,1)S(1)}, bf16[8,2,16,384]{3,2,1,0:T(8,128)(2,1)S(1)}, u32[]{:S(2)}, u32[]{:S(2)}) collective-permute-start(bf16[8,2,16,384]{3,2,1,0:T(8,128)(2,1)S(1)} %all-to-all-done), channel_id=1, source_target_pairs={{0,16},{8,24},{16,0},{24,8},{1,17},{9,25},{17,1},{25,9},{2,18},{10... | collective-permute-start | bytes 589832 | tf_op jit(solution)/shard_map/ppermute | solution.py:210
  21.9 0.2 collective-permute-start.2
  22.2 6.5 %collective-permute-done = bf16[8,2,16,384]{3,2,1,0:T(8,128)(2,1)S(1)} collective-permute-done((bf16[8,2,16,384]{3,2,1,0:T(8,128)(2,1)S(1)}, bf16[8,2,16,384]{3,2,1,0:T(8,128)(2,1)S(1)}, u32[]{:S(2)}, u32[]{:S(2)}) %collective-permute-start) | collective-permute-done | bytes 196640 | tf_op jit(solution)/shard_map/ppermute | solution.py:210
  28.6 7.9 %collective-permute-done.1 = bf16[8,2,16,384]{3,2,1,0:T(8,128)(2,1)S(1)} collective-permute-done((bf16[8,2,16,384]{3,2,1,0:T(8,128)(2,1)S(1)}, bf16[8,2,16,384]{3,2,1,0:T(8,128)(2,1)S(1)}, u32[]{:S(2)}, u32[]{:S(2)}) %collective-permute-start.1) | collective-permute-done | bytes 196640 | tf_op jit(solution)/shard_map/ppermute | solution.py:210
  36.5 1.2 %all-to-all-done.1.refs_4_ = bf16[8,4,64,384]{3,2,1,0:T(8,128)(2,1)S(1)} async-done(((bf16[8,4,64,384]{3,2,1,0:T(8,128)(2,1)}), bf16[8,4,64,384]{3,2,1,0:T(8,128)(2,1)S(1)}, u32[]{:S(2)}, u32[]{:S(2)}) %all-to-all-start.1) | async-done | bytes 1572896 | tf_op jit(solution)/shard_map/all_to_all | solution.py:204
  37.7 6.2 %attend.1 = bf16[4,4,32,896]{3,2,1,0:T(8,128)(2,1)} custom-call(s32[1]{0:T(128)} %bitcast.1.plane_ref, bf16[1,8,2,16,384]{4,3,2,1,0:T(8,128)(2,1)S(1)} %bitcast.31, bf16[1,8,2,16,384]{4,3,2,1,0:T(8,128)(2,1)S(1)} %bitcast.32, bf16[1,8,2,16,384]{4,3,2,1,0:T(8,128)(2,1)S(1)} %bitcast.33, bf16[1,8,2,16,384]{4,3,2,1,0:T(8,128)(2,1)S(1)} %bitcast.34, ...), custom_call_target="tpu_custom_call" | custom-call | tf_op jit(solution)/shard_map/attend/pallas_call | solution.py:102
  43.9 6.2 %all-to-all-start.2 = ((bf16[16,32,896]{2,1,0:T(8,128)(2,1)}), bf16[16,32,896]{2,1,0:T(8,128)(2,1)S(1)}, u32[]{:S(2)}, u32[]{:S(2)}) async-start(bf16[16,32,896]{2,1,0:T(8,128)(2,1)} %bitcast.8), calls=%async_computation.2 | async-start | bytes 1835008 | tf_op jit(solution)/shard_map/all_to_all | solution.py:219
  50.1 20.8 %all-to-all-done.2 = bf16[16,32,896]{2,1,0:T(8,128)(2,1)S(1)} async-done(((bf16[16,32,896]{2,1,0:T(8,128)(2,1)}), bf16[16,32,896]{2,1,0:T(8,128)(2,1)S(1)}, u32[]{:S(2)}, u32[]{:S(2)}) %all-to-all-start.2) | async-done | bytes 917536 | tf_op jit(solution)/shard_map/all_to_all | solution.py:219
  70.9 7.5 %project.2 = (bf16[64,2560]{1,0:T(8,128)(2,1)S(1)}, bf16[64,1536]{1,0:T(8,128)(2,1)S(1)}) custom-call(s32[1]{0:T(128)S(6)} %sub.3.half_ref, bf16[4,4,32,896]{3,2,1,0:T(8,128)(2,1)S(1)} %bitcast.30, bf16[1536,5120]{1,0:T(8,128)(2,1)} %weight_ref.3), custom_call_target="tpu_custom_call" | custom-call | flops 503316480 | bytes 7864320 | tf_op jit(solution)/shard_map/project/pallas_call | solution.py:173
  78.4 1.6 %collective-permute-start.3 = (bf16[64,2560]{1,0:T(8,128)(2,1)S(1)}, bf16[64,2560]{1,0:T(8,128)(2,1)S(1)}, u32[]{:S(2)}, u32[]{:S(2)}) collective-permute-start(bf16[64,2560]{1,0:T(8,128)(2,1)S(1)} %get-tuple-element.5), channel_id=1, source_target_pairs={{0,1},{1,0},{2,3},{3,2},{4,5},{5,4},{6,7},{7,6},{8,9},{9,8},{10,11... | collective-permute-start | bytes 983048 | tf_op jit(solution)/shard_map/ppermute | solution.py:230
  79.9 5.5 %project.3 = f32[64,2560]{1,0:T(8,128)S(1)} custom-call(s32[1]{0:T(128)} %bitcast.half_ref, bf16[64,1536]{1,0:T(8,128)(2,1)S(1)} %get-tuple-element.4.both_ref, bf16[1536,5120]{1,0:T(8,128)(2,1)} %weight_ref.3), custom_call_target="tpu_custom_call" | custom-call | flops 503316480 | bytes 7864320 | tf_op jit(solution)/shard_map/project/pallas_call | solution.py:173
  85.4 3.0 %collective-permute-done.3 = bf16[64,2560]{1,0:T(8,128)(2,1)S(1)} collective-permute-done((bf16[64,2560]{1,0:T(8,128)(2,1)S(1)}, bf16[64,2560]{1,0:T(8,128)(2,1)S(1)}, u32[]{:S(2)}, u32[]{:S(2)}) %collective-permute-start.3) | collective-permute-done | bytes 327712 | tf_op jit(solution)/shard_map/ppermute | solution.py:230
  88.5 0.1 add_convert_fusion
  88.5 0.7 fusion
  (17 shorter events, 0.4 us)
Async XLA Ops:
  0.6 7.8 %copy-start = (bf16[64,3072]{1,0:T(8,128)(2,1)S(1)}, bf16[64,3072]{1,0:T(8,128)(2,1)}, u32[]{:S(2)}) copy-start(bf16[64,3072]{1,0:T(8,128)(2,1)} %param.9) | copy-start | bytes 1179652
  0.6 8.0 %copy-start.1 = (bf16[64,3072]{1,0:T(8,128)(2,1)S(1)}, bf16[64,3072]{1,0:T(8,128)(2,1)}, u32[]{:S(2)}) copy-start(bf16[64,3072]{1,0:T(8,128)(2,1)} %param.10) | copy-start | bytes 1179652
  3.3 10.8 %all-to-all-start = ((bf16[8,2,16,384]{3,2,1,0:T(8,128)(2,1)}), bf16[8,2,16,384]{3,2,1,0:T(8,128)(2,1)S(1)}, u32[]{:S(2)}, u32[]{:S(2)}) async-start(bf16[8,2,16,384]{3,2,1,0:T(8,128)(2,1)} %maximum_bitcast_fusion.1), calls=%async_computation | async-start | bytes 393216 | tf_op jit(solution)/shard_map/all_to_all | solution.py:204
  8.5 1.0 %copy-start.2 = (bf16[64,3072]{1,0:T(8,128)(2,1)S(1)}, bf16[64,3072]{1,0:T(8,128)(2,1)}, u32[]{:S(2)}) copy-start(bf16[64,3072]{1,0:T(8,128)(2,1)} %param.11) | copy-start | bytes 1179652
  8.6 1.0 %copy-start.3 = (bf16[64,3072]{1,0:T(8,128)(2,1)S(1)}, bf16[64,3072]{1,0:T(8,128)(2,1)}, u32[]{:S(2)}) copy-start(bf16[64,3072]{1,0:T(8,128)(2,1)} %param.12) | copy-start | bytes 1179652
  14.1 23.6 %all-to-all-start.1 = ((bf16[8,4,64,384]{3,2,1,0:T(8,128)(2,1)}), bf16[8,4,64,384]{3,2,1,0:T(8,128)(2,1)S(1)}, u32[]{:S(2)}, u32[]{:S(2)}) async-start(bf16[8,4,64,384]{3,2,1,0:T(8,128)(2,1)} %maximum_bitcast_fusion), calls=%async_computation.1 | async-start | bytes 3145728 | tf_op jit(solution)/shard_map/all_to_all | solution.py:204
  17.7 10.9 %collective-permute-start = (bf16[8,2,16,384]{3,2,1,0:T(8,128)(2,1)S(1)}, bf16[8,2,16,384]{3,2,1,0:T(8,128)(2,1)S(1)}, u32[]{:S(2)}, u32[]{:S(2)}) collective-permute-start(bf16[8,2,16,384]{3,2,1,0:T(8,128)(2,1)S(1)} %all-to-all-done), channel_id=1, source_target_pairs={{0,8},{8,0},{16,24},{24,16},{1,9},{9,1},{17,25},{25,17},{2,10},{10... | collective-permute-start | bytes 589832 | tf_op jit(solution)/shard_map/ppermute | solution.py:210
  19.3 17.1 %collective-permute-start.1 = (bf16[8,2,16,384]{3,2,1,0:T(8,128)(2,1)S(1)}, bf16[8,2,16,384]{3,2,1,0:T(8,128)(2,1)S(1)}, u32[]{:S(2)}, u32[]{:S(2)}) collective-permute-start(bf16[8,2,16,384]{3,2,1,0:T(8,128)(2,1)S(1)} %all-to-all-done), channel_id=1, source_target_pairs={{0,16},{8,24},{16,0},{24,8},{1,17},{9,25},{17,1},{25,9},{2,18},{10... | collective-permute-start | bytes 589832 | tf_op jit(solution)/shard_map/ppermute | solution.py:210
  21.9 14.5 %collective-permute-start.2 = (bf16[8,2,16,384]{3,2,1,0:T(8,128)(2,1)S(1)}, bf16[8,2,16,384]{3,2,1,0:T(8,128)(2,1)S(1)}, u32[]{:S(2)}, u32[]{:S(2)}) collective-permute-start(bf16[8,2,16,384]{3,2,1,0:T(8,128)(2,1)S(1)} %all-to-all-done), channel_id=1, source_target_pairs={{0,24},{8,16},{16,8},{24,0},{1,25},{9,17},{17,9},{25,1},{2,26},{10... | collective-permute-start | bytes 589832 | tf_op jit(solution)/shard_map/ppermute | solution.py:210
  43.9 27.0 %all-to-all-start.2 = ((bf16[16,32,896]{2,1,0:T(8,128)(2,1)}), bf16[16,32,896]{2,1,0:T(8,128)(2,1)S(1)}, u32[]{:S(2)}, u32[]{:S(2)}) async-start(bf16[16,32,896]{2,1,0:T(8,128)(2,1)} %bitcast.8), calls=%async_computation.2 | async-start | bytes 1835008 | tf_op jit(solution)/shard_map/all_to_all | solution.py:219
  78.4 10.1 %collective-permute-start.3 = (bf16[64,2560]{1,0:T(8,128)(2,1)S(1)}, bf16[64,2560]{1,0:T(8,128)(2,1)S(1)}, u32[]{:S(2)}, u32[]{:S(2)}) collective-permute-start(bf16[64,2560]{1,0:T(8,128)(2,1)S(1)} %get-tuple-element.5), channel_id=1, source_target_pairs={{0,1},{1,0},{2,3},{3,2},{4,5},{5,4},{6,7},{7,6},{8,9},{9,8},{10,11... | collective-permute-start | bytes 983048 | tf_op jit(solution)/shard_map/ppermute | solution.py:230

commit v2 on v1

v2 whole, which is shorter than its diff:
```python
import functools
import math

import jax
import jax.numpy as jnp
from jax import lax
from jax.experimental import pallas as pl
from jax.experimental.pallas import tpu as pltpu
from jax.sharding import Mesh, PartitionSpec as P

H = 24
DH = 128
NT = (((1,), (1,)), ((), ()))
ATTEND_VMEM = 24 * 2**20
PROJECT_VMEM = 20 * 2**20


def split_bf16(x, parts):
    terms = []
    for _ in range(parts):
        term = x.astype(jnp.bfloat16)
        terms.append(term)
        x = x - term.astype(jnp.float32)
    return terms


def attend_kernel(heads, row_len, plane_ref, *refs):
    query_refs, (kv_ref, out_ref) = refs[:-2], refs[-2:]
    group, _, key_rows, _ = kv_ref.shape
    keys = group * key_rows
    plane_rows = group * row_len
    g_count, head_axis = out_ref.shape[1], out_ref.shape[2] // row_len
    scale = DH ** (-0.5)

    def some_planes(blocks, planes):
        rows = len(blocks) * plane_rows
        lane = lax.broadcasted_iota(jnp.int32, (rows, DH), 1)
        packed = jnp.zeros((rows, DH), jnp.float32)

        def put(x, columns):
            for i, plane in enumerate(planes):
                for head in range(head_axis):
                    for g in range(g_count):
                        here = i * plane_rows + (head * g_count + g) * row_len
                        there = slice(head * row_len, (head + 1) * row_len)
                        out_ref[plane, g, there, columns] = x[here : here + row_len]

        for h in range(heads):
            lanes = slice(h * DH, (h + 1) * DH)
            key, key_tan, value, value_tan = (
                kv_ref[:, t, :, lanes].reshape(keys, DH) for t in range(4)
            )
            query, qtan = (
                jnp.concatenate(
                    [ref[j, :, t, :, lanes].reshape(plane_rows, DH) for ref, j in blocks]
                )
                for t in range(2)
            )
            scores = lax.dot_general(query, key, NT, preferred_element_type=jnp.float32) * scale
            slopes = (
                lax.dot_general(
                    jnp.concatenate([qtan, query], axis=1),
                    jnp.concatenate([key, key_tan], axis=1),
                    NT,
                    preferred_element_type=jnp.float32,
                )
                * scale
            )
            peak = jnp.max(scores, axis=1, keepdims=True)
            unnormed = jnp.exp(scores - peak)
            tilted = unnormed * slopes
            total = jnp.sum(unnormed, axis=1, keepdims=True)
            slope_sum = jnp.sum(tilted, axis=1, keepdims=True)
            sums = jnp.dot(
                unnormed.astype(jnp.bfloat16),
                jnp.concatenate([value, value_tan], axis=1),
                preferred_element_type=jnp.float32,
            )
            tilted_sum = jnp.dot(
                tilted.astype(jnp.bfloat16), value, preferred_element_type=jnp.float32
            )
            inv = 1.0 / total
            mean_slope = slope_sum * inv
            mean_value = sums[:, :DH] * inv
            tangent = (sums[:, DH:] + tilted_sum) * inv - mean_slope * mean_value
            both = jnp.concatenate([mean_value, tangent], axis=1).astype(jnp.bfloat16)
            put(both, slice(2 * h * DH, 2 * (h + 1) * DH))
            lse = peak + jnp.log(total)
            for i, stat in enumerate(split_bf16(lse, 3) + split_bf16(mean_slope, 2)):
                packed = jnp.where(lane == i * heads + h, stat.astype(jnp.float32), packed)
        put(packed.astype(jnp.bfloat16), slice(2 * heads * DH, (2 * heads + 1) * DH))

    if len(query_refs) > 1:
        planes = [plane_ref[0] ^ d for d in range(len(query_refs))]
        some_planes([(ref, 0) for ref in query_refs], planes)
    else:
        (ref,) = query_refs
        count = math.gcd(ref.shape[0], 4)

        @pl.loop(0, ref.shape[0] // count)
        def _(step):
            planes = [step * count + j for j in range(count)]
            some_planes([(ref, j) for j in planes], planes)


def attend(queries, kv, plane, k, g_count, head_axis):
    heads = kv.shape[3] // DH
    row_len = queries[0].shape[3]
    out_shape = (k, g_count, head_axis * row_len, heads * 2 * DH + DH)
    whole = pl.BlockSpec(memory_space=pltpu.VMEM)
    return pl.pallas_call(
        functools.partial(attend_kernel, heads, row_len),
        out_shape=jax.ShapeDtypeStruct(out_shape, jnp.bfloat16),
        in_specs=[pl.BlockSpec(memory_space=pltpu.SMEM)] + [whole] * (len(queries) + 1),
        out_specs=whole,
        compiler_params=pltpu.CompilerParams(vmem_limit_bytes=ATTEND_VMEM),
        name="attend",
    )(plane, *queries, kv)


def merge(parts_ref, both_ref, heads):
    k, g_count, rows, _ = parts_ref.shape
    tail = heads * 2 * DH
    for g in range(g_count):
        stats = [parts_ref[j, g, :, tail : tail + DH].astype(jnp.float32) for j in range(k)]
        for h in range(heads):

            def stat(j, i):
                return stats[j][:, i * heads + h : i * heads + h + 1]

            lse = [stat(j, 0) + stat(j, 1) + stat(j, 2) for j in range(k)]
            slope = [stat(j, 3) + stat(j, 4) for j in range(k)]
            top = functools.reduce(jnp.maximum, lse)
            share = [jnp.exp(e - top) for e in lse]
            inv = 1.0 / sum(share)
            share = [e * inv for e in share]
            mean_slope = sum(e * s for e, s in zip(share, slope))
            value = jnp.zeros((rows, DH), jnp.float32)
            tangent = jnp.zeros((rows, DH), jnp.float32)
            for j in range(k):
                col = h * 2 * DH
                part = parts_ref[j, g, :, col : col + DH].astype(jnp.float32)
                part_tan = parts_ref[j, g, :, col + DH : col + 2 * DH].astype(jnp.float32)
                value += share[j] * part
                tangent += share[j] * part_tan + (share[j] * (slope[j] - mean_slope)) * part
            col = (g * heads + h) * DH
            both_ref[:rows, col : col + DH] = value.astype(jnp.bfloat16)
            both_ref[rows:, col : col + DH] = tangent.astype(jnp.bfloat16)


def first_kernel(heads, half_ref, parts_ref, weight_ref, out_ref, both_ref, held, sems):
    copies = fetch(half_ref, weight_ref, held, sems)
    merge(parts_ref, both_ref, heads)
    times_held(copies, both_ref, out_ref, held)


def second_kernel(half_ref, both_ref, weight_ref, out_ref, held, sems):
    times_held(fetch(half_ref, weight_ref, held, sems), both_ref, out_ref, held)


def fetch(half_ref, weight_ref, held, sems):
    chunks, _, tile = held.shape
    copies = []
    for i in range(chunks):
        first = pl.multiple_of((half_ref[0] * chunks + i) * tile, tile)
        copy = pltpu.make_async_copy(weight_ref.at[:, pl.ds(first, tile)], held.at[i], sems.at[i])
        copy.start()
        copies.append(copy)
    return copies


def times_held(copies, both_ref, out_ref, held):
    tile = held.shape[2]
    for i, copy in enumerate(copies):
        copy.wait()
        out_ref[:, i * tile : (i + 1) * tile] = jnp.dot(
            both_ref[...], held[i], preferred_element_type=jnp.float32
        ).astype(out_ref.dtype)


def project(kernel, half, left, weight, width, dtype, merged=None):
    depth = weight.shape[0]
    chunks = 4
    rows = merged[0] if merged else left.shape[0]
    outs = [jax.ShapeDtypeStruct((rows, width), dtype)]
    if merged:
        outs.append(jax.ShapeDtypeStruct(merged, jnp.bfloat16))
    whole = pl.BlockSpec(memory_space=pltpu.VMEM)
    return pl.pallas_call(
        kernel,
        out_shape=outs,
        in_specs=[
            pl.BlockSpec(memory_space=pltpu.SMEM),
            whole,
            pl.BlockSpec(memory_space=pl.ANY),
        ],
        out_specs=[whole] * len(outs),
        scratch_shapes=[
            pltpu.VMEM((chunks, depth, width // chunks), jnp.bfloat16),
            pltpu.SemaphoreType.DMA((chunks,)),
        ],
        compiler_params=pltpu.CompilerParams(vmem_limit_bytes=PROJECT_VMEM),
        cost_estimate=pl.CostEstimate(
            flops=2 * rows * depth * width, bytes_accessed=2 * depth * width, transcendentals=0
        ),
        name="project",
    )(half, left, pltpu.with_memory_space_constraint(weight, pltpu.HBM))


def pack_kernel(*refs):
    *matrix_refs, out_ref, sems = refs
    group, _, _, width = out_ref.shape
    copies = [
        pltpu.make_async_copy(
            ref.at[:, pl.ds(i * width, width)], out_ref.at[i, t], sems.at[i, t]
        )
        for i in range(group)
        for t, ref in enumerate(matrix_refs)
    ]
    for copy in copies:
        copy.start()
    for copy in copies:
        copy.wait()


def pack(group, *matrices):
    rows, columns = matrices[0].shape
    return pl.pallas_call(
        pack_kernel,
        out_shape=jax.ShapeDtypeStruct(
            (group, len(matrices), rows, columns // group), jnp.bfloat16
        ),
        in_specs=[pl.BlockSpec(memory_space=pl.ANY)] * len(matrices),
        out_specs=pl.BlockSpec(memory_space=pltpu.VMEM),
        scratch_shapes=[pltpu.SemaphoreType.DMA((group, len(matrices)))],
        compiler_params=pltpu.CompilerParams(vmem_limit_bytes=8 * 2**20),
        name="pack",
    )(*(pltpu.with_memory_space_constraint(m, pltpu.HBM) for m in matrices))


def local(queries, query_tangent, key_rows, key_tangent, value_rows, value_tangent, out_weight):
    k, g_count, head_axis = (lax.axis_size(a) for a in ("k", "g", "head"))
    plane_axes = ("head", "g")
    group = g_count * head_axis
    heads = H // group
    rows = queries.shape[0] * head_axis

    def within_plane(x):
        return lax.all_to_all(x, plane_axes, split_axis=0, concat_axis=0, tiled=True)

    plane_queries = within_plane(pack(group, queries, query_tangent))
    kv = within_plane(pack(group, key_rows, key_tangent, value_rows, value_tangent))
    if k in (2, 4, 8):
        all_queries = [plane_queries[None]] + [
            lax.ppermute(plane_queries, "k", [(i, i ^ d) for i in range(k)])[None]
            for d in range(1, k)
        ]
    else:
        all_queries = [lax.all_gather(plane_queries, "k", axis=0, tiled=False)]

    plane = lax.axis_index("k").astype(jnp.int32).reshape(1)
    parts = attend(all_queries, kv, plane, k, g_count, head_axis)
    parts = parts.reshape((k * g_count,) + parts.shape[2:])
    parts = lax.all_to_all(parts, ("k", "g"), split_axis=0, concat_axis=0, tiled=True)
    parts = parts.reshape((k, g_count) + parts.shape[1:])

    width = out_weight.shape[1] // head_axis
    mine = lax.axis_index("head").astype(jnp.int32).reshape(1)
    merged = (2 * rows, out_weight.shape[0])
    merging = functools.partial(first_kernel, heads)
    if head_axis == 2:
        sent, both = project(merging, 1 - mine, parts, out_weight, width, jnp.bfloat16, merged)
        received = lax.ppermute(sent, "head", [(0, 1), (1, 0)])
        (own,) = project(second_kernel, mine, both, out_weight, width, jnp.float32)
        total = own + received.astype(jnp.float32)
    else:
        partial, _ = project(
            merging, 0 * mine, parts, out_weight, width * head_axis, jnp.float32, merged
        )
        total = lax.psum_scatter(partial, "head", scatter_dimension=1, tiled=True)
    total = total.astype(jnp.bfloat16)
    return (total[:rows], total[rows:])


def solution(mesh):
    blk, head_axis = mesh.shape["blk"], mesh.shape["head"]
    g_count = math.gcd(H // head_axis, blk)
    fine = Mesh(mesh.devices.reshape(blk // g_count, g_count, head_axis), ("k", "g", "head"))
    rows = P(("k", "g", "head"), None)
    return jax.shard_map(
        local,
        mesh=fine,
        in_specs=(rows,) * 6 + (P("head", None),),
        out_specs=(P(("k", "g"), "head"),) * 2,
        check_vma=False,
    )
```

time: 89.9 us -> 83.4 us (0.928)
  local copies, waits for them, and re-layouts: 3.85 us -> 0.74 us
  Pallas kernels: 19.2 us -> 16.5 us
  other arithmetic: 2.16 us -> 0.06 us
  waiting for transfers between devices: 42.4 us -> 43.9 us
    unnamed x14 -> x0, local copies, waits for them, and re-layouts: 2.89 us -> none
    pallas_call x3 -> x5, Pallas kernels: 19.2 us -> 16.5 us  [the longest x2 8.44 us: project(): pl.pallas_call(kernel, out_shape=outs, in_specs=[pl.BlockSpec(memory_spac...]
    transpose x2 -> x0, other arithmetic: 2.1 us -> none  [pack(): stacked.reshape(count, rows, group, columns // group).transpose(2, 0, 1, 3)]
    ppermute x1, waiting for transfers between devices: 3.05 us -> 4.71 us  [local(): received = lax.ppermute(sent, 'head', [(0, 1), (1, 0)])]
  transfers between devices with their start and end apart: 7 -> 7, of which waited for: 6 -> 6; matrix products, arithmetic and copies ran while one was open for 2% -> 0% of each run, Pallas kernels for 6% -> 8%
where the time goes in v2:
time: 83.4 us; the launch traced here: 82.8 us
  waiting for transfers between devices  43.9 us (53%)
  starting transfers between devices  20.9 us (25%)
  Pallas kernels  16.5 us (20%)
    all_to_all x1, waiting for transfers between devices, local(): lax.all_to_all(parts, ('k', 'g'), split_axis=0, concat_axis=0, tiled=True)  20.8 us
    ppermute x3, waiting for transfers between devices, local(): lax.ppermute(plane_queries, 'k', [(i, i ^ d) for i in range(k)])[None]  14.3 us
    all_to_all x2, starting transfers between devices, within_plane(): lax.all_to_all(x, plane_axes, split_axis=0, concat_axis=0, tiled=True)  8.76 us
    pallas_call x2, Pallas kernels, project(): pl.pallas_call(kernel, out_shape=outs, in_specs=[pl.BlockSpec(memory_spac...  8.44 us
    all_to_all x1, starting transfers between devices, local(): lax.all_to_all(parts, ('k', 'g'), split_axis=0, concat_axis=0, tiled=True)  6.16 us
    ppermute x1, waiting for transfers between devices, local(): received = lax.ppermute(sent, 'head', [(0, 1), (1, 0)])  4.71 us
    pallas_call x2, Pallas kernels, pack(): pl.pallas_call(pack_kernel, out_shape=jax.ShapeDtypeStruct((group, len(ma...  4.49 us
    ppermute x3, starting transfers between devices, local(): lax.ppermute(plane_queries, 'k', [(i, i ^ d) for i in range(k)])[None]  4.45 us
  transfers between devices with their start and end apart: 7, of which 6 were waited for; matrix products, arithmetic and copies ran while one was open for 0% of the time, Pallas kernels for 8%

profile of v2, /device:TPU:0, one launch (start us, length us, event | category | flops | bytes accessed | tf_op | source)
XLA Modules:
  0.0 82.8 jit_solution(14972954754444923960)
XLA Ops:
  0.6 1.7 %pack.2 = bf16[8,2,16,384]{3,2,1,0:T(8,128)(2,1)} custom-call(bf16[16,3072]{1,0:T(8,128)(2,1)} %refs_0_.2, bf16[16,3072]{1,0:T(8,128)(2,1)} %refs_1_.2), custom_call_target="tpu_custom_call" | custom-call | tf_op jit(solution)/shard_map/pack/pallas_call | solution.py:228
  2.3 5.2 %all-to-all-start = ((bf16[8,2,16,384]{3,2,1,0:T(8,128)(2,1)}), bf16[8,2,16,384]{3,2,1,0:T(8,128)(2,1)S(1)}, u32[]{:S(2)}, u32[]{:S(2)}) async-start(bf16[8,2,16,384]{3,2,1,0:T(8,128)(2,1)} %pack.2), calls=%async_computation | async-start | bytes 393216 | tf_op jit(solution)/shard_map/all_to_all | solution.py:249
  7.5 2.8 %pack.3 = bf16[8,4,64,384]{3,2,1,0:T(8,128)(2,1)} custom-call(bf16[64,3072]{1,0:T(8,128)(2,1)} %refs_0_.3, bf16[64,3072]{1,0:T(8,128)(2,1)} %refs_1_.3, bf16[64,3072]{1,0:T(8,128)(2,1)} %refs_2_.1, bf16[64,3072]{1,0:T(8,128)(2,1)} %refs_3_.1), custom_call_target="tpu_custom_call" | custom-call | tf_op jit(solution)/shard_map/pack/pallas_call | solution.py:228
  10.3 2.8 %all-to-all-done = bf16[8,2,16,384]{3,2,1,0:T(8,128)(2,1)S(1)} async-done(((bf16[8,2,16,384]{3,2,1,0:T(8,128)(2,1)}), bf16[8,2,16,384]{3,2,1,0:T(8,128)(2,1)S(1)}, u32[]{:S(2)}, u32[]{:S(2)}) %all-to-all-start) | async-done | bytes 196640 | tf_op jit(solution)/shard_map/all_to_all | solution.py:249
  13.2 3.6 %all-to-all-start.1 = ((bf16[8,4,64,384]{3,2,1,0:T(8,128)(2,1)}), bf16[8,4,64,384]{3,2,1,0:T(8,128)(2,1)S(1)}, u32[]{:S(2)}, u32[]{:S(2)}) async-start(bf16[8,4,64,384]{3,2,1,0:T(8,128)(2,1)} %pack.3), calls=%async_computation.1 | async-start | bytes 3145728 | tf_op jit(solution)/shard_map/all_to_all | solution.py:249
  16.7 1.6 %collective-permute-start = (bf16[8,2,16,384]{3,2,1,0:T(8,128)(2,1)S(1)}, bf16[8,2,16,384]{3,2,1,0:T(8,128)(2,1)S(1)}, u32[]{:S(2)}, u32[]{:S(2)}) collective-permute-start(bf16[8,2,16,384]{3,2,1,0:T(8,128)(2,1)S(1)} %all-to-all-done), channel_id=1, source_target_pairs={{0,8},{8,0},{16,24},{24,16},{1,9},{9,1},{17,25},{25,17},{2,10},{10... | collective-permute-start | bytes 589832 | tf_op jit(solution)/shard_map/ppermute | solution.py:255
  18.4 2.6 %collective-permute-start.1 = (bf16[8,2,16,384]{3,2,1,0:T(8,128)(2,1)S(1)}, bf16[8,2,16,384]{3,2,1,0:T(8,128)(2,1)S(1)}, u32[]{:S(2)}, u32[]{:S(2)}) collective-permute-start(bf16[8,2,16,384]{3,2,1,0:T(8,128)(2,1)S(1)} %all-to-all-done), channel_id=1, source_target_pairs={{0,16},{8,24},{16,0},{24,8},{1,17},{9,25},{17,1},{25,9},{2,18},{10... | collective-permute-start | bytes 589832 | tf_op jit(solution)/shard_map/ppermute | solution.py:255
  21.0 0.2 collective-permute-start.2
  21.2 6.5 %collective-permute-done = bf16[8,2,16,384]{3,2,1,0:T(8,128)(2,1)S(1)} collective-permute-done((bf16[8,2,16,384]{3,2,1,0:T(8,128)(2,1)S(1)}, bf16[8,2,16,384]{3,2,1,0:T(8,128)(2,1)S(1)}, u32[]{:S(2)}, u32[]{:S(2)}) %collective-permute-start) | collective-permute-done | bytes 196640 | tf_op jit(solution)/shard_map/ppermute | solution.py:255
  27.7 7.9 %collective-permute-done.1 = bf16[8,2,16,384]{3,2,1,0:T(8,128)(2,1)S(1)} collective-permute-done((bf16[8,2,16,384]{3,2,1,0:T(8,128)(2,1)S(1)}, bf16[8,2,16,384]{3,2,1,0:T(8,128)(2,1)S(1)}, u32[]{:S(2)}, u32[]{:S(2)}) %collective-permute-start.1) | collective-permute-done | bytes 196640 | tf_op jit(solution)/shard_map/ppermute | solution.py:255
  35.5 0.0 collective-permute-done.2
  35.5 1.2 %all-to-all-done.1.refs_4_ = bf16[8,4,64,384]{3,2,1,0:T(8,128)(2,1)S(1)} async-done(((bf16[8,4,64,384]{3,2,1,0:T(8,128)(2,1)}), bf16[8,4,64,384]{3,2,1,0:T(8,128)(2,1)S(1)}, u32[]{:S(2)}, u32[]{:S(2)}) %all-to-all-start.1) | async-done | bytes 1572896 | tf_op jit(solution)/shard_map/all_to_all | solution.py:249
  36.7 3.6 %attend.1 = bf16[4,4,32,896]{3,2,1,0:T(8,128)(2,1)} custom-call(s32[1]{0:T(128)} %bitcast.1.plane_ref, bf16[1,8,2,16,384]{4,3,2,1,0:T(8,128)(2,1)S(1)} %bitcast.9, bf16[1,8,2,16,384]{4,3,2,1,0:T(8,128)(2,1)S(1)} %bitcast.10, bf16[1,8,2,16,384]{4,3,2,1,0:T(8,128)(2,1)S(1)} %bitcast.11, bf16[1,8,2,16,384]{4,3,2,1,0:T(8,128)(2,1)S(1)} %bitcast.12, ...), custom_call_target="tpu_custom_call" | custom-call | tf_op jit(solution)/shard_map/attend/pallas_call | solution.py:111
  40.3 6.2 %all-to-all-start.2 = ((bf16[16,32,896]{2,1,0:T(8,128)(2,1)}), bf16[16,32,896]{2,1,0:T(8,128)(2,1)S(1)}, u32[]{:S(2)}, u32[]{:S(2)}) async-start(bf16[16,32,896]{2,1,0:T(8,128)(2,1)} %bitcast.6), calls=%async_computation.2 | async-start | bytes 1835008 | tf_op jit(solution)/shard_map/all_to_all | solution.py:264
  46.5 20.8 %all-to-all-done.2 = bf16[16,32,896]{2,1,0:T(8,128)(2,1)S(1)} async-done(((bf16[16,32,896]{2,1,0:T(8,128)(2,1)}), bf16[16,32,896]{2,1,0:T(8,128)(2,1)S(1)}, u32[]{:S(2)}, u32[]{:S(2)}) %all-to-all-start.2) | async-done | bytes 917536 | tf_op jit(solution)/shard_map/all_to_all | solution.py:264
  67.3 4.6 %project.2 = (bf16[64,2560]{1,0:T(8,128)(2,1)S(1)}, bf16[64,1536]{1,0:T(8,128)(2,1)S(1)}) custom-call(s32[1]{0:T(128)S(6)} %sub.3.half_ref, bf16[4,4,32,896]{3,2,1,0:T(8,128)(2,1)S(1)} %bitcast.8, bf16[1536,5120]{1,0:T(8,128)(2,1)} %weight_ref.3), custom_call_target="tpu_custom_call" | custom-call | flops 503316480 | bytes 7864320 | tf_op jit(solution)/shard_map/project/pallas_call | solution.py:189
  71.9 1.6 %collective-permute-start.3 = (bf16[64,2560]{1,0:T(8,128)(2,1)S(1)}, bf16[64,2560]{1,0:T(8,128)(2,1)S(1)}, u32[]{:S(2)}, u32[]{:S(2)}) collective-permute-start(bf16[64,2560]{1,0:T(8,128)(2,1)S(1)} %get-tuple-element.5), channel_id=1, source_target_pairs={{0,1},{1,0},{2,3},{3,2},{4,5},{5,4},{6,7},{7,6},{8,9},{9,8},{10,11... | collective-permute-start | bytes 983048 | tf_op jit(solution)/shard_map/ppermute | solution.py:273
  73.4 3.8 %project.3 = f32[64,2560]{1,0:T(8,128)S(1)} custom-call(s32[1]{0:T(128)} %bitcast.half_ref, bf16[64,1536]{1,0:T(8,128)(2,1)S(1)} %get-tuple-element.4.both_ref, bf16[1536,5120]{1,0:T(8,128)(2,1)} %weight_ref.3), custom_call_target="tpu_custom_call" | custom-call | flops 503316480 | bytes 7864320 | tf_op jit(solution)/shard_map/project/pallas_call | solution.py:189
  77.3 4.7 %collective-permute-done.3 = bf16[64,2560]{1,0:T(8,128)(2,1)S(1)} collective-permute-done((bf16[64,2560]{1,0:T(8,128)(2,1)S(1)}, bf16[64,2560]{1,0:T(8,128)(2,1)S(1)}, u32[]{:S(2)}, u32[]{:S(2)}) %collective-permute-start.3) | collective-permute-done | bytes 327712 | tf_op jit(solution)/shard_map/ppermute | solution.py:273
  82.0 0.1 add_convert_fusion
  82.1 0.7 fusion
Async XLA Ops:
  2.3 10.8 %all-to-all-start = ((bf16[8,2,16,384]{3,2,1,0:T(8,128)(2,1)}), bf16[8,2,16,384]{3,2,1,0:T(8,128)(2,1)S(1)}, u32[]{:S(2)}, u32[]{:S(2)}) async-start(bf16[8,2,16,384]{3,2,1,0:T(8,128)(2,1)} %pack.2), calls=%async_computation | async-start | bytes 393216 | tf_op jit(solution)/shard_map/all_to_all | solution.py:249
  13.2 23.6 %all-to-all-start.1 = ((bf16[8,4,64,384]{3,2,1,0:T(8,128)(2,1)}), bf16[8,4,64,384]{3,2,1,0:T(8,128)(2,1)S(1)}, u32[]{:S(2)}, u32[]{:S(2)}) async-start(bf16[8,4,64,384]{3,2,1,0:T(8,128)(2,1)} %pack.3), calls=%async_computation.1 | async-start | bytes 3145728 | tf_op jit(solution)/shard_map/all_to_all | solution.py:249
  16.7 10.9 %collective-permute-start = (bf16[8,2,16,384]{3,2,1,0:T(8,128)(2,1)S(1)}, bf16[8,2,16,384]{3,2,1,0:T(8,128)(2,1)S(1)}, u32[]{:S(2)}, u32[]{:S(2)}) collective-permute-start(bf16[8,2,16,384]{3,2,1,0:T(8,128)(2,1)S(1)} %all-to-all-done), channel_id=1, source_target_pairs={{0,8},{8,0},{16,24},{24,16},{1,9},{9,1},{17,25},{25,17},{2,10},{10... | collective-permute-start | bytes 589832 | tf_op jit(solution)/shard_map/ppermute | solution.py:255
  18.4 17.1 %collective-permute-start.1 = (bf16[8,2,16,384]{3,2,1,0:T(8,128)(2,1)S(1)}, bf16[8,2,16,384]{3,2,1,0:T(8,128)(2,1)S(1)}, u32[]{:S(2)}, u32[]{:S(2)}) collective-permute-start(bf16[8,2,16,384]{3,2,1,0:T(8,128)(2,1)S(1)} %all-to-all-done), channel_id=1, source_target_pairs={{0,16},{8,24},{16,0},{24,8},{1,17},{9,25},{17,1},{25,9},{2,18},{10... | collective-permute-start | bytes 589832 | tf_op jit(solution)/shard_map/ppermute | solution.py:255
  21.0 14.5 %collective-permute-start.2 = (bf16[8,2,16,384]{3,2,1,0:T(8,128)(2,1)S(1)}, bf16[8,2,16,384]{3,2,1,0:T(8,128)(2,1)S(1)}, u32[]{:S(2)}, u32[]{:S(2)}) collective-permute-start(bf16[8,2,16,384]{3,2,1,0:T(8,128)(2,1)S(1)} %all-to-all-done), channel_id=1, source_target_pairs={{0,24},{8,16},{16,8},{24,0},{1,25},{9,17},{17,9},{25,1},{2,26},{10... | collective-permute-start | bytes 589832 | tf_op jit(solution)/shard_map/ppermute | solution.py:255
  40.3 27.0 %all-to-all-start.2 = ((bf16[16,32,896]{2,1,0:T(8,128)(2,1)}), bf16[16,32,896]{2,1,0:T(8,128)(2,1)S(1)}, u32[]{:S(2)}, u32[]{:S(2)}) async-start(bf16[16,32,896]{2,1,0:T(8,128)(2,1)} %bitcast.6), calls=%async_computation.2 | async-start | bytes 1835008 | tf_op jit(solution)/shard_map/all_to_all | solution.py:264
  71.9 10.1 %collective-permute-start.3 = (bf16[64,2560]{1,0:T(8,128)(2,1)S(1)}, bf16[64,2560]{1,0:T(8,128)(2,1)S(1)}, u32[]{:S(2)}, u32[]{:S(2)}) collective-permute-start(bf16[64,2560]{1,0:T(8,128)(2,1)S(1)} %get-tuple-element.5), channel_id=1, source_target_pairs={{0,1},{1,0},{2,3},{3,2},{4,5},{5,4},{6,7},{7,6},{8,9},{9,8},{10,11... | collective-permute-start | bytes 983048 | tf_op jit(solution)/shard_map/ppermute | solution.py:273

commit v3 on v2

--- a/solution.py
+++ b/solution.py
@@ -24,17 +24,14 @@
     return terms
 
 
-def attend_kernel(heads, row_len, plane_ref, *refs):
-    query_refs, (kv_ref, out_ref) = refs[:-2], refs[-2:]
-    group, _, key_rows, _ = kv_ref.shape
-    keys = group * key_rows
+def attend_kernel(heads, row_len, group, plane_ref, *refs):
+    query_refs, kv_refs, out_ref = refs[: -group - 1], refs[-group - 1 : -1], refs[-1]
     plane_rows = group * row_len
     g_count, head_axis = out_ref.shape[1], out_ref.shape[2] // row_len
     scale = DH ** (-0.5)
 
     def some_planes(blocks, planes):
         rows = len(blocks) * plane_rows
-        lane = lax.broadcasted_iota(jnp.int32, (rows, DH), 1)
         packed = jnp.zeros((rows, DH), jnp.float32)
 
         def put(x, columns):
@@ -48,7 +45,7 @@
         for h in range(heads):
             lanes = slice(h * DH, (h + 1) * DH)
             key, key_tan, value, value_tan = (
-                kv_ref[:, t, :, lanes].reshape(keys, DH) for t in range(4)
+                jnp.concatenate([ref[t, :, lanes] for ref in kv_refs]) for t in range(4)
             )
             query, qtan = (
                 jnp.concatenate(
@@ -86,8 +83,7 @@
             both = jnp.concatenate([mean_value, tangent], axis=1).astype(jnp.bfloat16)
             put(both, slice(2 * h * DH, 2 * (h + 1) * DH))
             lse = peak + jnp.log(total)
-            for i, stat in enumerate(split_bf16(lse, 3) + split_bf16(mean_slope, 2)):
-                packed = jnp.where(lane == i * heads + h, stat.astype(jnp.float32), packed)
+            packed = stats_columns(packed, h, heads, lse, mean_slope)
         put(packed.astype(jnp.bfloat16), slice(2 * heads * DH, (2 * heads + 1) * DH))
 
     if len(query_refs) > 1:
@@ -104,48 +100,94 @@
 
 
 def attend(queries, kv, plane, k, g_count, head_axis):
-    heads = kv.shape[3] // DH
+    heads = kv[0].shape[2] // DH
     row_len = queries[0].shape[3]
     out_shape = (k, g_count, head_axis * row_len, heads * 2 * DH + DH)
     whole = pl.BlockSpec(memory_space=pltpu.VMEM)
     return pl.pallas_call(
-        functools.partial(attend_kernel, heads, row_len),
+        functools.partial(attend_kernel, heads, row_len, len(kv)),
         out_shape=jax.ShapeDtypeStruct(out_shape, jnp.bfloat16),
-        in_specs=[pl.BlockSpec(memory_space=pltpu.SMEM)] + [whole] * (len(queries) + 1),
+        in_specs=[pl.BlockSpec(memory_space=pltpu.SMEM)] + [whole] * (len(queries) + len(kv)),
         out_specs=whole,
         compiler_params=pltpu.CompilerParams(vmem_limit_bytes=ATTEND_VMEM),
         name="attend",
-    )(plane, *queries, kv)
+    )(plane, *queries, *kv)
+
+
+def merge_head(parts, stats, h, heads):
+    def stat(j, i):
+        return stats[j][:, i * heads + h : i * heads + h + 1]
+
+    lse = [stat(j, 0) + stat(j, 1) + stat(j, 2) for j in range(len(parts))]
+    slope = [stat(j, 3) + stat(j, 4) for j in range(len(parts))]
+    top = functools.reduce(jnp.maximum, lse)
+    share = [jnp.exp(e - top) for e in lse]
+    total = sum(share)
+    inv = 1.0 / total
+    share = [e * inv for e in share]
+    mean_slope = sum(e * s for e, s in zip(share, slope))
+    value = tangent = 0.0
+    for part, e, s in zip(parts, share, slope):
+        col = h * 2 * DH
+        own = part[:, col : col + DH].astype(jnp.float32)
+        own_tan = part[:, col + DH : col + 2 * DH].astype(jnp.float32)
+        value += e * own
+        tangent += e * own_tan + (e * (s - mean_slope)) * own
+    return value, tangent, top + jnp.log(total), mean_slope
 
 
 def merge(parts_ref, both_ref, heads):
     k, g_count, rows, _ = parts_ref.shape
-    tail = heads * 2 * DH
+    tail = slice(2 * heads * DH, (2 * heads + 1) * DH)
     for g in range(g_count):
-        stats = [parts_ref[j, g, :, tail : tail + DH].astype(jnp.float32) for j in range(k)]
+        parts = [parts_ref[j, g] for j in range(k)]
+        stats = [part[:, tail].astype(jnp.float32) for part in parts]
         for h in range(heads):
-
-            def stat(j, i):
-                return stats[j][:, i * heads + h : i * heads + h + 1]
-
-            lse = [stat(j, 0) + stat(j, 1) + stat(j, 2) for j in range(k)]
-            slope = [stat(j, 3) + stat(j, 4) for j in range(k)]
-            top = functools.reduce(jnp.maximum, lse)
-            share = [jnp.exp(e - top) for e in lse]
-            inv = 1.0 / sum(share)
-            share = [e * inv for e in share]
-            mean_slope = sum(e * s for e, s in zip(share, slope))
-            value = jnp.zeros((rows, DH), jnp.float32)
-            tangent = jnp.zeros((rows, DH), jnp.float32)
-            for j in range(k):
-                col = h * 2 * DH
-                part = parts_ref[j, g, :, col : col + DH].astype(jnp.float32)
-                part_tan = parts_ref[j, g, :, col + DH : col + 2 * DH].astype(jnp.float32)
-                value += share[j] * part
-                tangent += share[j] * part_tan + (share[j] * (slope[j] - mean_slope)) * part
+            value, tangent, _, _ = merge_head(parts, stats, h, heads)
             col = (g * heads + h) * DH
             both_ref[:rows, col : col + DH] = value.astype(jnp.bfloat16)
             both_ref[rows:, col : col + DH] = tangent.astype(jnp.bfloat16)
+
+
+def stats_columns(packed, h, heads, lse, slope):
+    lane = lax.broadcasted_iota(jnp.int32, packed.shape, 1)
+    for i, stat in enumerate(split_bf16(lse, 3) + split_bf16(slope, 2)):
+        packed = jnp.where(lane == i * heads + h, stat.astype(jnp.float32), packed)
+    return packed
+
+
+def pair_kernel(heads, home_ref, away_ref, out_ref):
+    rows = home_ref.shape[1]
+    count = math.gcd(home_ref.shape[0], 8)
+
+    @pl.loop(0, home_ref.shape[0] // count)
+    def _(step):
+        some = pl.ds(step * count, count)
+        parts = [ref[some].reshape(count * rows, ref.shape[2]) for ref in (home_ref, away_ref)]
+        tail = slice(2 * heads * DH, (2 * heads + 1) * DH)
+        stats = [part[:, tail].astype(jnp.float32) for part in parts]
+        packed = jnp.zeros((count * rows, DH), jnp.float32)
+
+        def put(x, columns):
+            out_ref[some, :, columns] = x.astype(jnp.bfloat16).reshape(count, rows, x.shape[1])
+
+        for h in range(heads):
+            value, tangent, lse, slope = merge_head(parts, stats, h, heads)
+            put(jnp.concatenate([value, tangent], axis=1), slice(2 * h * DH, 2 * (h + 1) * DH))
+            packed = stats_columns(packed, h, heads, lse, slope)
+        put(packed, tail)
+
+
+def merge_pair(home, away, heads):
+    whole = pl.BlockSpec(memory_space=pltpu.VMEM)
+    return pl.pallas_call(
+        functools.partial(pair_kernel, heads),
+        out_shape=jax.ShapeDtypeStruct(home.shape, home.dtype),
+        in_specs=[whole, whole],
+        out_specs=whole,
+        compiler_params=pltpu.CompilerParams(vmem_limit_bytes=ATTEND_VMEM),
+        name="merge_pair",
+    )(home, away)
 
 
 def first_kernel(heads, half_ref, parts_ref, weight_ref, out_ref, both_ref, held, sems):
@@ -238,29 +280,71 @@
     )(*(pltpu.with_memory_space_constraint(m, pltpu.HBM) for m in matrices))
 
 
+def pieces_kernel(group, columns_ref, after_ref, *refs):
+    matrix_refs, out_refs, sems = refs[: -group - 1], refs[-group - 1 : -1], refs[-1]
+    width = out_refs[0].shape[2]
+    copies = []
+    for d, out_ref in enumerate(out_refs):
+        first = pl.multiple_of(columns_ref[d] * width, width)
+        for t, ref in enumerate(matrix_refs):
+            copies.append(
+                pltpu.make_async_copy(ref.at[:, pl.ds(first, width)], out_ref.at[t], sems.at[d, t])
+            )
+    for copy in copies:
+        copy.start()
+    for copy in copies:
+        copy.wait()
+
+
+def pieces(group, order, after, *matrices):
+    rows, columns = matrices[0].shape
+    shape = jax.ShapeDtypeStruct((len(matrices), rows, columns // group), jnp.bfloat16)
+    return pl.pallas_call(
+        functools.partial(pieces_kernel, group),
+        out_shape=[shape] * group,
+        in_specs=[pl.BlockSpec(memory_space=pltpu.SMEM)]
+        + [pl.BlockSpec(memory_space=pl.ANY)] * (1 + len(matrices)),
+        out_specs=[pl.BlockSpec(memory_space=pltpu.VMEM)] * group,
+        scratch_shapes=[pltpu.SemaphoreType.DMA((group, len(matrices)))],
+        compiler_params=pltpu.CompilerParams(vmem_limit_bytes=8 * 2**20),
+        name="pieces",
+    )(order, after, *(pltpu.with_memory_space_constraint(m, pltpu.HBM) for m in matrices))
+
+
 def local(queries, query_tangent, key_rows, key_tangent, value_rows, value_tangent, out_weight):
     k, g_count, head_axis = (lax.axis_size(a) for a in ("k", "g", "head"))
     plane_axes = ("head", "g")
     group = g_count * head_axis
     heads = H // group
     rows = queries.shape[0] * head_axis
+    swap = [(0, 1), (1, 0)]
 
     def within_plane(x):
         return lax.all_to_all(x, plane_axes, split_axis=0, concat_axis=0, tiled=True)
 
-    plane_queries = within_plane(pack(group, queries, query_tangent))
-    kv = within_plane(pack(group, key_rows, key_tangent, value_rows, value_tangent))
-    if k in (2, 4, 8):
-        all_queries = [plane_queries[None]] + [
-            lax.ppermute(plane_queries, "k", [(i, i ^ d) for i in range(k)])[None]
-            for d in range(1, k)
-        ]
+    packed_queries = pack(group, queries, query_tangent)
+    plane_queries = within_plane(packed_queries)
+    partner = lax.axis_index(("g", "head")).astype(jnp.int32) ^ jnp.arange(group, dtype=jnp.int32)
+    order = (partner % head_axis) * g_count + partner // head_axis
+    kv = pieces(
+        group, order, packed_queries, key_rows, key_tangent, value_rows, value_tangent
+    )
+    kv = [
+        lax.ppermute(piece, ("g", "head"), [(i, i ^ d) for i in range(group)]) if d else piece
+        for d, piece in enumerate(kv)
+    ]
+    if k == 2:
+        home_queries = [plane_queries[None], lax.ppermute(plane_queries, "k", swap)[None]]
     else:
-        all_queries = [lax.all_gather(plane_queries, "k", axis=0, tiled=False)]
+        home_queries = [lax.all_gather(plane_queries, "k", axis=0, tiled=False)]
+    away_queries = [lax.ppermute(q, "core", swap) for q in home_queries]
 
     plane = lax.axis_index("k").astype(jnp.int32).reshape(1)
-    parts = attend(all_queries, kv, plane, k, g_count, head_axis)
-    parts = parts.reshape((k * g_count,) + parts.shape[2:])
+    away, home = (
+        attend(some, kv, plane, k, g_count, head_axis).reshape(k * g_count, rows, -1)
+        for some in (away_queries, home_queries)
+    )
+    parts = merge_pair(home, lax.ppermute(away, "core", swap), heads)
     parts = lax.all_to_all(parts, ("k", "g"), split_axis=0, concat_axis=0, tiled=True)
     parts = parts.reshape((k, g_count) + parts.shape[1:])
 
@@ -270,7 +354,7 @@
     merging = functools.partial(first_kernel, heads)
     if head_axis == 2:
         sent, both = project(merging, 1 - mine, parts, out_weight, width, jnp.bfloat16, merged)
-        received = lax.ppermute(sent, "head", [(0, 1), (1, 0)])
+        received = lax.ppermute(sent, "head", swap)
         (own,) = project(second_kernel, mine, both, out_weight, width, jnp.float32)
         total = own + received.astype(jnp.float32)
     else:
@@ -284,13 +368,16 @@
 
 def solution(mesh):
     blk, head_axis = mesh.shape["blk"], mesh.shape["head"]
-    g_count = math.gcd(H // head_axis, blk)
-    fine = Mesh(mesh.devices.reshape(blk // g_count, g_count, head_axis), ("k", "g", "head"))
-    rows = P(("k", "g", "head"), None)
+    g_count = math.gcd(H // head_axis, blk // 2)
+    fine = Mesh(
+        mesh.devices.reshape(blk // (2 * g_count), g_count, 2, head_axis),
+        ("k", "g", "core", "head"),
+    )
+    rows = P(("k", "g", "core", "head"), None)
     return jax.shard_map(
         local,
         mesh=fine,
         in_specs=(rows,) * 6 + (P("head", None),),
-        out_specs=(P(("k", "g"), "head"),) * 2,
+        out_specs=(P(("k", "g", "core"), "head"),) * 2,
         check_vma=False,
     )

time: 83.4 us -> 76.6 us (0.918)
  waiting for transfers between devices: 43.9 us -> 31.1 us
  starting transfers between devices: 20.9 us -> 26.4 us
    ppermute x4 -> x12, starting transfers between devices: 6.01 us -> 15.5 us  [the longest x7 11.6 us: local(): lax.ppermute(piece, ('g', 'head'), [(i, i ^ d) for i in range(group)])]
    all_to_all x1, waiting for transfers between devices: 20.8 us -> 13.5 us  [local(): lax.all_to_all(parts, ('k', 'g'), split_axis=0, concat_axis=0, tiled=True)]
    all_to_all x2 -> x1, waiting for transfers between devices: 4.05 us -> 0.01 us  [within_plane(): lax.all_to_all(x, plane_axes, split_axis=0, concat_axis=0, tiled=True)]
    pallas_call x1 -> x4, Pallas kernels: 3.56 us -> 7.35 us  [the longest x2 3.17 us: attend(): pl.pallas_call(functools.partial(attend_kernel, heads, row_len, len(kv)),...]
    pallas_call x2 -> x1, Pallas kernels: 4.49 us -> 1.7 us  [pack(): pl.pallas_call(pack_kernel, out_shape=jax.ShapeDtypeStruct((group, len(ma...]
    all_to_all x2 -> x1, starting transfers between devices: 8.76 us -> 6.2 us  [within_plane(): lax.all_to_all(x, plane_axes, split_axis=0, concat_axis=0, tiled=True)]
    ppermute x4 -> x12, waiting for transfers between devices: 19 us -> 17.5 us  [the longest x7 13.3 us: local(): lax.ppermute(piece, ('g', 'head'), [(i, i ^ d) for i in range(group)])]
    all_to_all x1, starting transfers between devices: 6.16 us -> 4.76 us  [local(): lax.all_to_all(parts, ('k', 'g'), split_axis=0, concat_axis=0, tiled=True)]
  transfers between devices with their start and end apart: 7 -> 14, of which waited for: 6 -> 8; matrix products, arithmetic and copies ran while one was open for 0% -> 0% of each run, Pallas kernels for 8% -> 10%
where the time goes in v3:
time: 76.6 us; the launch traced here: 76.2 us
  waiting for transfers between devices  31.1 us (41%)
  starting transfers between devices  26.4 us (34%)
  Pallas kernels  17.2 us (22%)
    all_to_all x1, waiting for transfers between devices, local(): lax.all_to_all(parts, ('k', 'g'), split_axis=0, concat_axis=0, tiled=True)  13.5 us
    ppermute x7, waiting for transfers between devices, local(): lax.ppermute(piece, ('g', 'head'), [(i, i ^ d) for i in range(group)])  13.3 us
    ppermute x7, starting transfers between devices, local(): lax.ppermute(piece, ('g', 'head'), [(i, i ^ d) for i in range(group)])  11.6 us
    pallas_call x2, Pallas kernels, project(): pl.pallas_call(kernel, out_shape=outs, in_specs=[pl.BlockSpec(memory_spac...  8.1 us
    all_to_all x1, starting transfers between devices, within_plane(): lax.all_to_all(x, plane_axes, split_axis=0, concat_axis=0, tiled=True)  6.2 us
    all_to_all x1, starting transfers between devices, local(): lax.all_to_all(parts, ('k', 'g'), split_axis=0, concat_axis=0, tiled=True)  4.76 us
    ppermute x1, waiting for transfers between devices, local(): received = lax.ppermute(sent, 'head', swap)  3.98 us
    pallas_call x2, Pallas kernels, attend(): pl.pallas_call(functools.partial(attend_kernel, heads, row_len, len(kv)),...  3.17 us
  transfers between devices with their start and end apart: 14, of which 8 were waited for; matrix products, arithmetic and copies ran while one was open for 0% of the time, Pallas kernels for 10%

profile of v3, /device:TPU:0, one launch (start us, length us, event | category | flops | bytes accessed | tf_op | source)
XLA Modules:
  0.0 76.2 jit_solution(7895900600634568194)
XLA Ops:
  0.6 1.7 %pack.1.after_ref = bf16[8,2,16,384]{3,2,1,0:T(8,128)(2,1)} custom-call(bf16[16,3072]{1,0:T(8,128)(2,1)} %refs_0_.2, bf16[16,3072]{1,0:T(8,128)(2,1)} %refs_1_.2), custom_call_target="tpu_custom_call" | custom-call | tf_op jit(solution)/shard_map/pack/pallas_call | solution.py:270
  2.3 6.2 %all-to-all-start = ((bf16[8,2,16,384]{3,2,1,0:T(8,128)(2,1)}), bf16[8,2,16,384]{3,2,1,0:T(8,128)(2,1)S(1)}, u32[]{:S(2)}, u32[]{:S(2)}) async-start(bf16[8,2,16,384]{3,2,1,0:T(8,128)(2,1)} %pack.1.after_ref), calls=%async_computation | async-start | bytes 393216 | tf_op jit(solution)/shard_map/all_to_all | solution.py:323
  8.6 2.2 %pieces.1 = (bf16[4,64,384]{2,1,0:T(8,128)(2,1)S(1)}, bf16[4,64,384]{2,1,0:T(8,128)(2,1)S(1)}, bf16[4,64,384]{2,1,0:T(8,128)(2,1)S(1)}, bf16[4,64,384]{2,1,0:T(8...) custom-call(s32[8]{0:T(128)S(1)} %fusion.1.columns_ref, ...), custom_call_target="tpu_custom_call" | custom-call | tf_op jit(solution)/shard_map/pieces/pallas_call | solution.py:302
  10.8 2.1 %collective-permute-start.1 = (bf16[4,64,384]{2,1,0:T(8,128)(2,1)S(1)}, bf16[4,64,384]{2,1,0:T(8,128)(2,1)S(1)}, u32[]{:S(2)}, u32[]{:S(2)}) collective-permute-start(bf16[4,64,384]{2,1,0:T(8,128)(2,1)S(1)} %get-tuple-element.13), channel_id=1, source_target_pairs={{0,1},{1,0},{4,5},{5,4},{8,9},{9,8},{12,13},{13,12},{2,3},{3,2},{6... | collective-permute-start | bytes 589832 | tf_op jit(solution)/shard_map/ppermute | solution.py:333
  12.9 1.5 %collective-permute-start.2 = (bf16[4,64,384]{2,1,0:T(8,128)(2,1)S(1)}, bf16[4,64,384]{2,1,0:T(8,128)(2,1)S(1)}, u32[]{:S(2)}, u32[]{:S(2)}) collective-permute-start(bf16[4,64,384]{2,1,0:T(8,128)(2,1)S(1)} %get-tuple-element.14), channel_id=1, source_target_pairs={{0,4},{1,5},{4,0},{5,1},{8,12},{9,13},{12,8},{13,9},{2,6},{3,7},{6... | collective-permute-start | bytes 589832 | tf_op jit(solution)/shard_map/ppermute | solution.py:333
  14.4 1.9 %collective-permute-start.4 = (bf16[4,64,384]{2,1,0:T(8,128)(2,1)S(1)}, bf16[4,64,384]{2,1,0:T(8,128)(2,1)S(1)}, u32[]{:S(2)}, u32[]{:S(2)}) collective-permute-start(bf16[4,64,384]{2,1,0:T(8,128)(2,1)S(1)} %get-tuple-element.16), channel_id=1, source_target_pairs={{0,8},{1,9},{4,12},{5,13},{8,0},{9,1},{12,4},{13,5},{2,10},{3,11},... | collective-permute-start | bytes 589832 | tf_op jit(solution)/shard_map/ppermute | solution.py:333
  16.4 2.6 %collective-permute-start = (bf16[8,2,16,384]{3,2,1,0:T(8,128)(2,1)S(1)}, bf16[8,2,16,384]{3,2,1,0:T(8,128)(2,1)S(1)}, u32[]{:S(2)}, u32[]{:S(2)}) collective-permute-start(bf16[8,2,16,384]{3,2,1,0:T(8,128)(2,1)S(1)} %all-to-all-done), channel_id=1, source_target_pairs={{0,16},{16,0},{1,17},{17,1},{2,18},{18,2},{3,19},{19,3},{4,20},{20... | collective-permute-start | bytes 589832 | tf_op jit(solution)/shard_map/ppermute | solution.py:337
  18.9 2.7 %collective-permute-start.5 = (bf16[4,64,384]{2,1,0:T(8,128)(2,1)S(1)}, bf16[4,64,384]{2,1,0:T(8,128)(2,1)S(1)}, u32[]{:S(2)}, u32[]{:S(2)}) collective-permute-start(bf16[4,64,384]{2,1,0:T(8,128)(2,1)S(1)} %get-tuple-element.17), channel_id=1, source_target_pairs={{0,9},{1,8},{4,13},{5,12},{8,1},{9,0},{12,5},{13,4},{2,11},{3,10},... | collective-permute-start | bytes 589832 | tf_op jit(solution)/shard_map/ppermute | solution.py:333
  21.9 3.3 %collective-permute-start.6 = (bf16[4,64,384]{2,1,0:T(8,128)(2,1)S(1)}, bf16[4,64,384]{2,1,0:T(8,128)(2,1)S(1)}, u32[]{:S(2)}, u32[]{:S(2)}) collective-permute-start(bf16[4,64,384]{2,1,0:T(8,128)(2,1)S(1)} %get-tuple-element.18), channel_id=1, source_target_pairs={{0,12},{1,13},{4,8},{5,9},{8,4},{9,5},{12,0},{13,1},{2,14},{3,15},... | collective-permute-start | bytes 589832 | tf_op jit(solution)/shard_map/ppermute | solution.py:333
  25.2 0.7 collective-permute-done.4.refs_6_
  25.9 0.5 collective-permute-start.9
  26.4 5.1 %collective-permute-done.5.refs_7_ = bf16[4,64,384]{2,1,0:T(8,128)(2,1)S(1)} collective-permute-done((bf16[4,64,384]{2,1,0:T(8,128)(2,1)S(1)}, bf16[4,64,384]{2,1,0:T(8,128)(2,1)S(1)}, u32[]{:S(2)}, u32[]{:S(2)}) %collective-permute-start.5) | collective-permute-done | bytes 196640 | tf_op jit(solution)/shard_map/ppermute | solution.py:333
  31.5 4.1 %collective-permute-done.6.refs_8_ = bf16[4,64,384]{2,1,0:T(8,128)(2,1)S(1)} collective-permute-done((bf16[4,64,384]{2,1,0:T(8,128)(2,1)S(1)}, bf16[4,64,384]{2,1,0:T(8,128)(2,1)S(1)}, u32[]{:S(2)}, u32[]{:S(2)}) %collective-permute-start.6) | collective-permute-done | bytes 196640 | tf_op jit(solution)/shard_map/ppermute | solution.py:333
  35.6 3.2 %collective-permute-done.7.refs_9_ = bf16[4,64,384]{2,1,0:T(8,128)(2,1)S(1)} collective-permute-done((bf16[4,64,384]{2,1,0:T(8,128)(2,1)S(1)}, bf16[4,64,384]{2,1,0:T(8,128)(2,1)S(1)}, u32[]{:S(2)}, u32[]{:S(2)}) %collective-permute-start.7) | collective-permute-done | bytes 196640 | tf_op jit(solution)/shard_map/ppermute | solution.py:333
  38.8 1.6 %attend.3 = bf16[2,4,32,896]{3,2,1,0:T(8,128)(2,1)S(1)} custom-call(s32[1]{0:T(128)} %bitcast.1.plane_ref, bf16[1,8,2,16,384]{4,3,2,1,0:T(8,128)(2,1)S(1)} %collective-permute-done.8.refs_0_, bf16[1,8,2,16,384]{4,3,2,1,0:T(8,128)(2,1)S(1)} %collective-permute-done.9.refs_1_, bf16[4,64,384]{2,1,0:T(8,128)(2,1)S(1)} %get-tuple-element.12.refs_2_, ...), custom_call_target="tpu_custom_call" | custom-call | tf_op jit(solution)/shard_map/attend/pallas_call | solution.py:107
  40.5 1.6 %attend.2 = bf16[2,4,32,896]{3,2,1,0:T(8,128)(2,1)S(1)} custom-call(s32[1]{0:T(128)} %bitcast.1.plane_ref, bf16[1,8,2,16,384]{4,3,2,1,0:T(8,128)(2,1)S(1)} %bitcast.10, bf16[1,8,2,16,384]{4,3,2,1,0:T(8,128)(2,1)S(1)} %bitcast.13, bf16[4,64,384]{2,1,0:T(8,128)(2,1)S(1)} %get-tuple-element.12.refs_2_, bf16[4,64,384]{2,1,0:T(8,128)(2,1)S(1)} %collective-permute-done.1.refs_3_, ...), custom_call_target="tpu_custom_call" | custom-call | tf_op jit(solution)/shard_map/attend/pallas_call | solution.py:107
  42.3 2.0 %merge_pair.1 = bf16[8,32,896]{2,1,0:T(8,128)(2,1)} custom-call(bf16[8,32,896]{2,1,0:T(8,128)(2,1)S(1)} %bitcast.8, bf16[8,32,896]{2,1,0:T(8,128)(2,1)S(1)} %collective-permute-done.10.away_ref), custom_call_target="tpu_custom_call" | custom-call | tf_op jit(solution)/shard_map/merge_pair/pallas_call | solution.py:183
  44.2 4.8 %all-to-all-start.1 = ((bf16[8,32,896]{2,1,0:T(8,128)(2,1)}), bf16[8,32,896]{2,1,0:T(8,128)(2,1)S(1)}, u32[]{:S(2)}, u32[]{:S(2)}) async-start(bf16[8,32,896]{2,1,0:T(8,128)(2,1)} %merge_pair.1), calls=%async_computation.1 | async-start | bytes 917504 | tf_op jit(solution)/shard_map/all_to_all | solution.py:348
  49.0 13.5 %all-to-all-done.1 = bf16[8,32,896]{2,1,0:T(8,128)(2,1)S(1)} async-done(((bf16[8,32,896]{2,1,0:T(8,128)(2,1)}), bf16[8,32,896]{2,1,0:T(8,128)(2,1)S(1)}, u32[]{:S(2)}, u32[]{:S(2)}) %all-to-all-start.1) | async-done | bytes 458784 | tf_op jit(solution)/shard_map/all_to_all | solution.py:348
  62.5 4.3 %project.2 = (bf16[64,2560]{1,0:T(8,128)(2,1)S(1)}, bf16[64,1536]{1,0:T(8,128)(2,1)S(1)}) custom-call(s32[1]{0:T(128)S(6)} %sub.7.half_ref, bf16[2,4,32,896]{3,2,1,0:T(8,128)(2,1)S(1)} %bitcast.7, bf16[1536,5120]{1,0:T(8,128)(2,1)} %weight_ref.3), custom_call_target="tpu_custom_call" | custom-call | flops 503316480 | bytes 7864320 | tf_op jit(solution)/shard_map/project/pallas_call | solution.py:231
  66.8 0.7 collective-permute-start.11
  67.5 3.8 %project.3 = f32[64,2560]{1,0:T(8,128)S(1)} custom-call(s32[1]{0:T(128)} %bitcast.half_ref, bf16[64,1536]{1,0:T(8,128)(2,1)S(1)} %get-tuple-element.20.both_ref, bf16[1536,5120]{1,0:T(8,128)(2,1)} %weight_ref.3), custom_call_target="tpu_custom_call" | custom-call | flops 503316480 | bytes 7864320 | tf_op jit(solution)/shard_map/project/pallas_call | solution.py:231
  71.4 4.0 %collective-permute-done.11 = bf16[64,2560]{1,0:T(8,128)(2,1)S(1)} collective-permute-done((bf16[64,2560]{1,0:T(8,128)(2,1)S(1)}, bf16[64,2560]{1,0:T(8,128)(2,1)S(1)}, u32[]{:S(2)}, u32[]{:S(2)}) %collective-permute-start.11) | collective-permute-done | bytes 327712 | tf_op jit(solution)/shard_map/ppermute | solution.py:357
  75.4 0.7 fusion.2
  (14 shorter events, 0.7 us)
Async XLA Ops:
  2.3 14.0 %all-to-all-start = ((bf16[8,2,16,384]{3,2,1,0:T(8,128)(2,1)}), bf16[8,2,16,384]{3,2,1,0:T(8,128)(2,1)S(1)}, u32[]{:S(2)}, u32[]{:S(2)}) async-start(bf16[8,2,16,384]{3,2,1,0:T(8,128)(2,1)} %pack.1.after_ref), calls=%async_computation | async-start | bytes 393216 | tf_op jit(solution)/shard_map/all_to_all | solution.py:323
  10.8 8.2 %collective-permute-start.1 = (bf16[4,64,384]{2,1,0:T(8,128)(2,1)S(1)}, bf16[4,64,384]{2,1,0:T(8,128)(2,1)S(1)}, u32[]{:S(2)}, u32[]{:S(2)}) collective-permute-start(bf16[4,64,384]{2,1,0:T(8,128)(2,1)S(1)} %get-tuple-element.13), channel_id=1, source_target_pairs={{0,1},{1,0},{4,5},{5,4},{8,9},{9,8},{12,13},{13,12},{2,3},{3,2},{6... | collective-permute-start | bytes 589832 | tf_op jit(solution)/shard_map/ppermute | solution.py:333
  12.9 9.0 %collective-permute-start.2 = (bf16[4,64,384]{2,1,0:T(8,128)(2,1)S(1)}, bf16[4,64,384]{2,1,0:T(8,128)(2,1)S(1)}, u32[]{:S(2)}, u32[]{:S(2)}) collective-permute-start(bf16[4,64,384]{2,1,0:T(8,128)(2,1)S(1)} %get-tuple-element.14), channel_id=1, source_target_pairs={{0,4},{1,5},{4,0},{5,1},{8,12},{9,13},{12,8},{13,9},{2,6},{3,7},{6... | collective-permute-start | bytes 589832 | tf_op jit(solution)/shard_map/ppermute | solution.py:333
  14.3 10.9 %collective-permute-start.3 = (bf16[4,64,384]{2,1,0:T(8,128)(2,1)S(1)}, bf16[4,64,384]{2,1,0:T(8,128)(2,1)S(1)}, u32[]{:S(2)}, u32[]{:S(2)}) collective-permute-start(bf16[4,64,384]{2,1,0:T(8,128)(2,1)S(1)} %get-tuple-element.15), channel_id=1, source_target_pairs={{0,5},{1,4},{4,1},{5,0},{8,13},{9,12},{12,9},{13,8},{2,7},{3,6},{6... | collective-permute-start | bytes 589832 | tf_op jit(solution)/shard_map/ppermute | solution.py:333
  14.4 11.5 %collective-permute-start.4 = (bf16[4,64,384]{2,1,0:T(8,128)(2,1)S(1)}, bf16[4,64,384]{2,1,0:T(8,128)(2,1)S(1)}, u32[]{:S(2)}, u32[]{:S(2)}) collective-permute-start(bf16[4,64,384]{2,1,0:T(8,128)(2,1)S(1)} %get-tuple-element.16), channel_id=1, source_target_pairs={{0,8},{1,9},{4,12},{5,13},{8,0},{9,1},{12,4},{13,5},{2,10},{3,11},... | collective-permute-start | bytes 589832 | tf_op jit(solution)/shard_map/ppermute | solution.py:333
  16.4 9.6 %collective-permute-start = (bf16[8,2,16,384]{3,2,1,0:T(8,128)(2,1)S(1)}, bf16[8,2,16,384]{3,2,1,0:T(8,128)(2,1)S(1)}, u32[]{:S(2)}, u32[]{:S(2)}) collective-permute-start(bf16[8,2,16,384]{3,2,1,0:T(8,128)(2,1)S(1)} %all-to-all-done), channel_id=1, source_target_pairs={{0,16},{16,0},{1,17},{17,1},{2,18},{18,2},{3,19},{19,3},{4,20},{20... | collective-permute-start | bytes 589832 | tf_op jit(solution)/shard_map/ppermute | solution.py:337
  18.9 12.5 %collective-permute-start.5 = (bf16[4,64,384]{2,1,0:T(8,128)(2,1)S(1)}, bf16[4,64,384]{2,1,0:T(8,128)(2,1)S(1)}, u32[]{:S(2)}, u32[]{:S(2)}) collective-permute-start(bf16[4,64,384]{2,1,0:T(8,128)(2,1)S(1)} %get-tuple-element.17), channel_id=1, source_target_pairs={{0,9},{1,8},{4,13},{5,12},{8,1},{9,0},{12,5},{13,4},{2,11},{3,10},... | collective-permute-start | bytes 589832 | tf_op jit(solution)/shard_map/ppermute | solution.py:333
  21.9 13.7 %collective-permute-start.6 = (bf16[4,64,384]{2,1,0:T(8,128)(2,1)S(1)}, bf16[4,64,384]{2,1,0:T(8,128)(2,1)S(1)}, u32[]{:S(2)}, u32[]{:S(2)}) collective-permute-start(bf16[4,64,384]{2,1,0:T(8,128)(2,1)S(1)} %get-tuple-element.18), channel_id=1, source_target_pairs={{0,12},{1,13},{4,8},{5,9},{8,4},{9,5},{12,0},{13,1},{2,14},{3,15},... | collective-permute-start | bytes 589832 | tf_op jit(solution)/shard_map/ppermute | solution.py:333
  25.2 13.5 %collective-permute-start.7 = (bf16[4,64,384]{2,1,0:T(8,128)(2,1)S(1)}, bf16[4,64,384]{2,1,0:T(8,128)(2,1)S(1)}, u32[]{:S(2)}, u32[]{:S(2)}) collective-permute-start(bf16[4,64,384]{2,1,0:T(8,128)(2,1)S(1)} %get-tuple-element.19), channel_id=1, source_target_pairs={{0,13},{1,12},{4,9},{5,8},{8,5},{9,4},{12,1},{13,0},{2,15},{3,14},... | collective-permute-start | bytes 589832 | tf_op jit(solution)/shard_map/ppermute | solution.py:333
  25.9 12.9 %collective-permute-start.8 = (bf16[1,8,2,16,384]{4,3,2,1,0:T(8,128)(2,1)S(1)}, bf16[1,8,2,16,384]{4,3,2,1,0:T(8,128)(2,1)S(1)}, u32[]{:S(2)}, u32[]{:S(2)}) collective-permute-start(bf16[1,8,2,16,384]{4,3,2,1,0:T(8,128)(2,1)S(1)} %bitcast.9), channel_id=1, source_target_pairs={{0,2},{2,0},{1,3},{3,1},{4,6},{6,4},{5,7},{7,5},{8,10},{10,8},{9,1... | collective-permute-start | bytes 589832 | tf_op jit(solution)/shard_map/ppermute | solution.py:340
  25.9 12.9 %collective-permute-start.9 = (bf16[1,8,2,16,384]{4,3,2,1,0:T(8,128)(2,1)S(1)}, bf16[1,8,2,16,384]{4,3,2,1,0:T(8,128)(2,1)S(1)}, u32[]{:S(2)}, u32[]{:S(2)}) collective-permute-start(bf16[1,8,2,16,384]{4,3,2,1,0:T(8,128)(2,1)S(1)} %bitcast.12), channel_id=1, source_target_pairs={{0,2},{2,0},{1,3},{3,1},{4,6},{6,4},{5,7},{7,5},{8,10},{10,8},{9,1... | collective-permute-start | bytes 589832 | tf_op jit(solution)/shard_map/ppermute | solution.py:340
  40.4 1.9 %collective-permute-start.10 = (bf16[8,32,896]{2,1,0:T(8,128)(2,1)S(1)}, bf16[8,32,896]{2,1,0:T(8,128)(2,1)S(1)}, u32[]{:S(2)}, u32[]{:S(2)}) collective-permute-start(bf16[8,32,896]{2,1,0:T(8,128)(2,1)S(1)} %bitcast.11), channel_id=1, source_target_pairs={{0,2},{2,0},{1,3},{3,1},{4,6},{6,4},{5,7},{7,5},{8,10},{10,8},{9,1... | collective-permute-start | bytes 1376264 | tf_op jit(solution)/shard_map/ppermute | solution.py:347
  44.2 18.3 %all-to-all-start.1 = ((bf16[8,32,896]{2,1,0:T(8,128)(2,1)}), bf16[8,32,896]{2,1,0:T(8,128)(2,1)S(1)}, u32[]{:S(2)}, u32[]{:S(2)}) async-start(bf16[8,32,896]{2,1,0:T(8,128)(2,1)} %merge_pair.1), calls=%async_computation.1 | async-start | bytes 917504 | tf_op jit(solution)/shard_map/all_to_all | solution.py:348
  66.8 8.6 %collective-permute-start.11 = (bf16[64,2560]{1,0:T(8,128)(2,1)S(1)}, bf16[64,2560]{1,0:T(8,128)(2,1)S(1)}, u32[]{:S(2)}, u32[]{:S(2)}) collective-permute-start(bf16[64,2560]{1,0:T(8,128)(2,1)S(1)} %get-tuple-element.21), channel_id=1, source_target_pairs={{0,1},{1,0},{2,3},{3,2},{4,5},{5,4},{6,7},{7,6},{8,9},{9,8},{10,11... | collective-permute-start | bytes 983048 | tf_op jit(solution)/shard_map/ppermute | solution.py:357

commit v4 on v3

v4 whole, which is shorter than its diff:
```python
import functools
import math

import jax
import jax.numpy as jnp
from jax import lax
from jax.experimental import pallas as pl
from jax.experimental.pallas import tpu as pltpu
from jax.sharding import Mesh, PartitionSpec as P

H = 24
DH = 128
NT = (((1,), (1,)), ((), ()))
TURNS = (0, 6, 1, 5, 2, 7, 4, 3)
ATTEND_VMEM = 24 * 2**20
PROJECT_VMEM = 20 * 2**20


def split_bf16(x, parts):
    terms = []
    for _ in range(parts):
        term = x.astype(jnp.bfloat16)
        terms.append(term)
        x = x - term.astype(jnp.float32)
    return terms


def attend_kernel(heads, row_len, group, plane_ref, *refs):
    query_refs, kv_refs, out_ref = refs[: -group - 1], refs[-group - 1 : -1], refs[-1]
    plane_rows = group * row_len
    g_count, head_axis = out_ref.shape[1], out_ref.shape[2] // row_len
    scale = DH ** (-0.5)

    def some_planes(blocks, planes):
        rows = len(blocks) * plane_rows
        lane = lax.broadcasted_iota(jnp.int32, (rows, DH), 1)
        lse = slopes_mean = jnp.zeros((rows, DH), jnp.float32)

        def put(x, columns):
            for i, plane in enumerate(planes):
                for head in range(head_axis):
                    for g in range(g_count):
                        here = i * plane_rows + (head * g_count + g) * row_len
                        there = slice(head * row_len, (head + 1) * row_len)
                        out_ref[plane, g, there, columns] = x[here : here + row_len]

        for h in range(heads):
            lanes = slice(h * DH, (h + 1) * DH)
            key, key_tan, value, value_tan = (
                jnp.concatenate([ref[t, :, lanes] for ref in kv_refs]) for t in range(4)
            )
            query, qtan = (
                jnp.concatenate(
                    [ref[j, :, t, :, lanes].reshape(plane_rows, DH) for ref, j in blocks]
                )
                for t in range(2)
            )
            scores = lax.dot_general(query, key, NT, preferred_element_type=jnp.float32) * scale
            slopes = (
                lax.dot_general(
                    jnp.concatenate([qtan, query], axis=1),
                    jnp.concatenate([key, key_tan], axis=1),
                    NT,
                    preferred_element_type=jnp.float32,
                )
                * scale
            )
            peak = jnp.max(scores, axis=1, keepdims=True)
            unnormed = jnp.exp(scores - peak)
            tilted = unnormed * slopes
            total = jnp.sum(unnormed, axis=1, keepdims=True)
            slope_sum = jnp.sum(tilted, axis=1, keepdims=True)
            sums = jnp.dot(
                unnormed.astype(jnp.bfloat16),
                jnp.concatenate([value, value_tan], axis=1),
                preferred_element_type=jnp.float32,
            )
            tilted_sum = jnp.dot(
                tilted.astype(jnp.bfloat16), value, preferred_element_type=jnp.float32
            )
            inv = 1.0 / total
            mean_slope = slope_sum * inv
            mean_value = sums[:, :DH] * inv
            tangent = (sums[:, DH:] + tilted_sum) * inv - mean_slope * mean_value
            both = jnp.concatenate([mean_value, tangent], axis=1).astype(jnp.bfloat16)
            put(both, slice(2 * h * DH, 2 * (h + 1) * DH))
            lse = jnp.where(lane == h, peak + jnp.log(total), lse)
            slopes_mean = jnp.where(lane == h, mean_slope, slopes_mean)
        put(packed_stats(lse, slopes_mean, heads), slice(2 * heads * DH, (2 * heads + 1) * DH))

    if len(query_refs) > 1:
        planes = [plane_ref[0] ^ d for d in range(len(query_refs))]
        some_planes([(ref, 0) for ref in query_refs], planes)
    else:
        (ref,) = query_refs
        count = math.gcd(ref.shape[0], 4)

        @pl.loop(0, ref.shape[0] // count)
        def _(step):
            planes = [step * count + j for j in range(count)]
            some_planes([(ref, j) for j in planes], planes)


def attend(queries, kv, plane, k, g_count, head_axis):
    heads = kv[0].shape[2] // DH
    row_len = queries[0].shape[3]
    out_shape = (k, g_count, head_axis * row_len, heads * 2 * DH + DH)
    whole = pl.BlockSpec(memory_space=pltpu.VMEM)
    return pl.pallas_call(
        functools.partial(attend_kernel, heads, row_len, len(kv)),
        out_shape=jax.ShapeDtypeStruct(out_shape, jnp.bfloat16),
        in_specs=[pl.BlockSpec(memory_space=pltpu.SMEM)] + [whole] * (len(queries) + len(kv)),
        out_specs=whole,
        compiler_params=pltpu.CompilerParams(vmem_limit_bytes=ATTEND_VMEM),
        name="attend",
    )(plane, *queries, *kv)


def packed_stats(lse, slope, heads):
    lane = lax.broadcasted_iota(jnp.int32, lse.shape, 1)
    total = 0.0
    terms = split_bf16(jnp.where(lane < heads, lse, 0.0), 3)
    terms += split_bf16(jnp.where(lane < heads, slope, 0.0), 2)
    for i, term in enumerate(terms):
        term = term.astype(jnp.float32)
        total += pltpu.roll(term, i * heads, 1) if i else term
    return total.astype(jnp.bfloat16)


def merge_stats(tails, heads):
    def term(tail, i):
        return pltpu.roll(tail, DH - i * heads, 1) if i else tail

    tails = [tail.astype(jnp.float32) for tail in tails]
    lse = [term(tail, 0) + term(tail, 1) + term(tail, 2) for tail in tails]
    slope = [term(tail, 3) + term(tail, 4) for tail in tails]
    top = functools.reduce(jnp.maximum, lse)
    share = [jnp.exp(e - top) for e in lse]
    total = sum(share)
    inv = 1.0 / total
    share = [e * inv for e in share]
    mean_slope = sum(e * s for e, s in zip(share, slope))
    shift = [e * (s - mean_slope) for e, s in zip(share, slope)]
    return share, shift, top + jnp.log(total), mean_slope


def merge_head(parts, share, shift, h):
    value = tangent = 0.0
    for part, e, s in zip(parts, share, shift):
        own = part[:, 2 * h * DH : (2 * h + 1) * DH].astype(jnp.float32)
        own_tan = part[:, (2 * h + 1) * DH : (2 * h + 2) * DH].astype(jnp.float32)
        e, s = e[:, h : h + 1], s[:, h : h + 1]
        value += e * own
        tangent += e * own_tan + s * own
    return value, tangent


def merge(place_ref, parts_refs, both_ref, heads, g_count):
    rows = parts_refs[0].shape[0]
    tail = slice(2 * heads * DH, (2 * heads + 1) * DH)
    for d in range(g_count):
        g = (place_ref[0] ^ d) % g_count
        parts = [ref[...] for ref in parts_refs[d::g_count]]
        share, shift, _, _ = merge_stats([part[:, tail] for part in parts], heads)
        for h in range(heads):
            value, tangent = merge_head(parts, share, shift, h)
            columns = pl.ds(pl.multiple_of((g * heads + h) * DH, DH), DH)
            both_ref[:rows, columns] = value.astype(jnp.bfloat16)
            both_ref[rows:, columns] = tangent.astype(jnp.bfloat16)


def pair_kernel(heads, place_ref, home_ref, away_ref, *out_refs):
    tail = slice(2 * heads * DH, (2 * heads + 1) * DH)
    for d, out_ref in enumerate(out_refs):
        parts = [ref[place_ref[0] ^ d] for ref in (home_ref, away_ref)]
        share, shift, lse, slope = merge_stats([part[:, tail] for part in parts], heads)
        for h in range(heads):
            both = jnp.concatenate(merge_head(parts, share, shift, h), axis=1)
            out_ref[:, 2 * h * DH : 2 * (h + 1) * DH] = both.astype(jnp.bfloat16)
        out_ref[:, tail] = packed_stats(lse, slope, heads)


def merge_pair(place, home, away, heads):
    whole = pl.BlockSpec(memory_space=pltpu.VMEM)
    count = home.shape[0]
    return pl.pallas_call(
        functools.partial(pair_kernel, heads),
        out_shape=[jax.ShapeDtypeStruct(home.shape[1:], home.dtype)] * count,
        in_specs=[pl.BlockSpec(memory_space=pltpu.SMEM), whole, whole],
        out_specs=[whole] * count,
        compiler_params=pltpu.CompilerParams(vmem_limit_bytes=ATTEND_VMEM),
        name="merge_pair",
    )(place, home, away)


def first_kernel(heads, g_count, half_ref, place_ref, weight_ref, *refs):
    *parts_refs, out_ref, both_ref, held, sems = refs
    copies = fetch(half_ref, weight_ref, held, sems)
    merge(place_ref, parts_refs, both_ref, heads, g_count)
    times_held(copies, both_ref, out_ref, held)


def second_kernel(half_ref, place_ref, weight_ref, both_ref, out_ref, held, sems):
    times_held(fetch(half_ref, weight_ref, held, sems), both_ref, out_ref, held)


def fetch(half_ref, weight_ref, held, sems):
    chunks, _, tile = held.shape
    copies = []
    for i in range(chunks):
        first = pl.multiple_of((half_ref[0] * chunks + i) * tile, tile)
        copy = pltpu.make_async_copy(weight_ref.at[:, pl.ds(first, tile)], held.at[i], sems.at[i])
        copy.start()
        copies.append(copy)
    return copies


def times_held(copies, both_ref, out_ref, held):
    tile = held.shape[2]
    for i, copy in enumerate(copies):
        copy.wait()
        out_ref[:, i * tile : (i + 1) * tile] = jnp.dot(
            both_ref[...], held[i], preferred_element_type=jnp.float32
        ).astype(out_ref.dtype)


def project(kernel, half, place, left, weight, width, dtype, merged=None):
    depth = weight.shape[0]
    chunks = 4
    rows = merged[0] if merged else left[0].shape[0]
    outs = [jax.ShapeDtypeStruct((rows, width), dtype)]
    if merged:
        outs.append(jax.ShapeDtypeStruct(merged, jnp.bfloat16))
    whole = pl.BlockSpec(memory_space=pltpu.VMEM)
    scalar = pl.BlockSpec(memory_space=pltpu.SMEM)
    return pl.pallas_call(
        kernel,
        out_shape=outs,
        in_specs=[scalar, scalar, pl.BlockSpec(memory_space=pl.ANY)] + [whole] * len(left),
        out_specs=[whole] * len(outs),
        scratch_shapes=[
            pltpu.VMEM((chunks, depth, width // chunks), jnp.bfloat16),
            pltpu.SemaphoreType.DMA((chunks,)),
        ],
        compiler_params=pltpu.CompilerParams(vmem_limit_bytes=PROJECT_VMEM),
        cost_estimate=pl.CostEstimate(
            flops=2 * rows * depth * width, bytes_accessed=2 * depth * width, transcendentals=0
        ),
        name="project",
    )(half, place, pltpu.with_memory_space_constraint(weight, pltpu.HBM), *left)


def pack_kernel(turns, g_count, head_axis, place_ref, *refs):
    group = len(turns)
    matrix_refs, query_ref, piece_refs, sems = refs[:6], refs[6], refs[7:-1], refs[-1]
    width = query_ref.shape[3]
    copies = []

    def copy(ref, first, to, *sem):
        columns = pl.ds(pl.multiple_of(first * width, width), width)
        copies.append(pltpu.make_async_copy(ref.at[:, columns], to, sems.at[sem]))

    for i in range(group):
        for t in range(2):
            copy(matrix_refs[t], i, query_ref.at[i, t], i, t)
    for i, turn in enumerate(turns):
        partner = place_ref[0] ^ turn
        column = (partner % head_axis) * g_count + partner // head_axis
        for t in range(4):
            copy(matrix_refs[2 + t], column, piece_refs[i].at[t], i, 2 + t)
    for each in copies:
        each.start()
    for each in copies:
        each.wait()


def pack(turns, g_count, head_axis, place, *matrices):
    group = len(turns)
    rows, columns = matrices[0].shape
    width = columns // group
    piece = jax.ShapeDtypeStruct((4, matrices[2].shape[0], width), jnp.bfloat16)
    outs = [jax.ShapeDtypeStruct((group, 2, rows, width), jnp.bfloat16)] + [piece] * group
    return pl.pallas_call(
        functools.partial(pack_kernel, turns, g_count, head_axis),
        out_shape=outs,
        in_specs=[pl.BlockSpec(memory_space=pltpu.SMEM)]
        + [pl.BlockSpec(memory_space=pl.ANY)] * len(matrices),
        out_specs=[pl.BlockSpec(memory_space=pltpu.VMEM)] * len(outs),
        scratch_shapes=[pltpu.SemaphoreType.DMA((group, len(matrices)))],
        compiler_params=pltpu.CompilerParams(vmem_limit_bytes=8 * 2**20),
        name="pack",
    )(place, *(pltpu.with_memory_space_constraint(m, pltpu.HBM) for m in matrices))


def local(queries, query_tangent, key_rows, key_tangent, value_rows, value_tangent, out_weight):
    k, g_count, head_axis = (lax.axis_size(a) for a in ("k", "g", "head"))
    plane_axes = ("head", "g")
    group = g_count * head_axis
    heads = H // group
    rows = queries.shape[0] * head_axis
    swap = [(0, 1), (1, 0)]

    def within_plane(x):
        return lax.all_to_all(x, plane_axes, split_axis=0, concat_axis=0, tiled=True)

    turns = sorted(range(group), key=TURNS.index)
    in_plane = lax.axis_index(("g", "head")).astype(jnp.int32).reshape(1)
    packed_queries, *kv = pack(
        turns,
        g_count,
        head_axis,
        in_plane,
        queries,
        query_tangent,
        key_rows,
        key_tangent,
        value_rows,
        value_tangent,
    )
    plane_queries = within_plane(packed_queries)
    kv = [
        lax.ppermute(piece, ("g", "head"), [(i, i ^ d) for i in range(group)]) if d else piece
        for d, piece in zip(turns, kv)
    ]
    if k == 2:
        home_queries = [plane_queries[None], lax.ppermute(plane_queries, "k", swap)[None]]
    else:
        home_queries = [lax.all_gather(plane_queries, "k", axis=0, tiled=False)]
    away_queries = [lax.ppermute(q, "core", swap) for q in home_queries]

    plane = lax.axis_index("k").astype(jnp.int32).reshape(1)
    away, home = (
        attend(some, kv, plane, k, g_count, head_axis).reshape(k * g_count, rows, -1)
        for some in (away_queries, home_queries)
    )
    place = lax.axis_index(("k", "g")).astype(jnp.int32).reshape(1)
    parts = merge_pair(place, home, lax.ppermute(away, "core", swap), heads)
    count = k * g_count
    parts = [
        lax.ppermute(part, ("k", "g"), [(i, i ^ d) for i in range(count)]) if d else part
        for d, part in enumerate(parts)
    ]

    width = out_weight.shape[1] // head_axis
    mine = lax.axis_index("head").astype(jnp.int32).reshape(1)
    merged = (2 * rows, out_weight.shape[0])
    merging = functools.partial(first_kernel, heads, g_count)
    if head_axis == 2:
        sent, both = project(
            merging, 1 - mine, place, parts, out_weight, width, jnp.bfloat16, merged
        )
        received = lax.ppermute(sent, "head", swap)
        (own,) = project(second_kernel, mine, place, [both], out_weight, width, jnp.float32)
        total = own + received.astype(jnp.float32)
    else:
        partial, _ = project(
            merging, 0 * mine, place, parts, out_weight, width * head_axis, jnp.float32, merged
        )
        total = lax.psum_scatter(partial, "head", scatter_dimension=1, tiled=True)
    total = total.astype(jnp.bfloat16)
    return (total[:rows], total[rows:])


def solution(mesh):
    blk, head_axis = mesh.shape["blk"], mesh.shape["head"]
    g_count = math.gcd(H // head_axis, blk // 2)
    fine = Mesh(
        mesh.devices.reshape(blk // (2 * g_count), g_count, 2, head_axis),
        ("k", "g", "core", "head"),
    )
    rows = P(("k", "g", "core", "head"), None)
    return jax.shard_map(
        local,
        mesh=fine,
        in_specs=(rows,) * 6 + (P("head", None),),
        out_specs=(P(("k", "g", "core"), "head"),) * 2,
        check_vma=False,
    )
```

time: 76.6 us -> 70.6 us (0.922)
  waiting for transfers between devices: 31.1 us -> 23.1 us
  starting transfers between devices: 26.4 us -> 30.5 us
  Pallas kernels: 17.2 us -> 15.1 us
    all_to_all x1 -> x0, waiting for transfers between devices: 13.5 us -> none  [local(): lax.all_to_all(parts, ('k', 'g'), split_axis=0, concat_axis=0, tiled=True)]
    ppermute x1 -> x8, starting transfers between devices: 0.07 us -> 11.3 us  [the longest x7 11.2 us: local(): lax.ppermute(part, ('k', 'g'), [(i, i ^ d) for i in range(count)])]
    ppermute x1 -> x8, waiting for transfers between devices: 0.21 us -> 5.51 us  [the longest x7 5.21 us: local(): lax.ppermute(part, ('k', 'g'), [(i, i ^ d) for i in range(count)])]
    all_to_all x1 -> x0, starting transfers between devices: 4.76 us -> none  [local(): lax.all_to_all(parts, ('k', 'g'), split_axis=0, concat_axis=0, tiled=True)]
    all_to_all x1, waiting for transfers between devices: 0.01 us -> 3.05 us  [within_plane(): lax.all_to_all(x, plane_axes, split_axis=0, concat_axis=0, tiled=True)]
    ppermute x7, starting transfers between devices: 11.6 us -> 9.4 us  [local(): lax.ppermute(piece, ('g', 'head'), [(i, i ^ d) for i in range(group)])]
    pallas_call x5 -> x4, Pallas kernels: 14 us -> 12.2 us  [the longest x2 8.1 us: project(): pl.pallas_call(kernel, out_shape=outs, in_specs=[scalar, scalar, pl.Block...]
    ppermute x7, waiting for transfers between devices: 13.3 us -> 11.8 us  [local(): lax.ppermute(piece, ('g', 'head'), [(i, i ^ d) for i in range(group)])]
  transfers between devices with their start and end apart: 14 -> 20, of which waited for: 8 -> 11; matrix products, arithmetic and copies ran while one was open for 0% -> 0% of each run, Pallas kernels for 10% -> 8%
where the time goes in v4:
time: 70.6 us; the launch traced here: 70.3 us
  starting transfers between devices  30.5 us (43%)
  waiting for transfers between devices  23.1 us (33%)
  Pallas kernels  15.1 us (21%)
  local copies, waits for them, and re-layouts  0.74 us (1%)
  between operations  0.73 us (1%)
    ppermute x7, waiting for transfers between devices, local(): lax.ppermute(piece, ('g', 'head'), [(i, i ^ d) for i in range(group)])  11.8 us
    ppermute x7, starting transfers between devices, local(): lax.ppermute(part, ('k', 'g'), [(i, i ^ d) for i in range(count)])  11.2 us
    ppermute x7, starting transfers between devices, local(): lax.ppermute(piece, ('g', 'head'), [(i, i ^ d) for i in range(group)])  9.4 us
    pallas_call x2, Pallas kernels, project(): pl.pallas_call(kernel, out_shape=outs, in_specs=[scalar, scalar, pl.Block...  8.1 us
    all_to_all x1, starting transfers between devices, within_plane(): lax.all_to_all(x, plane_axes, split_axis=0, concat_axis=0, tiled=True)  6.2 us
    ppermute x7, waiting for transfers between devices, local(): lax.ppermute(part, ('k', 'g'), [(i, i ^ d) for i in range(count)])  5.21 us
    all_to_all x1, waiting for transfers between devices, within_plane(): lax.all_to_all(x, plane_axes, split_axis=0, concat_axis=0, tiled=True)  3.05 us
    pallas_call x2, Pallas kernels, attend(): pl.pallas_call(functools.partial(attend_kernel, heads, row_len, len(kv)),...  2.97 us
  transfers between devices with their start and end apart: 20, of which 11 were waited for; matrix products, arithmetic and copies ran while one was open for 0% of the time, Pallas kernels for 8%

profile of v4, /device:TPU:0, one launch (start us, length us, event | category | flops | bytes accessed | tf_op | source)
XLA Modules:
  0.0 70.3 jit_solution(13468061183382560720)
XLA Ops:
  0.6 2.6 %pack.1 = (bf16[8,2,16,384]{3,2,1,0:T(8,128)(2,1)}, bf16[4,64,384]{2,1,0:T(8,128)(2,1)S(1)}, bf16[4,64,384]{2,1,0:T(8,128)(2,1)S(1)}, bf16[4,64,384]{2,1,0:T(8,1...) custom-call(s32[1]{0:T(128)} %bitcast.3.place_ref, ...), custom_call_target="tpu_custom_call" | custom-call | tf_op jit(solution)/shard_map/pack/pallas_call | solution.py:283
  3.3 6.2 %all-to-all-start = ((bf16[8,2,16,384]{3,2,1,0:T(8,128)(2,1)}), bf16[8,2,16,384]{3,2,1,0:T(8,128)(2,1)S(1)}, u32[]{:S(2)}, u32[]{:S(2)}) async-start(bf16[8,2,16,384]{3,2,1,0:T(8,128)(2,1)} %get-tuple-element.21), calls=%async_computation | async-start | bytes 393216 | tf_op jit(solution)/shard_map/all_to_all | solution.py:304
  9.5 2.9 %collective-permute-start.1 = (bf16[4,64,384]{2,1,0:T(8,128)(2,1)S(1)}, bf16[4,64,384]{2,1,0:T(8,128)(2,1)S(1)}, u32[]{:S(2)}, u32[]{:S(2)}) collective-permute-start(bf16[4,64,384]{2,1,0:T(8,128)(2,1)S(1)} %get-tuple-element.23), channel_id=1, source_target_pairs={{0,12},{1,13},{4,8},{5,9},{8,4},{9,5},{12,0},{13,1},{2,14},{3,15},... | collective-permute-start | bytes 589832 | tf_op jit(solution)/shard_map/ppermute | solution.py:322
  12.4 1.5 %collective-permute-start.2 = (bf16[4,64,384]{2,1,0:T(8,128)(2,1)S(1)}, bf16[4,64,384]{2,1,0:T(8,128)(2,1)S(1)}, u32[]{:S(2)}, u32[]{:S(2)}) collective-permute-start(bf16[4,64,384]{2,1,0:T(8,128)(2,1)S(1)} %get-tuple-element.24), channel_id=1, source_target_pairs={{0,1},{1,0},{4,5},{5,4},{8,9},{9,8},{12,13},{13,12},{2,3},{3,2},{6... | collective-permute-start | bytes 589832 | tf_op jit(solution)/shard_map/ppermute | solution.py:322
  14.4 3.0 %all-to-all-done = bf16[8,2,16,384]{3,2,1,0:T(8,128)(2,1)S(1)} async-done(((bf16[8,2,16,384]{3,2,1,0:T(8,128)(2,1)}), bf16[8,2,16,384]{3,2,1,0:T(8,128)(2,1)S(1)}, u32[]{:S(2)}, u32[]{:S(2)}) %all-to-all-start) | async-done | bytes 196640 | tf_op jit(solution)/shard_map/all_to_all | solution.py:304
  17.5 2.6 %collective-permute-start = (bf16[8,2,16,384]{3,2,1,0:T(8,128)(2,1)S(1)}, bf16[8,2,16,384]{3,2,1,0:T(8,128)(2,1)S(1)}, u32[]{:S(2)}, u32[]{:S(2)}) collective-permute-start(bf16[8,2,16,384]{3,2,1,0:T(8,128)(2,1)S(1)} %all-to-all-done), channel_id=1, source_target_pairs={{0,16},{16,0},{1,17},{17,1},{2,18},{18,2},{3,19},{19,3},{4,20},{20... | collective-permute-start | bytes 589832 | tf_op jit(solution)/shard_map/ppermute | solution.py:326
  20.1 4.6 %collective-permute-done.1.refs_3_ = bf16[4,64,384]{2,1,0:T(8,128)(2,1)S(1)} collective-permute-done((bf16[4,64,384]{2,1,0:T(8,128)(2,1)S(1)}, bf16[4,64,384]{2,1,0:T(8,128)(2,1)S(1)}, u32[]{:S(2)}, u32[]{:S(2)}) %collective-permute-start.1) | collective-permute-done | bytes 196640 | tf_op jit(solution)/shard_map/ppermute | solution.py:322
  25.2 2.5 %collective-permute-start.6 = (bf16[4,64,384]{2,1,0:T(8,128)(2,1)S(1)}, bf16[4,64,384]{2,1,0:T(8,128)(2,1)S(1)}, u32[]{:S(2)}, u32[]{:S(2)}) collective-permute-start(bf16[4,64,384]{2,1,0:T(8,128)(2,1)S(1)} %get-tuple-element.28), channel_id=1, source_target_pairs={{0,8},{1,9},{4,12},{5,13},{8,0},{9,1},{12,4},{13,5},{2,10},{3,11},... | collective-permute-start | bytes 589832 | tf_op jit(solution)/shard_map/ppermute | solution.py:322
  27.6 1.3 %collective-permute-done.3.refs_5_ = bf16[4,64,384]{2,1,0:T(8,128)(2,1)S(1)} collective-permute-done((bf16[4,64,384]{2,1,0:T(8,128)(2,1)S(1)}, bf16[4,64,384]{2,1,0:T(8,128)(2,1)S(1)}, u32[]{:S(2)}, u32[]{:S(2)}) %collective-permute-start.3) | collective-permute-done | bytes 196640 | tf_op jit(solution)/shard_map/ppermute | solution.py:322
  28.9 1.5 %collective-permute-start.7 = (bf16[4,64,384]{2,1,0:T(8,128)(2,1)S(1)}, bf16[4,64,384]{2,1,0:T(8,128)(2,1)S(1)}, u32[]{:S(2)}, u32[]{:S(2)}) collective-permute-start(bf16[4,64,384]{2,1,0:T(8,128)(2,1)S(1)} %get-tuple-element.29), channel_id=1, source_target_pairs={{0,5},{1,4},{4,1},{5,0},{8,13},{9,12},{12,9},{13,8},{2,7},{3,6},{6... | collective-permute-start | bytes 589832 | tf_op jit(solution)/shard_map/ppermute | solution.py:322
  30.9 3.4 %collective-permute-done.5.refs_7_ = bf16[4,64,384]{2,1,0:T(8,128)(2,1)S(1)} collective-permute-done((bf16[4,64,384]{2,1,0:T(8,128)(2,1)S(1)}, bf16[4,64,384]{2,1,0:T(8,128)(2,1)S(1)}, u32[]{:S(2)}, u32[]{:S(2)}) %collective-permute-start.5) | collective-permute-done | bytes 196640 | tf_op jit(solution)/shard_map/ppermute | solution.py:322
  35.0 1.8 %collective-permute-done.7.refs_9_ = bf16[4,64,384]{2,1,0:T(8,128)(2,1)S(1)} collective-permute-done((bf16[4,64,384]{2,1,0:T(8,128)(2,1)S(1)}, bf16[4,64,384]{2,1,0:T(8,128)(2,1)S(1)}, u32[]{:S(2)}, u32[]{:S(2)}) %collective-permute-start.7) | collective-permute-done | bytes 196640 | tf_op jit(solution)/shard_map/ppermute | solution.py:322
  36.8 1.5 %attend.3 = bf16[2,4,32,896]{3,2,1,0:T(8,128)(2,1)S(1)} custom-call(s32[1]{0:T(128)} %bitcast.2.plane_ref, bf16[1,8,2,16,384]{4,3,2,1,0:T(8,128)(2,1)S(1)} %collective-permute-done.8.refs_0_, bf16[1,8,2,16,384]{4,3,2,1,0:T(8,128)(2,1)S(1)} %collective-permute-done.9.refs_1_, bf16[4,64,384]{2,1,0:T(8,128)(2,1)S(1)} %get-tuple-element.22.refs_2_, ...), custom_call_target="tpu_custom_call" | custom-call | tf_op jit(solution)/shard_map/attend/pallas_call | solution.py:109
  38.4 1.5 %attend.2 = bf16[2,4,32,896]{3,2,1,0:T(8,128)(2,1)S(1)} custom-call(s32[1]{0:T(128)} %bitcast.2.plane_ref, bf16[1,8,2,16,384]{4,3,2,1,0:T(8,128)(2,1)S(1)} %bitcast.10, bf16[1,8,2,16,384]{4,3,2,1,0:T(8,128)(2,1)S(1)} %bitcast.13, bf16[4,64,384]{2,1,0:T(8,128)(2,1)S(1)} %get-tuple-element.22.refs_2_, bf16[4,64,384]{2,1,0:T(8,128)(2,1)S(1)} %collective-permute-done.1.refs_3_, ...), custom_call_target="tpu_custom_call" | custom-call | tf_op jit(solution)/shard_map/attend/pallas_call | solution.py:109
  40.2 1.4 %merge_pair.1 = (bf16[32,896]{1,0:T(8,128)(2,1)S(1)}, bf16[32,896]{1,0:T(8,128)(2,1)S(1)}, bf16[32,896]{1,0:T(8,128)(2,1)S(1)}, bf16[32,896]{1,0:T(8,128)(2,1)S(...) custom-call(s32[1]{0:T(128)} %bitcast.1.place_ref, ...), custom_call_target="tpu_custom_call" | custom-call | tf_op jit(solution)/shard_map/merge_pair/pallas_call | solution.py:186
  42.5 2.6 %collective-permute-start.13 = (bf16[32,896]{1,0:T(8,128)(2,1)S(1)}, bf16[32,896]{1,0:T(8,128)(2,1)S(1)}, u32[]{:S(2)}, u32[]{:S(2)}) collective-permute-start(bf16[32,896]{1,0:T(8,128)(2,1)S(1)} %get-tuple-element.33), channel_id=1, source_target_pairs={{0,12},{4,8},{8,4},{12,0},{16,28},{20,24},{24,20},{28,16},{1,13},{... | collective-permute-start | bytes 172040 | tf_op jit(solution)/shard_map/ppermute | solution.py:340
  45.2 1.1 %collective-permute-start.14 = (bf16[32,896]{1,0:T(8,128)(2,1)S(1)}, bf16[32,896]{1,0:T(8,128)(2,1)S(1)}, u32[]{:S(2)}, u32[]{:S(2)}) collective-permute-start(bf16[32,896]{1,0:T(8,128)(2,1)S(1)} %get-tuple-element.34), channel_id=1, source_target_pairs={{0,16},{4,20},{8,24},{12,28},{16,0},{20,4},{24,8},{28,12},{1,17},{... | collective-permute-start | bytes 172040 | tf_op jit(solution)/shard_map/ppermute | solution.py:340
  46.3 1.8 %collective-permute-start.15 = (bf16[32,896]{1,0:T(8,128)(2,1)S(1)}, bf16[32,896]{1,0:T(8,128)(2,1)S(1)}, u32[]{:S(2)}, u32[]{:S(2)}) collective-permute-start(bf16[32,896]{1,0:T(8,128)(2,1)S(1)} %get-tuple-element.35), channel_id=1, source_target_pairs={{0,20},{4,16},{8,28},{12,24},{16,4},{20,0},{24,12},{28,8},{1,21},{... | collective-permute-start | bytes 172040 | tf_op jit(solution)/shard_map/ppermute | solution.py:340
  48.1 3.0 %collective-permute-start.16 = (bf16[32,896]{1,0:T(8,128)(2,1)S(1)}, bf16[32,896]{1,0:T(8,128)(2,1)S(1)}, u32[]{:S(2)}, u32[]{:S(2)}) collective-permute-start(bf16[32,896]{1,0:T(8,128)(2,1)S(1)} %get-tuple-element.36), channel_id=1, source_target_pairs={{0,24},{4,28},{8,16},{12,20},{16,8},{20,12},{24,0},{28,4},{1,25},{... | collective-permute-start | bytes 172040 | tf_op jit(solution)/shard_map/ppermute | solution.py:340
  51.1 1.8 %collective-permute-start.17 = (bf16[32,896]{1,0:T(8,128)(2,1)S(1)}, bf16[32,896]{1,0:T(8,128)(2,1)S(1)}, u32[]{:S(2)}, u32[]{:S(2)}) collective-permute-start(bf16[32,896]{1,0:T(8,128)(2,1)S(1)} %get-tuple-element.37), channel_id=1, source_target_pairs={{0,28},{4,24},{8,20},{12,16},{16,12},{20,8},{24,4},{28,0},{1,29},{... | collective-permute-start | bytes 172040 | tf_op jit(solution)/shard_map/ppermute | solution.py:340
  54.4 3.7 %collective-permute-done.17.refs_7_ = bf16[32,896]{1,0:T(8,128)(2,1)S(1)} collective-permute-done((bf16[32,896]{1,0:T(8,128)(2,1)S(1)}, bf16[32,896]{1,0:T(8,128)(2,1)S(1)}, u32[]{:S(2)}, u32[]{:S(2)}) %collective-permute-start.17) | collective-permute-done | bytes 57376 | tf_op jit(solution)/shard_map/ppermute | solution.py:340
  58.0 4.3 %project.2 = (bf16[64,2560]{1,0:T(8,128)(2,1)S(1)}, bf16[64,1536]{1,0:T(8,128)(2,1)S(1)}) custom-call(s32[1]{0:T(128)S(6)} %sub.3.half_ref, s32[1]{0:T(128)} %bitcast.1.place_ref, bf16[1536,5120]{1,0:T(8,128)(2,1)} %weight_ref.3, bf16[32,896]{1,0:T(8,128)(2,1)S(1)} %get-tuple-element.30.refs_0_, bf16[32,896]{1,0:T(8,128)(2,1)S(1)} %collective-permute-done.11.refs_1_, ...), custom_call_target="tpu_custom_call" | custom-call | flops 503316480 | bytes 7864320 | tf_op jit(solution)/shard_map/project/pallas_call | solution.py:236
  62.9 3.8 %project.3 = f32[64,2560]{1,0:T(8,128)S(1)} custom-call(s32[1]{0:T(128)} %bitcast.half_ref, s32[1]{0:T(128)} %bitcast.1.place_ref, bf16[1536,5120]{1,0:T(8,128)(2,1)} %weight_ref.3, bf16[64,1536]{1,0:T(8,128)(2,1)S(1)} %get-tuple-element.38.both_ref), custom_call_target="tpu_custom_call" | custom-call | flops 503316480 | bytes 7864320 | tf_op jit(solution)/shard_map/project/pallas_call | solution.py:236
  66.7 2.7 %collective-permute-done.18 = bf16[64,2560]{1,0:T(8,128)(2,1)S(1)} collective-permute-done((bf16[64,2560]{1,0:T(8,128)(2,1)S(1)}, bf16[64,2560]{1,0:T(8,128)(2,1)S(1)}, u32[]{:S(2)}, u32[]{:S(2)}) %collective-permute-start.18) | collective-permute-done | bytes 327712 | tf_op jit(solution)/shard_map/ppermute | solution.py:352
  (24 shorter events, 6.4 us)
Async XLA Ops:
  3.3 14.2 %all-to-all-start = ((bf16[8,2,16,384]{3,2,1,0:T(8,128)(2,1)}), bf16[8,2,16,384]{3,2,1,0:T(8,128)(2,1)S(1)}, u32[]{:S(2)}, u32[]{:S(2)}) async-start(bf16[8,2,16,384]{3,2,1,0:T(8,128)(2,1)} %get-tuple-element.21), calls=%async_computation | async-start | bytes 393216 | tf_op jit(solution)/shard_map/all_to_all | solution.py:304
  9.5 15.2 %collective-permute-start.1 = (bf16[4,64,384]{2,1,0:T(8,128)(2,1)S(1)}, bf16[4,64,384]{2,1,0:T(8,128)(2,1)S(1)}, u32[]{:S(2)}, u32[]{:S(2)}) collective-permute-start(bf16[4,64,384]{2,1,0:T(8,128)(2,1)S(1)} %get-tuple-element.23), channel_id=1, source_target_pairs={{0,12},{1,13},{4,8},{5,9},{8,4},{9,5},{12,0},{13,1},{2,14},{3,15},... | collective-permute-start | bytes 589832 | tf_op jit(solution)/shard_map/ppermute | solution.py:322
  12.4 12.8 %collective-permute-start.2 = (bf16[4,64,384]{2,1,0:T(8,128)(2,1)S(1)}, bf16[4,64,384]{2,1,0:T(8,128)(2,1)S(1)}, u32[]{:S(2)}, u32[]{:S(2)}) collective-permute-start(bf16[4,64,384]{2,1,0:T(8,128)(2,1)S(1)} %get-tuple-element.24), channel_id=1, source_target_pairs={{0,1},{1,0},{4,5},{5,4},{8,9},{9,8},{12,13},{13,12},{2,3},{3,2},{6... | collective-permute-start | bytes 589832 | tf_op jit(solution)/shard_map/ppermute | solution.py:322
  13.9 15.1 %collective-permute-start.3 = (bf16[4,64,384]{2,1,0:T(8,128)(2,1)S(1)}, bf16[4,64,384]{2,1,0:T(8,128)(2,1)S(1)}, u32[]{:S(2)}, u32[]{:S(2)}) collective-permute-start(bf16[4,64,384]{2,1,0:T(8,128)(2,1)S(1)} %get-tuple-element.25), channel_id=1, source_target_pairs={{0,9},{1,8},{4,13},{5,12},{8,1},{9,0},{12,5},{13,4},{2,11},{3,10},... | collective-permute-start | bytes 589832 | tf_op jit(solution)/shard_map/ppermute | solution.py:322
  14.4 16.0 %collective-permute-start.4 = (bf16[4,64,384]{2,1,0:T(8,128)(2,1)S(1)}, bf16[4,64,384]{2,1,0:T(8,128)(2,1)S(1)}, u32[]{:S(2)}, u32[]{:S(2)}) collective-permute-start(bf16[4,64,384]{2,1,0:T(8,128)(2,1)S(1)} %get-tuple-element.26), channel_id=1, source_target_pairs={{0,4},{1,5},{4,0},{5,1},{8,12},{9,13},{12,8},{13,9},{2,6},{3,7},{6... | collective-permute-start | bytes 589832 | tf_op jit(solution)/shard_map/ppermute | solution.py:322
  17.5 12.9 %collective-permute-start = (bf16[8,2,16,384]{3,2,1,0:T(8,128)(2,1)S(1)}, bf16[8,2,16,384]{3,2,1,0:T(8,128)(2,1)S(1)}, u32[]{:S(2)}, u32[]{:S(2)}) collective-permute-start(bf16[8,2,16,384]{3,2,1,0:T(8,128)(2,1)S(1)} %all-to-all-done), channel_id=1, source_target_pairs={{0,16},{16,0},{1,17},{17,1},{2,18},{18,2},{3,19},{19,3},{4,20},{20... | collective-permute-start | bytes 589832 | tf_op jit(solution)/shard_map/ppermute | solution.py:326
  24.7 9.6 %collective-permute-start.5 = (bf16[4,64,384]{2,1,0:T(8,128)(2,1)S(1)}, bf16[4,64,384]{2,1,0:T(8,128)(2,1)S(1)}, u32[]{:S(2)}, u32[]{:S(2)}) collective-permute-start(bf16[4,64,384]{2,1,0:T(8,128)(2,1)S(1)} %get-tuple-element.27), channel_id=1, source_target_pairs={{0,13},{1,12},{4,9},{5,8},{8,5},{9,4},{12,1},{13,0},{2,15},{3,14},... | collective-permute-start | bytes 589832 | tf_op jit(solution)/shard_map/ppermute | solution.py:322
  25.2 9.8 %collective-permute-start.6 = (bf16[4,64,384]{2,1,0:T(8,128)(2,1)S(1)}, bf16[4,64,384]{2,1,0:T(8,128)(2,1)S(1)}, u32[]{:S(2)}, u32[]{:S(2)}) collective-permute-start(bf16[4,64,384]{2,1,0:T(8,128)(2,1)S(1)} %get-tuple-element.28), channel_id=1, source_target_pairs={{0,8},{1,9},{4,12},{5,13},{8,0},{9,1},{12,4},{13,5},{2,10},{3,11},... | collective-permute-start | bytes 589832 | tf_op jit(solution)/shard_map/ppermute | solution.py:322
  28.9 7.9 %collective-permute-start.7 = (bf16[4,64,384]{2,1,0:T(8,128)(2,1)S(1)}, bf16[4,64,384]{2,1,0:T(8,128)(2,1)S(1)}, u32[]{:S(2)}, u32[]{:S(2)}) collective-permute-start(bf16[4,64,384]{2,1,0:T(8,128)(2,1)S(1)} %get-tuple-element.29), channel_id=1, source_target_pairs={{0,5},{1,4},{4,1},{5,0},{8,13},{9,12},{12,9},{13,8},{2,7},{3,6},{6... | collective-permute-start | bytes 589832 | tf_op jit(solution)/shard_map/ppermute | solution.py:322
  30.4 6.4 %collective-permute-start.8 = (bf16[1,8,2,16,384]{4,3,2,1,0:T(8,128)(2,1)S(1)}, bf16[1,8,2,16,384]{4,3,2,1,0:T(8,128)(2,1)S(1)}, u32[]{:S(2)}, u32[]{:S(2)}) collective-permute-start(bf16[1,8,2,16,384]{4,3,2,1,0:T(8,128)(2,1)S(1)} %bitcast.9), channel_id=1, source_target_pairs={{0,2},{2,0},{1,3},{3,1},{4,6},{6,4},{5,7},{7,5},{8,10},{10,8},{9,1... | collective-permute-start | bytes 589832 | tf_op jit(solution)/shard_map/ppermute | solution.py:329
  30.4 6.4 %collective-permute-start.9 = (bf16[1,8,2,16,384]{4,3,2,1,0:T(8,128)(2,1)S(1)}, bf16[1,8,2,16,384]{4,3,2,1,0:T(8,128)(2,1)S(1)}, u32[]{:S(2)}, u32[]{:S(2)}) collective-permute-start(bf16[1,8,2,16,384]{4,3,2,1,0:T(8,128)(2,1)S(1)} %bitcast.12), channel_id=1, source_target_pairs={{0,2},{2,0},{1,3},{3,1},{4,6},{6,4},{5,7},{7,5},{8,10},{10,8},{9,1... | collective-permute-start | bytes 589832 | tf_op jit(solution)/shard_map/ppermute | solution.py:329
  38.3 1.9 %collective-permute-start.10 = (bf16[8,32,896]{2,1,0:T(8,128)(2,1)S(1)}, bf16[8,32,896]{2,1,0:T(8,128)(2,1)S(1)}, u32[]{:S(2)}, u32[]{:S(2)}) collective-permute-start(bf16[8,32,896]{2,1,0:T(8,128)(2,1)S(1)} %bitcast.11), channel_id=1, source_target_pairs={{0,2},{2,0},{1,3},{3,1},{4,6},{6,4},{5,7},{7,5},{8,10},{10,8},{9,1... | collective-permute-start | bytes 1376264 | tf_op jit(solution)/shard_map/ppermute | solution.py:337
  41.6 6.5 %collective-permute-start.11 = (bf16[32,896]{1,0:T(8,128)(2,1)S(1)}, bf16[32,896]{1,0:T(8,128)(2,1)S(1)}, u32[]{:S(2)}, u32[]{:S(2)}) collective-permute-start(bf16[32,896]{1,0:T(8,128)(2,1)S(1)} %get-tuple-element.31), channel_id=1, source_target_pairs={{0,4},{4,0},{8,12},{12,8},{16,20},{20,16},{24,28},{28,24},{1,5},{5... | collective-permute-start | bytes 172040 | tf_op jit(solution)/shard_map/ppermute | solution.py:340
  42.2 8.8 %collective-permute-start.12 = (bf16[32,896]{1,0:T(8,128)(2,1)S(1)}, bf16[32,896]{1,0:T(8,128)(2,1)S(1)}, u32[]{:S(2)}, u32[]{:S(2)}) collective-permute-start(bf16[32,896]{1,0:T(8,128)(2,1)S(1)} %get-tuple-element.32), channel_id=1, source_target_pairs={{0,8},{4,12},{8,0},{12,4},{16,24},{20,28},{24,16},{28,20},{1,9},{5... | collective-permute-start | bytes 172040 | tf_op jit(solution)/shard_map/ppermute | solution.py:340
  42.5 10.3 %collective-permute-start.13 = (bf16[32,896]{1,0:T(8,128)(2,1)S(1)}, bf16[32,896]{1,0:T(8,128)(2,1)S(1)}, u32[]{:S(2)}, u32[]{:S(2)}) collective-permute-start(bf16[32,896]{1,0:T(8,128)(2,1)S(1)} %get-tuple-element.33), channel_id=1, source_target_pairs={{0,12},{4,8},{8,4},{12,0},{16,28},{20,24},{24,20},{28,16},{1,13},{... | collective-permute-start | bytes 172040 | tf_op jit(solution)/shard_map/ppermute | solution.py:340
  45.2 8.1 %collective-permute-start.14 = (bf16[32,896]{1,0:T(8,128)(2,1)S(1)}, bf16[32,896]{1,0:T(8,128)(2,1)S(1)}, u32[]{:S(2)}, u32[]{:S(2)}) collective-permute-start(bf16[32,896]{1,0:T(8,128)(2,1)S(1)} %get-tuple-element.34), channel_id=1, source_target_pairs={{0,16},{4,20},{8,24},{12,28},{16,0},{20,4},{24,8},{28,12},{1,17},{... | collective-permute-start | bytes 172040 | tf_op jit(solution)/shard_map/ppermute | solution.py:340
  46.3 8.1 %collective-permute-start.15 = (bf16[32,896]{1,0:T(8,128)(2,1)S(1)}, bf16[32,896]{1,0:T(8,128)(2,1)S(1)}, u32[]{:S(2)}, u32[]{:S(2)}) collective-permute-start(bf16[32,896]{1,0:T(8,128)(2,1)S(1)} %get-tuple-element.35), channel_id=1, source_target_pairs={{0,20},{4,16},{8,28},{12,24},{16,4},{20,0},{24,12},{28,8},{1,21},{... | collective-permute-start | bytes 172040 | tf_op jit(solution)/shard_map/ppermute | solution.py:340
  48.1 6.3 %collective-permute-start.16 = (bf16[32,896]{1,0:T(8,128)(2,1)S(1)}, bf16[32,896]{1,0:T(8,128)(2,1)S(1)}, u32[]{:S(2)}, u32[]{:S(2)}) collective-permute-start(bf16[32,896]{1,0:T(8,128)(2,1)S(1)} %get-tuple-element.36), channel_id=1, source_target_pairs={{0,24},{4,28},{8,16},{12,20},{16,8},{20,12},{24,0},{28,4},{1,25},{... | collective-permute-start | bytes 172040 | tf_op jit(solution)/shard_map/ppermute | solution.py:340
  51.1 7.0 %collective-permute-start.17 = (bf16[32,896]{1,0:T(8,128)(2,1)S(1)}, bf16[32,896]{1,0:T(8,128)(2,1)S(1)}, u32[]{:S(2)}, u32[]{:S(2)}) collective-permute-start(bf16[32,896]{1,0:T(8,128)(2,1)S(1)} %get-tuple-element.37), channel_id=1, source_target_pairs={{0,28},{4,24},{8,20},{12,16},{16,12},{20,8},{24,4},{28,0},{1,29},{... | collective-permute-start | bytes 172040 | tf_op jit(solution)/shard_map/ppermute | solution.py:340
  62.3 7.2 %collective-permute-start.18 = (bf16[64,2560]{1,0:T(8,128)(2,1)S(1)}, bf16[64,2560]{1,0:T(8,128)(2,1)S(1)}, u32[]{:S(2)}, u32[]{:S(2)}) collective-permute-start(bf16[64,2560]{1,0:T(8,128)(2,1)S(1)} %get-tuple-element.39), channel_id=1, source_target_pairs={{0,1},{1,0},{2,3},{3,2},{4,5},{5,4},{6,7},{7,6},{8,9},{9,8},{10,11... | collective-permute-start | bytes 983048 | tf_op jit(solution)/shard_map/ppermute | solution.py:352

commit v5 on v4

--- a/solution.py
+++ b/solution.py
@@ -11,9 +11,17 @@
 H = 24
 DH = 128
 NT = (((1,), (1,)), ((), ()))
+PART_TURNS = (4, 6, 5, 7, 1, 2, 3, 0)
+HOLD = 4
 TURNS = (0, 6, 1, 5, 2, 7, 4, 3)
-ATTEND_VMEM = 24 * 2**20
+ATTEND_VMEM = 16 * 2**20
 PROJECT_VMEM = 20 * 2**20
+
+
+def position(device_ref, g_count, head_axis):
+    device = device_ref[0]
+    pair = 2 * head_axis
+    return device // (pair * g_count), device // pair % g_count, device % head_axis
 
 
 def split_bf16(x, parts):
@@ -25,7 +33,7 @@
     return terms
 
 
-def attend_kernel(heads, row_len, group, plane_ref, *refs):
+def attend_kernel(heads, row_len, group, device_ref, after_ref, *refs):
     query_refs, kv_refs, out_ref = refs[: -group - 1], refs[-group - 1 : -1], refs[-1]
     plane_rows = group * row_len
     g_count, head_axis = out_ref.shape[1], out_ref.shape[2] // row_len
@@ -89,7 +97,8 @@
         put(packed_stats(lse, slopes_mean, heads), slice(2 * heads * DH, (2 * heads + 1) * DH))
 
     if len(query_refs) > 1:
-        planes = [plane_ref[0] ^ d for d in range(len(query_refs))]
+        k, _, _ = position(device_ref, g_count, head_axis)
+        planes = [k ^ d for d in range(len(query_refs))]
         some_planes([(ref, 0) for ref in query_refs], planes)
     else:
         (ref,) = query_refs
@@ -101,7 +110,7 @@
             some_planes([(ref, j) for j in planes], planes)
 
 
-def attend(queries, kv, plane, k, g_count, head_axis):
+def attend(queries, kv, device, k, g_count, head_axis, after):
     heads = kv[0].shape[2] // DH
     row_len = queries[0].shape[3]
     out_shape = (k, g_count, head_axis * row_len, heads * 2 * DH + DH)
@@ -109,11 +118,12 @@
     return pl.pallas_call(
         functools.partial(attend_kernel, heads, row_len, len(kv)),
         out_shape=jax.ShapeDtypeStruct(out_shape, jnp.bfloat16),
-        in_specs=[pl.BlockSpec(memory_space=pltpu.SMEM)] + [whole] * (len(queries) + len(kv)),
+        in_specs=[pl.BlockSpec(memory_space=pltpu.SMEM), pl.BlockSpec(memory_space=pl.ANY)]
+        + [whole] * (len(queries) + len(kv)),
         out_specs=whole,
         compiler_params=pltpu.CompilerParams(vmem_limit_bytes=ATTEND_VMEM),
         name="attend",
-    )(plane, *queries, *kv)
+    )(device, after, *queries, *kv)
 
 
 def packed_stats(lse, slope, heads):
@@ -155,12 +165,12 @@
     return value, tangent
 
 
-def merge(place_ref, parts_refs, both_ref, heads, g_count):
+def merge(my_g, parts_refs, both_ref, heads, g_count, turns):
     rows = parts_refs[0].shape[0]
     tail = slice(2 * heads * DH, (2 * heads + 1) * DH)
     for d in range(g_count):
-        g = (place_ref[0] ^ d) % g_count
-        parts = [ref[...] for ref in parts_refs[d::g_count]]
+        g = my_g ^ d
+        parts = [parts_refs[turns.index(j)][...] for j in range(d, len(turns), g_count)]
         share, shift, _, _ = merge_stats([part[:, tail] for part in parts], heads)
         for h in range(heads):
             value, tangent = merge_head(parts, share, shift, h)
@@ -169,10 +179,11 @@
             both_ref[rows:, columns] = tangent.astype(jnp.bfloat16)
 
 
-def pair_kernel(heads, place_ref, home_ref, away_ref, *out_refs):
+def pair_kernel(heads, turns, g_count, head_axis, device_ref, home_ref, away_ref, *out_refs):
+    k, g, _ = position(device_ref, g_count, head_axis)
     tail = slice(2 * heads * DH, (2 * heads + 1) * DH)
-    for d, out_ref in enumerate(out_refs):
-        parts = [ref[place_ref[0] ^ d] for ref in (home_ref, away_ref)]
+    for d, out_ref in zip(turns, out_refs):
+        parts = [ref[(k * g_count + g) ^ d] for ref in (home_ref, away_ref)]
         share, shift, lse, slope = merge_stats([part[:, tail] for part in parts], heads)
         for h in range(heads):
             both = jnp.concatenate(merge_head(parts, share, shift, h), axis=1)
@@ -180,35 +191,51 @@
         out_ref[:, tail] = packed_stats(lse, slope, heads)
 
 
-def merge_pair(place, home, away, heads):
+def merge_pair(device, home, away, heads, turns, g_count, head_axis):
     whole = pl.BlockSpec(memory_space=pltpu.VMEM)
     count = home.shape[0]
     return pl.pallas_call(
-        functools.partial(pair_kernel, heads),
+        functools.partial(pair_kernel, heads, turns, g_count, head_axis),
         out_shape=[jax.ShapeDtypeStruct(home.shape[1:], home.dtype)] * count,
         in_specs=[pl.BlockSpec(memory_space=pltpu.SMEM), whole, whole],
         out_specs=[whole] * count,
         compiler_params=pltpu.CompilerParams(vmem_limit_bytes=ATTEND_VMEM),
         name="merge_pair",
-    )(place, home, away)
-
-
-def first_kernel(heads, g_count, half_ref, place_ref, weight_ref, *refs):
-    *parts_refs, out_ref, both_ref, held, sems = refs
-    copies = fetch(half_ref, weight_ref, held, sems)
-    merge(place_ref, parts_refs, both_ref, heads, g_count)
-    times_held(copies, both_ref, out_ref, held)
-
-
-def second_kernel(half_ref, place_ref, weight_ref, both_ref, out_ref, held, sems):
-    times_held(fetch(half_ref, weight_ref, held, sems), both_ref, out_ref, held)
-
-
-def fetch(half_ref, weight_ref, held, sems):
+    )(device, home, away)
+
+
+def first_kernel(heads, g_count, head_axis, turns, held_count, device_ref, weight_ref, *refs):
+    _, my_g, _ = position(device_ref, g_count, head_axis)
+    if held_count:
+        *refs, out_ref, both_ref = refs
+        parts_refs, held_refs = refs[:-held_count], refs[-held_count:]
+        merge(my_g, parts_refs, both_ref, heads, g_count, turns)
+        for i, held in enumerate(held_refs):
+            times(both_ref, held[...], out_ref, i)
+    else:
+        *parts_refs, out_ref, both_ref, held, sems = refs
+        copies = fetch(0, weight_ref, held, sems)
+        merge(my_g, parts_refs, both_ref, heads, g_count, turns)
+        times_held(copies, both_ref, out_ref, held)
+
+
+def times(both_ref, columns, out_ref, i):
+    tile = columns.shape[1]
+    out_ref[:, i * tile : (i + 1) * tile] = jnp.dot(
+        both_ref[...], columns, preferred_element_type=jnp.float32
+    ).astype(out_ref.dtype)
+
+
+def second_kernel(head_axis, device_ref, weight_ref, both_ref, out_ref, held, sems):
+    _, _, head = position(device_ref, 1, head_axis)
+    times_held(fetch(head, weight_ref, held, sems), both_ref, out_ref, held)
+
+
+def fetch(half, weight_ref, held, sems):
     chunks, _, tile = held.shape
     copies = []
     for i in range(chunks):
-        first = pl.multiple_of((half_ref[0] * chunks + i) * tile, tile)
+        first = pl.multiple_of((half * chunks + i) * tile, tile)
         copy = pltpu.make_async_copy(weight_ref.at[:, pl.ds(first, tile)], held.at[i], sems.at[i])
         copy.start()
         copies.append(copy)
@@ -216,15 +243,12 @@
 
 
 def times_held(copies, both_ref, out_ref, held):
-    tile = held.shape[2]
     for i, copy in enumerate(copies):
         copy.wait()
-        out_ref[:, i * tile : (i + 1) * tile] = jnp.dot(
-            both_ref[...], held[i], preferred_element_type=jnp.float32
-        ).astype(out_ref.dtype)
-
-
-def project(kernel, half, place, left, weight, width, dtype, merged=None):
+        times(both_ref, held[i], out_ref, i)
+
+
+def project(kernel, device, left, weight, width, dtype, merged=None, held=()):
     depth = weight.shape[0]
     chunks = 4
     rows = merged[0] if merged else left[0].shape[0]
@@ -233,27 +257,31 @@
         outs.append(jax.ShapeDtypeStruct(merged, jnp.bfloat16))
     whole = pl.BlockSpec(memory_space=pltpu.VMEM)
     scalar = pl.BlockSpec(memory_space=pltpu.SMEM)
+    scratch = [
+        pltpu.VMEM((chunks, depth, width // chunks), jnp.bfloat16),
+        pltpu.SemaphoreType.DMA((chunks,)),
+    ]
+    if held:
+        scratch = []
     return pl.pallas_call(
         kernel,
         out_shape=outs,
-        in_specs=[scalar, scalar, pl.BlockSpec(memory_space=pl.ANY)] + [whole] * len(left),
+        in_specs=[scalar, pl.BlockSpec(memory_space=pl.ANY)] + [whole] * (len(left) + len(held)),
         out_specs=[whole] * len(outs),
-        scratch_shapes=[
-            pltpu.VMEM((chunks, depth, width // chunks), jnp.bfloat16),
-            pltpu.SemaphoreType.DMA((chunks,)),
-        ],
+        scratch_shapes=scratch,
         compiler_params=pltpu.CompilerParams(vmem_limit_bytes=PROJECT_VMEM),
         cost_estimate=pl.CostEstimate(
             flops=2 * rows * depth * width, bytes_accessed=2 * depth * width, transcendentals=0
         ),
         name="project",
-    )(half, place, pltpu.with_memory_space_constraint(weight, pltpu.HBM), *left)
-
-
-def pack_kernel(turns, g_count, head_axis, place_ref, *refs):
+    )(device, pltpu.with_memory_space_constraint(weight, pltpu.HBM), *left, *held)
+
+
+def pack_kernel(turns, g_count, head_axis, device_ref, *refs):
     group = len(turns)
     matrix_refs, query_ref, piece_refs, sems = refs[:6], refs[6], refs[7:-1], refs[-1]
     width = query_ref.shape[3]
+    _, my_g, head = position(device_ref, g_count, head_axis)
     copies = []
 
     def copy(ref, first, to, *sem):
@@ -264,7 +292,7 @@
         for t in range(2):
             copy(matrix_refs[t], i, query_ref.at[i, t], i, t)
     for i, turn in enumerate(turns):
-        partner = place_ref[0] ^ turn
+        partner = (my_g * head_axis + head) ^ turn
         column = (partner % head_axis) * g_count + partner // head_axis
         for t in range(4):
             copy(matrix_refs[2 + t], column, piece_refs[i].at[t], i, 2 + t)
@@ -274,7 +302,7 @@
         each.wait()
 
 
-def pack(turns, g_count, head_axis, place, *matrices):
+def pack(turns, g_count, head_axis, device, *matrices):
     group = len(turns)
     rows, columns = matrices[0].shape
     width = columns // group
@@ -289,7 +317,42 @@
         scratch_shapes=[pltpu.SemaphoreType.DMA((group, len(matrices)))],
         compiler_params=pltpu.CompilerParams(vmem_limit_bytes=8 * 2**20),
         name="pack",
-    )(place, *(pltpu.with_memory_space_constraint(m, pltpu.HBM) for m in matrices))
+    )(device, *(pltpu.with_memory_space_constraint(m, pltpu.HBM) for m in matrices))
+
+
+def hold_kernel(head_axis, device_ref, weight_ref, after_ref, out_ref, sems):
+    count = sems.shape[0]
+    rows, width = out_ref.shape[0] // count, out_ref.shape[1]
+    _, _, head = position(device_ref, 1, head_axis)
+    columns = pl.ds(pl.multiple_of((1 - head) * width, width), width)
+    copies = [
+        pltpu.make_async_copy(
+            weight_ref.at[pl.ds(i * rows, rows), columns],
+            out_ref.at[pl.ds(i * rows, rows)],
+            sems.at[i],
+        )
+        for i in range(count)
+    ]
+    for copy in copies:
+        copy.start()
+    for copy in copies:
+        copy.wait()
+
+
+def hold(device, weight, head_axis, after):
+    anywhere = pl.BlockSpec(memory_space=pl.ANY)
+    width = weight.shape[1] // head_axis
+    size = weight.shape[0] * width
+    return pl.pallas_call(
+        functools.partial(hold_kernel, head_axis),
+        out_shape=jax.ShapeDtypeStruct((weight.shape[0], width), weight.dtype),
+        in_specs=[pl.BlockSpec(memory_space=pltpu.SMEM), anywhere, anywhere],
+        out_specs=pl.BlockSpec(memory_space=pltpu.VMEM),
+        scratch_shapes=[pltpu.SemaphoreType.DMA((8,))],
+        compiler_params=pltpu.CompilerParams(vmem_limit_bytes=12 * 2**20),
+        cost_estimate=pl.CostEstimate(flops=0, bytes_accessed=2 * size, transcendentals=0),
+        name="hold",
+    )(device, pltpu.with_memory_space_constraint(weight, pltpu.HBM), after)
 
 
 def local(queries, query_tangent, key_rows, key_tangent, value_rows, value_tangent, out_weight):
@@ -304,12 +367,12 @@
         return lax.all_to_all(x, plane_axes, split_axis=0, concat_axis=0, tiled=True)
 
     turns = sorted(range(group), key=TURNS.index)
-    in_plane = lax.axis_index(("g", "head")).astype(jnp.int32).reshape(1)
+    device = lax.axis_index(("k", "g", "core", "head")).astype(jnp.int32).reshape(1)
     packed_queries, *kv = pack(
         turns,
         g_count,
         head_axis,
-        in_plane,
+        device,
         queries,
         query_tangent,
         key_rows,
@@ -328,33 +391,35 @@
         home_queries = [lax.all_gather(plane_queries, "k", axis=0, tiled=False)]
     away_queries = [lax.ppermute(q, "core", swap) for q in home_queries]
 
-    plane = lax.axis_index("k").astype(jnp.int32).reshape(1)
+    width = out_weight.shape[1] // head_axis
+    held = [hold(device, out_weight, head_axis, kv[HOLD])] if head_axis == 2 else []
     away, home = (
-        attend(some, kv, plane, k, g_count, head_axis).reshape(k * g_count, rows, -1)
+        attend(some, kv, device, k, g_count, head_axis, (held + kv)[0])
         for some in (away_queries, home_queries)
     )
-    place = lax.axis_index(("k", "g")).astype(jnp.int32).reshape(1)
-    parts = merge_pair(place, home, lax.ppermute(away, "core", swap), heads)
+    away, home = (some.reshape(k * g_count, rows, -1) for some in (away, home))
     count = k * g_count
+    part_turns = PART_TURNS if count == len(PART_TURNS) else tuple(range(count))
+    arrived = lax.ppermute(away, "core", swap)
+    parts = merge_pair(device, home, arrived, heads, part_turns, g_count, head_axis)
     parts = [
         lax.ppermute(part, ("k", "g"), [(i, i ^ d) for i in range(count)]) if d else part
-        for d, part in enumerate(parts)
+        for d, part in zip(part_turns, parts)
     ]
 
-    width = out_weight.shape[1] // head_axis
-    mine = lax.axis_index("head").astype(jnp.int32).reshape(1)
     merged = (2 * rows, out_weight.shape[0])
-    merging = functools.partial(first_kernel, heads, g_count)
+    merging = functools.partial(first_kernel, heads, g_count, head_axis, part_turns, len(held))
     if head_axis == 2:
         sent, both = project(
-            merging, 1 - mine, place, parts, out_weight, width, jnp.bfloat16, merged
+            merging, device, parts, out_weight, width, jnp.bfloat16, merged, held
         )
         received = lax.ppermute(sent, "head", swap)
-        (own,) = project(second_kernel, mine, place, [both], out_weight, width, jnp.float32)
+        own_half = functools.partial(second_kernel, head_axis)
+        (own,) = project(own_half, device, [both], out_weight, width, jnp.float32)
         total = own + received.astype(jnp.float32)
     else:
         partial, _ = project(
-            merging, 0 * mine, place, parts, out_weight, width * head_axis, jnp.float32, merged
+            merging, device, parts, out_weight, width * head_axis, jnp.float32, merged
         )
         total = lax.psum_scatter(partial, "head", scatter_dimension=1, tiled=True)
     total = total.astype(jnp.bfloat16)

time: 70.6 us -> 68 us (0.963)
  waiting for transfers between devices: 23.1 us -> 20.5 us
  Pallas kernels: 15.1 us -> 16.1 us
  starting transfers between devices: 30.5 us -> 29.6 us
    ppermute x7, waiting for transfers between devices: 11.8 us -> 8.5 us  [local(): lax.ppermute(piece, ('g', 'head'), [(i, i ^ d) for i in range(group)])]
    ppermute x7, starting transfers between devices: 11.2 us -> 9.78 us  [local(): lax.ppermute(part, ('k', 'g'), [(i, i ^ d) for i in range(count)])]
    ppermute x1, waiting for transfers between devices: 2.74 us -> 4.03 us  [local(): received = lax.ppermute(sent, 'head', swap)]
    pallas_call x3 -> x4, Pallas kernels: 9.54 us -> 10.5 us  [the longest x2 5.73 us: project(): pl.pallas_call(kernel, out_shape=outs, in_specs=[scalar, pl.BlockSpec(mem...]
  transfers between devices with their start and end apart: 20 -> 20, of which waited for: 11 -> 14; matrix products, arithmetic and copies ran while one was open for 0% -> 0% of each run, Pallas kernels for 8% -> 13%
where the time goes in v5:
time: 68 us; the launch traced here: 67.7 us
  starting transfers between devices  29.6 us (44%)
  waiting for transfers between devices  20.5 us (30%)
  Pallas kernels  16.1 us (24%)
  local copies, waits for them, and re-layouts  0.74 us (1%)
  between operations  0.72 us (1%)
    ppermute x7, starting transfers between devices, local(): lax.ppermute(part, ('k', 'g'), [(i, i ^ d) for i in range(count)])  9.78 us
    ppermute x7, starting transfers between devices, local(): lax.ppermute(piece, ('g', 'head'), [(i, i ^ d) for i in range(group)])  9.6 us
    ppermute x7, waiting for transfers between devices, local(): lax.ppermute(piece, ('g', 'head'), [(i, i ^ d) for i in range(group)])  8.5 us
    all_to_all x1, starting transfers between devices, within_plane(): lax.all_to_all(x, plane_axes, split_axis=0, concat_axis=0, tiled=True)  6.2 us
    pallas_call x2, Pallas kernels, project(): pl.pallas_call(kernel, out_shape=outs, in_specs=[scalar, pl.BlockSpec(mem...  5.73 us
    ppermute x7, waiting for transfers between devices, local(): lax.ppermute(part, ('k', 'g'), [(i, i ^ d) for i in range(count)])  4.67 us
    ppermute x1, waiting for transfers between devices, local(): received = lax.ppermute(sent, 'head', swap)  4.03 us
    pallas_call x1, Pallas kernels, hold(): pl.pallas_call(functools.partial(hold_kernel, head_axis), out_shape=jax.S...  3.32 us
  transfers between devices with their start and end apart: 20, of which 14 were waited for; matrix products, arithmetic and copies ran while one was open for 0% of the time, Pallas kernels for 13%

profile of v5, /device:TPU:0, one launch (start us, length us, event | category | flops | bytes accessed | tf_op | source)
XLA Modules:
  0.0 67.7 jit_solution(5402995630884940903)
XLA Ops:
  0.6 2.6 %pack.1 = (bf16[8,2,16,384]{3,2,1,0:T(8,128)(2,1)}, bf16[4,64,384]{2,1,0:T(8,128)(2,1)S(1)}, bf16[4,64,384]{2,1,0:T(8,128)(2,1)S(1)}, bf16[4,64,384]{2,1,0:T(8,1...) custom-call(s32[1]{0:T(128)} %bitcast.device_ref, ...), custom_call_target="tpu_custom_call" | custom-call | tf_op jit(solution)/shard_map/pack/pallas_call | solution.py:311
  3.3 6.2 %all-to-all-start = ((bf16[8,2,16,384]{3,2,1,0:T(8,128)(2,1)}), bf16[8,2,16,384]{3,2,1,0:T(8,128)(2,1)S(1)}, u32[]{:S(2)}, u32[]{:S(2)}) async-start(bf16[8,2,16,384]{3,2,1,0:T(8,128)(2,1)} %get-tuple-element.22), calls=%async_computation | async-start | bytes 393216 | tf_op jit(solution)/shard_map/all_to_all | solution.py:367
  9.5 2.0 %collective-permute-start = (bf16[4,64,384]{2,1,0:T(8,128)(2,1)S(1)}, bf16[4,64,384]{2,1,0:T(8,128)(2,1)S(1)}, u32[]{:S(2)}, u32[]{:S(2)}) collective-permute-start(bf16[4,64,384]{2,1,0:T(8,128)(2,1)S(1)} %get-tuple-element.21), channel_id=1, source_target_pairs={{0,4},{1,5},{4,0},{5,1},{8,12},{9,13},{12,8},{13,9},{2,6},{3,7},{6... | collective-permute-start | bytes 589832 | tf_op jit(solution)/shard_map/ppermute | solution.py:385
  11.5 1.5 %collective-permute-start.2 = (bf16[4,64,384]{2,1,0:T(8,128)(2,1)S(1)}, bf16[4,64,384]{2,1,0:T(8,128)(2,1)S(1)}, u32[]{:S(2)}, u32[]{:S(2)}) collective-permute-start(bf16[4,64,384]{2,1,0:T(8,128)(2,1)S(1)} %get-tuple-element.24), channel_id=1, source_target_pairs={{0,12},{1,13},{4,8},{5,9},{8,4},{9,5},{12,0},{13,1},{2,14},{3,15},... | collective-permute-start | bytes 589832 | tf_op jit(solution)/shard_map/ppermute | solution.py:385
  13.0 1.5 %collective-permute-start.3 = (bf16[4,64,384]{2,1,0:T(8,128)(2,1)S(1)}, bf16[4,64,384]{2,1,0:T(8,128)(2,1)S(1)}, u32[]{:S(2)}, u32[]{:S(2)}) collective-permute-start(bf16[4,64,384]{2,1,0:T(8,128)(2,1)S(1)} %get-tuple-element.25), channel_id=1, source_target_pairs={{0,1},{1,0},{4,5},{5,4},{8,9},{9,8},{12,13},{13,12},{2,3},{3,2},{6... | collective-permute-start | bytes 589832 | tf_op jit(solution)/shard_map/ppermute | solution.py:385
  14.4 3.0 %all-to-all-done = bf16[8,2,16,384]{3,2,1,0:T(8,128)(2,1)S(1)} async-done(((bf16[8,2,16,384]{3,2,1,0:T(8,128)(2,1)}), bf16[8,2,16,384]{3,2,1,0:T(8,128)(2,1)S(1)}, u32[]{:S(2)}, u32[]{:S(2)}) %all-to-all-start) | async-done | bytes 196640 | tf_op jit(solution)/shard_map/all_to_all | solution.py:367
  17.4 2.6 %collective-permute-start.1 = (bf16[8,2,16,384]{3,2,1,0:T(8,128)(2,1)S(1)}, bf16[8,2,16,384]{3,2,1,0:T(8,128)(2,1)S(1)}, u32[]{:S(2)}, u32[]{:S(2)}) collective-permute-start(bf16[8,2,16,384]{3,2,1,0:T(8,128)(2,1)S(1)} %all-to-all-done), channel_id=1, source_target_pairs={{0,16},{16,0},{1,17},{17,1},{2,18},{18,2},{3,19},{19,3},{4,20},{20... | collective-permute-start | bytes 589832 | tf_op jit(solution)/shard_map/ppermute | solution.py:389
  20.0 1.4 %collective-permute-done.after_ref.refs_6_ = bf16[4,64,384]{2,1,0:T(8,128)(2,1)S(1)} collective-permute-done((bf16[4,64,384]{2,1,0:T(8,128)(2,1)S(1)}, bf16[4,64,384]{2,1,0:T(8,128)(2,1)S(1)}, u32[]{:S(2)}, u32[]{:S(2)}) %collective-permute-start) | collective-permute-done | bytes 196640 | tf_op jit(solution)/shard_map/ppermute | solution.py:385
  21.4 3.1 %collective-permute-start.5 = (bf16[4,64,384]{2,1,0:T(8,128)(2,1)S(1)}, bf16[4,64,384]{2,1,0:T(8,128)(2,1)S(1)}, u32[]{:S(2)}, u32[]{:S(2)}) collective-permute-start(bf16[4,64,384]{2,1,0:T(8,128)(2,1)S(1)} %get-tuple-element.27), channel_id=1, source_target_pairs={{0,13},{1,12},{4,9},{5,8},{8,5},{9,4},{12,1},{13,0},{2,15},{3,14},... | collective-permute-start | bytes 589832 | tf_op jit(solution)/shard_map/ppermute | solution.py:385
  26.3 2.7 %collective-permute-done.4.refs_5_ = bf16[4,64,384]{2,1,0:T(8,128)(2,1)S(1)} collective-permute-done((bf16[4,64,384]{2,1,0:T(8,128)(2,1)S(1)}, bf16[4,64,384]{2,1,0:T(8,128)(2,1)S(1)}, u32[]{:S(2)}, u32[]{:S(2)}) %collective-permute-start.4) | collective-permute-done | bytes 196640 | tf_op jit(solution)/shard_map/ppermute | solution.py:385
  29.5 3.3 %hold.1.after_ref.refs_8_ = bf16[1536,2560]{1,0:T(8,128)(2,1)S(1)} custom-call(s32[1]{0:T(128)} %bitcast.device_ref, bf16[1536,5120]{1,0:T(8,128)(2,1)} %weight_ref.5, bf16[4,64,384]{2,1,0:T(8,128)(2,1)S(1)} %collective-permute-done.after_ref.refs_6_), custom_call_target="tpu_custom_call" | custom-call | bytes 7864320 | tf_op jit(solution)/shard_map/hold/pallas_call | solution.py:346
  35.0 2.0 %collective-permute-done.7.refs_9_ = bf16[4,64,384]{2,1,0:T(8,128)(2,1)S(1)} collective-permute-done((bf16[4,64,384]{2,1,0:T(8,128)(2,1)S(1)}, bf16[4,64,384]{2,1,0:T(8,128)(2,1)S(1)}, u32[]{:S(2)}, u32[]{:S(2)}) %collective-permute-start.7) | collective-permute-done | bytes 196640 | tf_op jit(solution)/shard_map/ppermute | solution.py:385
  37.0 1.5 %attend.3 = bf16[2,4,32,896]{3,2,1,0:T(8,128)(2,1)S(1)} custom-call(s32[1]{0:T(128)} %bitcast.device_ref, bf16[1536,2560]{1,0:T(8,128)(2,1)S(1)} %hold.1.after_ref.refs_8_, bf16[1,8,2,16,384]{4,3,2,1,0:T(8,128)(2,1)S(1)} %collective-permute-done.8.refs_0_, bf16[1,8,2,16,384]{4,3,2,1,0:T(8,128)(2,1)S(1)} %collective-permute-done.9.refs_1_, ...), custom_call_target="tpu_custom_call" | custom-call | tf_op jit(solution)/shard_map/attend/pallas_call | solution.py:118
  38.6 1.5 %attend.2 = bf16[2,4,32,896]{3,2,1,0:T(8,128)(2,1)S(1)} custom-call(s32[1]{0:T(128)} %bitcast.device_ref, bf16[1536,2560]{1,0:T(8,128)(2,1)S(1)} %hold.1.after_ref.refs_8_, bf16[1,8,2,16,384]{4,3,2,1,0:T(8,128)(2,1)S(1)} %bitcast.7, bf16[1,8,2,16,384]{4,3,2,1,0:T(8,128)(2,1)S(1)} %bitcast.10, bf16[4,64,384]{2,1,0:T(8,128)(2,1)S(1)} %get-tuple-element.23.refs_2_, ...), custom_call_target="tpu_custom_call" | custom-call | tf_op jit(solution)/shard_map/attend/pallas_call | solution.py:118
  40.4 1.4 %merge_pair.1 = (bf16[32,896]{1,0:T(8,128)(2,1)S(1)}, bf16[32,896]{1,0:T(8,128)(2,1)S(1)}, bf16[32,896]{1,0:T(8,128)(2,1)S(1)}, bf16[32,896]{1,0:T(8,128)(2,1)S(...) custom-call(s32[1]{0:T(128)} %bitcast.device_ref, ...), custom_call_target="tpu_custom_call" | custom-call | tf_op jit(solution)/shard_map/merge_pair/pallas_call | solution.py:197
  41.8 1.9 %collective-permute-start.11 = (bf16[32,896]{1,0:T(8,128)(2,1)S(1)}, bf16[32,896]{1,0:T(8,128)(2,1)S(1)}, u32[]{:S(2)}, u32[]{:S(2)}) collective-permute-start(bf16[32,896]{1,0:T(8,128)(2,1)S(1)} %get-tuple-element.30), channel_id=1, source_target_pairs={{0,16},{4,20},{8,24},{12,28},{16,0},{20,4},{24,8},{28,12},{1,17},{... | collective-permute-start | bytes 172040 | tf_op jit(solution)/shard_map/ppermute | solution.py:406
  44.7 1.6 %collective-permute-start.13 = (bf16[32,896]{1,0:T(8,128)(2,1)S(1)}, bf16[32,896]{1,0:T(8,128)(2,1)S(1)}, u32[]{:S(2)}, u32[]{:S(2)}) collective-permute-start(bf16[32,896]{1,0:T(8,128)(2,1)S(1)} %get-tuple-element.32), channel_id=1, source_target_pairs={{0,20},{4,16},{8,28},{12,24},{16,4},{20,0},{24,12},{28,8},{1,21},{... | collective-permute-start | bytes 172040 | tf_op jit(solution)/shard_map/ppermute | solution.py:406
  46.3 2.3 %collective-permute-start.14 = (bf16[32,896]{1,0:T(8,128)(2,1)S(1)}, bf16[32,896]{1,0:T(8,128)(2,1)S(1)}, u32[]{:S(2)}, u32[]{:S(2)}) collective-permute-start(bf16[32,896]{1,0:T(8,128)(2,1)S(1)} %get-tuple-element.33), channel_id=1, source_target_pairs={{0,28},{4,24},{8,20},{12,16},{16,12},{20,8},{24,4},{28,0},{1,29},{... | collective-permute-start | bytes 172040 | tf_op jit(solution)/shard_map/ppermute | solution.py:406
  49.2 1.5 %collective-permute-done.11.refs_0_ = bf16[32,896]{1,0:T(8,128)(2,1)S(1)} collective-permute-done((bf16[32,896]{1,0:T(8,128)(2,1)S(1)}, bf16[32,896]{1,0:T(8,128)(2,1)S(1)}, u32[]{:S(2)}, u32[]{:S(2)}) %collective-permute-start.11) | collective-permute-done | bytes 57376 | tf_op jit(solution)/shard_map/ppermute | solution.py:406
  51.2 1.9 %collective-permute-start.17 = (bf16[32,896]{1,0:T(8,128)(2,1)S(1)}, bf16[32,896]{1,0:T(8,128)(2,1)S(1)}, u32[]{:S(2)}, u32[]{:S(2)}) collective-permute-start(bf16[32,896]{1,0:T(8,128)(2,1)S(1)} %get-tuple-element.36), channel_id=1, source_target_pairs={{0,12},{4,8},{8,4},{12,0},{16,28},{20,24},{24,20},{28,16},{1,13},{... | collective-permute-start | bytes 172040 | tf_op jit(solution)/shard_map/ppermute | solution.py:406
  53.2 1.3 %collective-permute-done.13.refs_2_ = bf16[32,896]{1,0:T(8,128)(2,1)S(1)} collective-permute-done((bf16[32,896]{1,0:T(8,128)(2,1)S(1)}, bf16[32,896]{1,0:T(8,128)(2,1)S(1)}, u32[]{:S(2)}, u32[]{:S(2)}) %collective-permute-start.13) | collective-permute-done | bytes 57376 | tf_op jit(solution)/shard_map/ppermute | solution.py:406
  56.3 1.9 %project.2 = (bf16[64,2560]{1,0:T(8,128)(2,1)S(1)}, bf16[64,1536]{1,0:T(8,128)(2,1)S(1)}) custom-call(s32[1]{0:T(128)} %bitcast.device_ref, bf16[1536,5120]{1,0:T(8,128)(2,1)} %weight_ref.5, bf16[32,896]{1,0:T(8,128)(2,1)S(1)} %collective-permute-done.11.refs_0_, bf16[32,896]{1,0:T(8,128)(2,1)S(1)} %collective-permute-done.12.refs_1_, ...), custom_call_target="tpu_custom_call" | custom-call | flops 503316480 | bytes 7864320 | tf_op jit(solution)/shard_map/project/pallas_call | solution.py:266
  59.0 3.8 %project.3 = f32[64,2560]{1,0:T(8,128)S(1)} custom-call(s32[1]{0:T(128)} %bitcast.device_ref, bf16[1536,5120]{1,0:T(8,128)(2,1)} %weight_ref.5, bf16[64,1536]{1,0:T(8,128)(2,1)S(1)} %get-tuple-element.38.both_ref), custom_call_target="tpu_custom_call" | custom-call | flops 503316480 | bytes 7864320 | tf_op jit(solution)/shard_map/project/pallas_call | solution.py:266
  62.9 4.0 %collective-permute-done.18 = bf16[64,2560]{1,0:T(8,128)(2,1)S(1)} collective-permute-done((bf16[64,2560]{1,0:T(8,128)(2,1)S(1)}, bf16[64,2560]{1,0:T(8,128)(2,1)S(1)}, u32[]{:S(2)}, u32[]{:S(2)}) %collective-permute-start.18) | collective-permute-done | bytes 327712 | tf_op jit(solution)/shard_map/ppermute | solution.py:416
  (25 shorter events, 10.3 us)
Async XLA Ops:
  3.3 14.2 %all-to-all-start = ((bf16[8,2,16,384]{3,2,1,0:T(8,128)(2,1)}), bf16[8,2,16,384]{3,2,1,0:T(8,128)(2,1)S(1)}, u32[]{:S(2)}, u32[]{:S(2)}) async-start(bf16[8,2,16,384]{3,2,1,0:T(8,128)(2,1)} %get-tuple-element.22), calls=%async_computation | async-start | bytes 393216 | tf_op jit(solution)/shard_map/all_to_all | solution.py:367
  9.5 12.0 %collective-permute-start = (bf16[4,64,384]{2,1,0:T(8,128)(2,1)S(1)}, bf16[4,64,384]{2,1,0:T(8,128)(2,1)S(1)}, u32[]{:S(2)}, u32[]{:S(2)}) collective-permute-start(bf16[4,64,384]{2,1,0:T(8,128)(2,1)S(1)} %get-tuple-element.21), channel_id=1, source_target_pairs={{0,4},{1,5},{4,0},{5,1},{8,12},{9,13},{12,8},{13,9},{2,6},{3,7},{6... | collective-permute-start | bytes 589832 | tf_op jit(solution)/shard_map/ppermute | solution.py:385
  11.5 13.2 %collective-permute-start.2 = (bf16[4,64,384]{2,1,0:T(8,128)(2,1)S(1)}, bf16[4,64,384]{2,1,0:T(8,128)(2,1)S(1)}, u32[]{:S(2)}, u32[]{:S(2)}) collective-permute-start(bf16[4,64,384]{2,1,0:T(8,128)(2,1)S(1)} %get-tuple-element.24), channel_id=1, source_target_pairs={{0,12},{1,13},{4,8},{5,9},{8,4},{9,5},{12,0},{13,1},{2,14},{3,15},... | collective-permute-start | bytes 589832 | tf_op jit(solution)/shard_map/ppermute | solution.py:385
  13.0 12.7 %collective-permute-start.3 = (bf16[4,64,384]{2,1,0:T(8,128)(2,1)S(1)}, bf16[4,64,384]{2,1,0:T(8,128)(2,1)S(1)}, u32[]{:S(2)}, u32[]{:S(2)}) collective-permute-start(bf16[4,64,384]{2,1,0:T(8,128)(2,1)S(1)} %get-tuple-element.25), channel_id=1, source_target_pairs={{0,1},{1,0},{4,5},{5,4},{8,9},{9,8},{12,13},{13,12},{2,3},{3,2},{6... | collective-permute-start | bytes 589832 | tf_op jit(solution)/shard_map/ppermute | solution.py:385
  14.4 14.6 %collective-permute-start.4 = (bf16[4,64,384]{2,1,0:T(8,128)(2,1)S(1)}, bf16[4,64,384]{2,1,0:T(8,128)(2,1)S(1)}, u32[]{:S(2)}, u32[]{:S(2)}) collective-permute-start(bf16[4,64,384]{2,1,0:T(8,128)(2,1)S(1)} %get-tuple-element.26), channel_id=1, source_target_pairs={{0,9},{1,8},{4,13},{5,12},{8,1},{9,0},{12,5},{13,4},{2,11},{3,10},... | collective-permute-start | bytes 589832 | tf_op jit(solution)/shard_map/ppermute | solution.py:385
  17.4 11.5 %collective-permute-start.1 = (bf16[8,2,16,384]{3,2,1,0:T(8,128)(2,1)S(1)}, bf16[8,2,16,384]{3,2,1,0:T(8,128)(2,1)S(1)}, u32[]{:S(2)}, u32[]{:S(2)}) collective-permute-start(bf16[8,2,16,384]{3,2,1,0:T(8,128)(2,1)S(1)} %all-to-all-done), channel_id=1, source_target_pairs={{0,16},{16,0},{1,17},{17,1},{2,18},{18,2},{3,19},{19,3},{4,20},{20... | collective-permute-start | bytes 589832 | tf_op jit(solution)/shard_map/ppermute | solution.py:389
  21.4 12.6 %collective-permute-start.5 = (bf16[4,64,384]{2,1,0:T(8,128)(2,1)S(1)}, bf16[4,64,384]{2,1,0:T(8,128)(2,1)S(1)}, u32[]{:S(2)}, u32[]{:S(2)}) collective-permute-start(bf16[4,64,384]{2,1,0:T(8,128)(2,1)S(1)} %get-tuple-element.27), channel_id=1, source_target_pairs={{0,13},{1,12},{4,9},{5,8},{8,5},{9,4},{12,1},{13,0},{2,15},{3,14},... | collective-permute-start | bytes 589832 | tf_op jit(solution)/shard_map/ppermute | solution.py:385
  24.7 10.3 %collective-permute-start.6 = (bf16[4,64,384]{2,1,0:T(8,128)(2,1)S(1)}, bf16[4,64,384]{2,1,0:T(8,128)(2,1)S(1)}, u32[]{:S(2)}, u32[]{:S(2)}) collective-permute-start(bf16[4,64,384]{2,1,0:T(8,128)(2,1)S(1)} %get-tuple-element.28), channel_id=1, source_target_pairs={{0,8},{1,9},{4,12},{5,13},{8,0},{9,1},{12,4},{13,5},{2,10},{3,11},... | collective-permute-start | bytes 589832 | tf_op jit(solution)/shard_map/ppermute | solution.py:385
  25.6 11.4 %collective-permute-start.7 = (bf16[4,64,384]{2,1,0:T(8,128)(2,1)S(1)}, bf16[4,64,384]{2,1,0:T(8,128)(2,1)S(1)}, u32[]{:S(2)}, u32[]{:S(2)}) collective-permute-start(bf16[4,64,384]{2,1,0:T(8,128)(2,1)S(1)} %get-tuple-element.29), channel_id=1, source_target_pairs={{0,5},{1,4},{4,1},{5,0},{8,13},{9,12},{12,9},{13,8},{2,7},{3,6},{6... | collective-permute-start | bytes 589832 | tf_op jit(solution)/shard_map/ppermute | solution.py:385
  29.0 8.0 %collective-permute-start.8 = (bf16[1,8,2,16,384]{4,3,2,1,0:T(8,128)(2,1)S(1)}, bf16[1,8,2,16,384]{4,3,2,1,0:T(8,128)(2,1)S(1)}, u32[]{:S(2)}, u32[]{:S(2)}) collective-permute-start(bf16[1,8,2,16,384]{4,3,2,1,0:T(8,128)(2,1)S(1)} %bitcast.6), channel_id=1, source_target_pairs={{0,2},{2,0},{1,3},{3,1},{4,6},{6,4},{5,7},{7,5},{8,10},{10,8},{9,1... | collective-permute-start | bytes 589832 | tf_op jit(solution)/shard_map/ppermute | solution.py:392
  29.0 8.0 %collective-permute-start.9 = (bf16[1,8,2,16,384]{4,3,2,1,0:T(8,128)(2,1)S(1)}, bf16[1,8,2,16,384]{4,3,2,1,0:T(8,128)(2,1)S(1)}, u32[]{:S(2)}, u32[]{:S(2)}) collective-permute-start(bf16[1,8,2,16,384]{4,3,2,1,0:T(8,128)(2,1)S(1)} %bitcast.9), channel_id=1, source_target_pairs={{0,2},{2,0},{1,3},{3,1},{4,6},{6,4},{5,7},{7,5},{8,10},{10,8},{9,1... | collective-permute-start | bytes 589832 | tf_op jit(solution)/shard_map/ppermute | solution.py:392
  38.5 1.9 %collective-permute-start.10 = (bf16[8,32,896]{2,1,0:T(8,128)(2,1)S(1)}, bf16[8,32,896]{2,1,0:T(8,128)(2,1)S(1)}, u32[]{:S(2)}, u32[]{:S(2)}) collective-permute-start(bf16[8,32,896]{2,1,0:T(8,128)(2,1)S(1)} %bitcast.8), channel_id=1, source_target_pairs={{0,2},{2,0},{1,3},{3,1},{4,6},{6,4},{5,7},{7,5},{8,10},{10,8},{9,1... | collective-permute-start | bytes 1376264 | tf_op jit(solution)/shard_map/ppermute | solution.py:403
  41.8 8.9 %collective-permute-start.11 = (bf16[32,896]{1,0:T(8,128)(2,1)S(1)}, bf16[32,896]{1,0:T(8,128)(2,1)S(1)}, u32[]{:S(2)}, u32[]{:S(2)}) collective-permute-start(bf16[32,896]{1,0:T(8,128)(2,1)S(1)} %get-tuple-element.30), channel_id=1, source_target_pairs={{0,16},{4,20},{8,24},{12,28},{16,0},{20,4},{24,8},{28,12},{1,17},{... | collective-permute-start | bytes 172040 | tf_op jit(solution)/shard_map/ppermute | solution.py:406
  43.8 7.4 %collective-permute-start.12 = (bf16[32,896]{1,0:T(8,128)(2,1)S(1)}, bf16[32,896]{1,0:T(8,128)(2,1)S(1)}, u32[]{:S(2)}, u32[]{:S(2)}) collective-permute-start(bf16[32,896]{1,0:T(8,128)(2,1)S(1)} %get-tuple-element.31), channel_id=1, source_target_pairs={{0,24},{4,28},{8,16},{12,20},{16,8},{20,12},{24,0},{28,4},{1,25},{... | collective-permute-start | bytes 172040 | tf_op jit(solution)/shard_map/ppermute | solution.py:406
  44.7 9.7 %collective-permute-start.13 = (bf16[32,896]{1,0:T(8,128)(2,1)S(1)}, bf16[32,896]{1,0:T(8,128)(2,1)S(1)}, u32[]{:S(2)}, u32[]{:S(2)}) collective-permute-start(bf16[32,896]{1,0:T(8,128)(2,1)S(1)} %get-tuple-element.32), channel_id=1, source_target_pairs={{0,20},{4,16},{8,28},{12,24},{16,4},{20,0},{24,12},{28,8},{1,21},{... | collective-permute-start | bytes 172040 | tf_op jit(solution)/shard_map/ppermute | solution.py:406
  46.3 8.1 %collective-permute-start.14 = (bf16[32,896]{1,0:T(8,128)(2,1)S(1)}, bf16[32,896]{1,0:T(8,128)(2,1)S(1)}, u32[]{:S(2)}, u32[]{:S(2)}) collective-permute-start(bf16[32,896]{1,0:T(8,128)(2,1)S(1)} %get-tuple-element.33), channel_id=1, source_target_pairs={{0,28},{4,24},{8,20},{12,16},{16,12},{20,8},{24,4},{28,0},{1,29},{... | collective-permute-start | bytes 172040 | tf_op jit(solution)/shard_map/ppermute | solution.py:406
  48.7 6.3 %collective-permute-start.15 = (bf16[32,896]{1,0:T(8,128)(2,1)S(1)}, bf16[32,896]{1,0:T(8,128)(2,1)S(1)}, u32[]{:S(2)}, u32[]{:S(2)}) collective-permute-start(bf16[32,896]{1,0:T(8,128)(2,1)S(1)} %get-tuple-element.34), channel_id=1, source_target_pairs={{0,4},{4,0},{8,12},{12,8},{16,20},{20,16},{24,28},{28,24},{1,5},{5... | collective-permute-start | bytes 172040 | tf_op jit(solution)/shard_map/ppermute | solution.py:406
  50.8 4.9 %collective-permute-start.16 = (bf16[32,896]{1,0:T(8,128)(2,1)S(1)}, bf16[32,896]{1,0:T(8,128)(2,1)S(1)}, u32[]{:S(2)}, u32[]{:S(2)}) collective-permute-start(bf16[32,896]{1,0:T(8,128)(2,1)S(1)} %get-tuple-element.35), channel_id=1, source_target_pairs={{0,8},{4,12},{8,0},{12,4},{16,24},{20,28},{24,16},{28,20},{1,9},{5... | collective-permute-start | bytes 172040 | tf_op jit(solution)/shard_map/ppermute | solution.py:406
  51.2 5.1 %collective-permute-start.17 = (bf16[32,896]{1,0:T(8,128)(2,1)S(1)}, bf16[32,896]{1,0:T(8,128)(2,1)S(1)}, u32[]{:S(2)}, u32[]{:S(2)}) collective-permute-start(bf16[32,896]{1,0:T(8,128)(2,1)S(1)} %get-tuple-element.36), channel_id=1, source_target_pairs={{0,12},{4,8},{8,4},{12,0},{16,28},{20,24},{24,20},{28,16},{1,13},{... | collective-permute-start | bytes 172040 | tf_op jit(solution)/shard_map/ppermute | solution.py:406
  58.2 8.7 %collective-permute-start.18 = (bf16[64,2560]{1,0:T(8,128)(2,1)S(1)}, bf16[64,2560]{1,0:T(8,128)(2,1)S(1)}, u32[]{:S(2)}, u32[]{:S(2)}) collective-permute-start(bf16[64,2560]{1,0:T(8,128)(2,1)S(1)} %get-tuple-element.39), channel_id=1, source_target_pairs={{0,1},{1,0},{2,3},{3,2},{4,5},{5,4},{6,7},{7,6},{8,9},{9,8},{10,11... | collective-permute-start | bytes 983048 | tf_op jit(solution)/shard_map/ppermute | solution.py:416

commit v6 on v5

--- a/solution.py
+++ b/solution.py
@@ -12,8 +12,9 @@
 DH = 128
 NT = (((1,), (1,)), ((), ()))
 PART_TURNS = (4, 6, 5, 7, 1, 2, 3, 0)
-HOLD = 4
-TURNS = (0, 6, 1, 5, 2, 7, 4, 3)
+SPLIT = 4
+TURNS = (2, 4, 1)
+FAR = 7
 ATTEND_VMEM = 16 * 2**20
 PROJECT_VMEM = 20 * 2**20
 
@@ -33,10 +34,10 @@
     return terms
 
 
-def attend_kernel(heads, row_len, group, device_ref, after_ref, *refs):
-    query_refs, kv_refs, out_ref = refs[: -group - 1], refs[-group - 1 : -1], refs[-1]
-    plane_rows = group * row_len
+def attend_kernel(heads, row_len, kv_count, device_ref, after_ref, *refs):
+    query_refs, kv_refs, out_ref = refs[: -kv_count - 1], refs[-kv_count - 1 : -1], refs[-1]
     g_count, head_axis = out_ref.shape[1], out_ref.shape[2] // row_len
+    plane_rows = g_count * head_axis * row_len
     scale = DH ** (-0.5)
 
     def some_planes(blocks, planes):
@@ -193,7 +194,7 @@
 
 def merge_pair(device, home, away, heads, turns, g_count, head_axis):
     whole = pl.BlockSpec(memory_space=pltpu.VMEM)
-    count = home.shape[0]
+    count = len(turns)
     return pl.pallas_call(
         functools.partial(pair_kernel, heads, turns, g_count, head_axis),
         out_shape=[jax.ShapeDtypeStruct(home.shape[1:], home.dtype)] * count,
@@ -277,47 +278,83 @@
     )(device, pltpu.with_memory_space_constraint(weight, pltpu.HBM), *left, *held)
 
 
-def pack_kernel(turns, g_count, head_axis, device_ref, *refs):
-    group = len(turns)
-    matrix_refs, query_ref, piece_refs, sems = refs[:6], refs[6], refs[7:-1], refs[-1]
+def pack_kernel(g_count, head_axis, device_ref, *refs):
+    matrix_refs, (query_ref, own_ref, far_ref, mine_ref, other_ref) = refs[:6], refs[6:11]
+    held_refs, sems = refs[11:-1], refs[-1]
     width = query_ref.shape[3]
-    _, my_g, head = position(device_ref, g_count, head_axis)
-    copies = []
-
-    def copy(ref, first, to, *sem):
-        columns = pl.ds(pl.multiple_of(first * width, width), width)
-        copies.append(pltpu.make_async_copy(ref.at[:, columns], to, sems.at[sem]))
-
-    for i in range(group):
-        for t in range(2):
-            copy(matrix_refs[t], i, query_ref.at[i, t], i, t)
-    for i, turn in enumerate(turns):
-        partner = (my_g * head_axis + head) ^ turn
-        column = (partner % head_axis) * g_count + partner // head_axis
-        for t in range(4):
-            copy(matrix_refs[2 + t], column, piece_refs[i].at[t], i, 2 + t)
-    for each in copies:
-        each.start()
-    for each in copies:
-        each.wait()
-
-
-def pack(turns, g_count, head_axis, device, *matrices):
-    group = len(turns)
+    _, g, head = position(device_ref, g_count, head_axis)
+    core = device_ref[0] // head_axis % 2
+    copies = [
+        pltpu.make_async_copy(ref, held, sems.at[i])
+        for i, (ref, held) in enumerate(zip(matrix_refs, held_refs))
+    ]
+    for copy in copies:
+        copy.start()
+    for t in range(2):
+        copies[t].wait()
+        for i in range(query_ref.shape[0]):
+            query_ref[i, t] = held_refs[t][:, i * width : (i + 1) * width]
+    for t in range(4):
+        copies[2 + t].wait()
+
+        def piece(turn):
+            partner = (g * head_axis + head) ^ turn
+            column = (partner % head_axis) * g_count + partner // head_axis
+            return held_refs[2 + t][:, pl.ds(pl.multiple_of(column * width, width), width)]
+
+        own_ref[t] = piece(0)
+        far_ref[t] = piece(FAR)
+        for j, turn in enumerate(TURNS):
+            mine_ref[j, t] = piece(turn ^ (FAR * core))
+            other_ref[j, t] = piece(turn ^ (FAR * (1 - core)))
+
+
+def pack(group, g_count, head_axis, device, *matrices):
     rows, columns = matrices[0].shape
     width = columns // group
-    piece = jax.ShapeDtypeStruct((4, matrices[2].shape[0], width), jnp.bfloat16)
-    outs = [jax.ShapeDtypeStruct((group, 2, rows, width), jnp.bfloat16)] + [piece] * group
-    return pl.pallas_call(
-        functools.partial(pack_kernel, turns, g_count, head_axis),
-        out_shape=outs,
+    piece = (4, matrices[2].shape[0], width)
+    shapes = [(group, 2, rows, width), piece, piece] + [(len(TURNS),) + piece] * 2
+    return pl.pallas_call(
+        functools.partial(pack_kernel, g_count, head_axis),
+        out_shape=[jax.ShapeDtypeStruct(shape, jnp.bfloat16) for shape in shapes],
         in_specs=[pl.BlockSpec(memory_space=pltpu.SMEM)]
         + [pl.BlockSpec(memory_space=pl.ANY)] * len(matrices),
-        out_specs=[pl.BlockSpec(memory_space=pltpu.VMEM)] * len(outs),
-        scratch_shapes=[pltpu.SemaphoreType.DMA((group, len(matrices)))],
+        out_specs=[pl.BlockSpec(memory_space=pltpu.VMEM)] * len(shapes),
+        scratch_shapes=[pltpu.VMEM(m.shape, m.dtype) for m in matrices]
+        + [pltpu.SemaphoreType.DMA((len(matrices),))],
         compiler_params=pltpu.CompilerParams(vmem_limit_bytes=8 * 2**20),
         name="pack",
     )(device, *(pltpu.with_memory_space_constraint(m, pltpu.HBM) for m in matrices))
+
+
+def join_kernel(mine_ref, theirs_ref, *out_refs):
+    rows = mine_ref.shape[2]
+    for j, out_ref in enumerate(out_refs):
+        out_ref[:, :rows] = mine_ref[j]
+        out_ref[:, rows:] = theirs_ref[j]
+
+
+def join(mine, theirs):
+    count, tensors, rows, width = mine.shape
+    whole = pl.BlockSpec(memory_space=pltpu.VMEM)
+    return pl.pallas_call(
+        join_kernel,
+        out_shape=[jax.ShapeDtypeStruct((tensors, 2 * rows, width), mine.dtype)] * count,
+        in_specs=[whole, whole],
+        out_specs=[whole] * count,
+        compiler_params=pltpu.CompilerParams(vmem_limit_bytes=8 * 2**20),
+        name="join",
+    )(mine, theirs)
+
+
+def across_chips(turn, g_count, head_axis):
+    pairs = []
+    for n in range(g_count * head_axis):
+        for core in range(2):
+            m = n ^ turn ^ (FAR * core)
+            number = [(i // head_axis * 2 + core) * head_axis + i % head_axis for i in (n, m)]
+            pairs.append(tuple(number))
+    return pairs
 
 
 def hold_kernel(head_axis, device_ref, weight_ref, after_ref, out_ref, sems):
@@ -366,10 +403,9 @@
     def within_plane(x):
         return lax.all_to_all(x, plane_axes, split_axis=0, concat_axis=0, tiled=True)
 
-    turns = sorted(range(group), key=TURNS.index)
     device = lax.axis_index(("k", "g", "core", "head")).astype(jnp.int32).reshape(1)
-    packed_queries, *kv = pack(
-        turns,
+    packed_queries, own, far, mine, other = pack(
+        group,
         g_count,
         head_axis,
         device,
@@ -381,10 +417,13 @@
         value_tangent,
     )
     plane_queries = within_plane(packed_queries)
-    kv = [
-        lax.ppermute(piece, ("g", "head"), [(i, i ^ d) for i in range(group)]) if d else piece
-        for d, piece in zip(turns, kv)
+    pieces = join(mine, lax.ppermute(other, "core", swap))
+    kv = [own]
+    kv += [
+        lax.ppermute(piece, ("g", "core", "head"), across_chips(turn, g_count, head_axis))
+        for turn, piece in zip(TURNS, pieces)
     ]
+    kv.append(lax.ppermute(far, ("g", "head"), [(i, i ^ FAR) for i in range(group)]))
     if k == 2:
         home_queries = [plane_queries[None], lax.ppermute(plane_queries, "k", swap)[None]]
     else:
@@ -392,7 +431,7 @@
     away_queries = [lax.ppermute(q, "core", swap) for q in home_queries]
 
     width = out_weight.shape[1] // head_axis
-    held = [hold(device, out_weight, head_axis, kv[HOLD])] if head_axis == 2 else []
+    held = [hold(device, out_weight, head_axis, own)] if head_axis == 2 else []
     away, home = (
         attend(some, kv, device, k, g_count, head_axis, (held + kv)[0])
         for some in (away_queries, home_queries)
@@ -401,7 +440,12 @@
     count = k * g_count
     part_turns = PART_TURNS if count == len(PART_TURNS) else tuple(range(count))
     arrived = lax.ppermute(away, "core", swap)
-    parts = merge_pair(device, home, arrived, heads, part_turns, g_count, head_axis)
+    part_turns = part_turns[SPLIT:] + part_turns[:SPLIT]
+    last, first = (
+        merge_pair(device, home, arrived, heads, some, g_count, head_axis)
+        for some in (part_turns[:-SPLIT], part_turns[-SPLIT:])
+    )
+    parts = last + first
     parts = [
         lax.ppermute(part, ("k", "g"), [(i, i ^ d) for i in range(count)]) if d else part
         for d, part in zip(part_turns, parts)

time: 68 us -> 66.9 us (0.984)
  waiting for transfers between devices: 20.5 us -> 19.5 us
    ppermute x7 -> x5, starting transfers between devices: 9.6 us -> 5.86 us  [the longest x1 3.82 us: local(): lax.ppermute(far, ('g', 'head'), [(i, i ^ FAR) for i in range(group)])]
    ppermute x1, starting transfers between devices: 0.08 us -> 2.87 us  [local(): arrived = lax.ppermute(away, 'core', swap)]
    ppermute x7, waiting for transfers between devices: 4.67 us -> 2.37 us  [local(): lax.ppermute(part, ('k', 'g'), [(i, i ^ d) for i in range(count)])]
    ppermute x1, waiting for transfers between devices: 0.01 us -> 1.85 us  [local(): lax.ppermute(plane_queries, 'k', swap)[None]]
    ppermute x7, starting transfers between devices: 9.78 us -> 11.4 us  [local(): lax.ppermute(part, ('k', 'g'), [(i, i ^ d) for i in range(count)])]
    all_to_all x1, waiting for transfers between devices: 3 us -> 3.82 us  [within_plane(): lax.all_to_all(x, plane_axes, split_axis=0, concat_axis=0, tiled=True)]
    ppermute x7 -> x5, waiting for transfers between devices: 8.5 us -> 7.89 us  [the longest x1 4.3 us: local(): lax.ppermute(far, ('g', 'head'), [(i, i ^ FAR) for i in range(group)])]
    pallas_call x1 -> x2, Pallas kernels: 2.62 us -> 2.33 us  [the longest x1 2.23 us: pack(): pl.pallas_call(functools.partial(pack_kernel, g_count, head_axis), out_sh...]
  transfers between devices with their start and end apart: 20 -> 18, of which waited for: 14 -> 9; matrix products, arithmetic and copies ran while one was open for 0% -> 0% of each run, Pallas kernels for 13% -> 14%
where the time goes in v6:
time: 66.9 us; the launch traced here: 66.7 us
  starting transfers between devices  29.8 us (45%)
  waiting for transfers between devices  19.5 us (29%)
  Pallas kernels  15.8 us (24%)
  between operations  0.76 us (1%)
  local copies, waits for them, and re-layouts  0.74 us (1%)
    ppermute x7, starting transfers between devices, local(): lax.ppermute(part, ('k', 'g'), [(i, i ^ d) for i in range(count)])  11.4 us
    all_to_all x1, starting transfers between devices, within_plane(): lax.all_to_all(x, plane_axes, split_axis=0, concat_axis=0, tiled=True)  5.76 us
    pallas_call x2, Pallas kernels, project(): pl.pallas_call(kernel, out_shape=outs, in_specs=[scalar, pl.BlockSpec(mem...  5.73 us
    ppermute x1, waiting for transfers between devices, local(): lax.ppermute(far, ('g', 'head'), [(i, i ^ FAR) for i in range(group)])  4.3 us
    ppermute x1, starting transfers between devices, local(): lax.ppermute(far, ('g', 'head'), [(i, i ^ FAR) for i in range(group)])  3.82 us
    all_to_all x1, waiting for transfers between devices, within_plane(): lax.all_to_all(x, plane_axes, split_axis=0, concat_axis=0, tiled=True)  3.82 us
    ppermute x3, waiting for transfers between devices, local(): lax.ppermute(piece, ('g', 'core', 'head'), across_chips(turn, g_count, he...  3.59 us
    ppermute x1, waiting for transfers between devices, local(): received = lax.ppermute(sent, 'head', swap)  3.56 us
  transfers between devices with their start and end apart: 18, of which 9 were waited for; matrix products, arithmetic and copies ran while one was open for 0% of the time, Pallas kernels for 14%

profile of v6, /device:TPU:0, one launch (start us, length us, event | category | flops | bytes accessed | tf_op | source)
XLA Modules:
  0.0 66.7 jit_solution(12152477279210143175)
XLA Ops:
  0.6 2.2 %pack.1 = (bf16[8,2,16,384]{3,2,1,0:T(8,128)(2,1)}, bf16[4,64,384]{2,1,0:T(8,128)(2,1)S(1)}, bf16[4,64,384]{2,1,0:T(8,128)(2,1)S(1)}, bf16[3,4,64,384]{3,2,1,0:T(8,128)(2,1)S(1)}, bf16[3,4,64,384]{3,2,1,0:T(8,128)(2,1)S(1)}) custom-call(s32[1]{0:T(128)} %bitcast.device_ref, bf16[16,3072]{1,0:T(8,128)(2,1)} %refs_0_.1, bf16[16,3072]{1,0:T(8,128)(2,1)} %refs_1_.1, ...), custom_call_target="tpu_custom_call" | custom-call | tf_op jit(solution)/shard_map/pack/pallas_call | solution.py:317
  3.4 5.8 %all-to-all-start = ((bf16[8,2,16,384]{3,2,1,0:T(8,128)(2,1)}), bf16[8,2,16,384]{3,2,1,0:T(8,128)(2,1)S(1)}, u32[]{:S(2)}, u32[]{:S(2)}) async-start(bf16[8,2,16,384]{3,2,1,0:T(8,128)(2,1)} %get-tuple-element.21), calls=%async_computation | async-start | bytes 393216 | tf_op jit(solution)/shard_map/all_to_all | solution.py:404
  9.2 3.8 %collective-permute-start.5 = (bf16[4,64,384]{2,1,0:T(8,128)(2,1)S(1)}, bf16[4,64,384]{2,1,0:T(8,128)(2,1)S(1)}, u32[]{:S(2)}, u32[]{:S(2)}) collective-permute-start(bf16[4,64,384]{2,1,0:T(8,128)(2,1)S(1)} %get-tuple-element.27), channel_id=1, source_target_pairs={{0,13},{1,12},{4,9},{5,8},{8,5},{9,4},{12,1},{13,0},{2,15},{3,14},... | collective-permute-start | bytes 589832 | tf_op jit(solution)/shard_map/ppermute | solution.py:426
  13.0 3.8 %all-to-all-done = bf16[8,2,16,384]{3,2,1,0:T(8,128)(2,1)S(1)} async-done(((bf16[8,2,16,384]{3,2,1,0:T(8,128)(2,1)}), bf16[8,2,16,384]{3,2,1,0:T(8,128)(2,1)S(1)}, u32[]{:S(2)}, u32[]{:S(2)}) %all-to-all-start) | async-done | bytes 196640 | tf_op jit(solution)/shard_map/all_to_all | solution.py:404
  16.8 2.6 %collective-permute-start = (bf16[8,2,16,384]{3,2,1,0:T(8,128)(2,1)S(1)}, bf16[8,2,16,384]{3,2,1,0:T(8,128)(2,1)S(1)}, u32[]{:S(2)}, u32[]{:S(2)}) collective-permute-start(bf16[8,2,16,384]{3,2,1,0:T(8,128)(2,1)S(1)} %all-to-all-done), channel_id=1, source_target_pairs={{0,16},{16,0},{1,17},{17,1},{2,18},{18,2},{3,19},{19,3},{4,20},{20... | collective-permute-start | bytes 589832 | tf_op jit(solution)/shard_map/ppermute | solution.py:428
  19.6 1.1 %collective-permute-start.3 = (bf16[4,128,384]{2,1,0:T(8,128)(2,1)S(1)}, bf16[4,128,384]{2,1,0:T(8,128)(2,1)S(1)}, u32[]{:S(2)}, u32[]{:S(2)}) collective-permute-start(bf16[4,128,384]{2,1,0:T(8,128)(2,1)S(1)} %get-tuple-element.25), channel_id=1, source_target_pairs={{0,8},{2,7},{1,9},{3,6},{4,12},{6,3},{5,13},{7,2},{8,0},{10,15},{9... | collective-permute-start | bytes 1179656 | tf_op jit(solution)/shard_map/ppermute | solution.py:423
  21.0 4.3 %collective-permute-done.5.refs_6_ = bf16[4,64,384]{2,1,0:T(8,128)(2,1)S(1)} collective-permute-done((bf16[4,64,384]{2,1,0:T(8,128)(2,1)S(1)}, bf16[4,64,384]{2,1,0:T(8,128)(2,1)S(1)}, u32[]{:S(2)}, u32[]{:S(2)}) %collective-permute-start.5) | collective-permute-done | bytes 196640 | tf_op jit(solution)/shard_map/ppermute | solution.py:426
  25.3 1.8 %collective-permute-done = bf16[8,2,16,384]{3,2,1,0:T(8,128)(2,1)S(1)} collective-permute-done((bf16[8,2,16,384]{3,2,1,0:T(8,128)(2,1)S(1)}, bf16[8,2,16,384]{3,2,1,0:T(8,128)(2,1)S(1)}, u32[]{:S(2)}, u32[]{:S(2)}) %collective-permute-start) | collective-permute-done | bytes 196640 | tf_op jit(solution)/shard_map/ppermute | solution.py:428
  27.2 3.3 %hold.1.after_ref.refs_8_ = bf16[1536,2560]{1,0:T(8,128)(2,1)S(1)} custom-call(s32[1]{0:T(128)} %bitcast.device_ref, bf16[1536,5120]{1,0:T(8,128)(2,1)} %weight_ref.5, bf16[4,64,384]{2,1,0:T(8,128)(2,1)S(1)} %get-tuple-element.20.after_ref.refs_2_), custom_call_target="tpu_custom_call" | custom-call | bytes 7864320 | tf_op jit(solution)/shard_map/hold/pallas_call | solution.py:383
  30.5 3.4 %collective-permute-done.3.refs_4_ = bf16[4,128,384]{2,1,0:T(8,128)(2,1)S(1)} collective-permute-done((bf16[4,128,384]{2,1,0:T(8,128)(2,1)S(1)}, bf16[4,128,384]{2,1,0:T(8,128)(2,1)S(1)}, u32[]{:S(2)}, u32[]{:S(2)}) %collective-permute-start.3) | collective-permute-done | bytes 393248 | tf_op jit(solution)/shard_map/ppermute | solution.py:423
  34.1 1.5 %attend.3 = bf16[2,4,32,896]{3,2,1,0:T(8,128)(2,1)S(1)} custom-call(s32[1]{0:T(128)} %bitcast.device_ref, bf16[1536,2560]{1,0:T(8,128)(2,1)S(1)} %hold.1.after_ref.refs_8_, bf16[1,8,2,16,384]{4,3,2,1,0:T(8,128)(2,1)S(1)} %collective-permute-done.6.refs_0_, bf16[1,8,2,16,384]{4,3,2,1,0:T(8,128)(2,1)S(1)} %collective-permute-done.7.refs_1_, ...), custom_call_target="tpu_custom_call" | custom-call | tf_op jit(solution)/shard_map/attend/pallas_call | solution.py:119
  35.6 2.9 %collective-permute-start.8 = (bf16[8,32,896]{2,1,0:T(8,128)(2,1)S(1)}, bf16[8,32,896]{2,1,0:T(8,128)(2,1)S(1)}, u32[]{:S(2)}, u32[]{:S(2)}) collective-permute-start(bf16[8,32,896]{2,1,0:T(8,128)(2,1)S(1)} %bitcast.9), channel_id=1, source_target_pairs={{0,2},{2,0},{1,3},{3,1},{4,6},{6,4},{5,7},{7,5},{8,10},{10,8},{9,1... | collective-permute-start | bytes 1376264 | tf_op jit(solution)/shard_map/ppermute | solution.py:442
  38.5 1.5 %attend.2 = bf16[2,4,32,896]{3,2,1,0:T(8,128)(2,1)S(1)} custom-call(s32[1]{0:T(128)} %bitcast.device_ref, bf16[1536,2560]{1,0:T(8,128)(2,1)S(1)} %hold.1.after_ref.refs_8_, bf16[1,8,2,16,384]{4,3,2,1,0:T(8,128)(2,1)S(1)} %bitcast.8, bf16[1,8,2,16,384]{4,3,2,1,0:T(8,128)(2,1)S(1)} %bitcast.11, bf16[4,64,384]{2,1,0:T(8,128)(2,1)S(1)} %get-tuple-element.20.after_ref.refs_2_, ...), custom_call_target="tpu_custom_call" | custom-call | tf_op jit(solution)/shard_map/attend/pallas_call | solution.py:119
  40.7 1.8 %collective-permute-start.12 = (bf16[32,896]{1,0:T(8,128)(2,1)S(1)}, bf16[32,896]{1,0:T(8,128)(2,1)S(1)}, u32[]{:S(2)}, u32[]{:S(2)}) collective-permute-start(bf16[32,896]{1,0:T(8,128)(2,1)S(1)} %get-tuple-element.32), channel_id=1, source_target_pairs={{0,16},{4,20},{8,24},{12,28},{16,0},{20,4},{24,8},{28,12},{1,17},{... | collective-permute-start | bytes 172040 | tf_op jit(solution)/shard_map/ppermute | solution.py:450
  43.1 2.2 %collective-permute-start.14 = (bf16[32,896]{1,0:T(8,128)(2,1)S(1)}, bf16[32,896]{1,0:T(8,128)(2,1)S(1)}, u32[]{:S(2)}, u32[]{:S(2)}) collective-permute-start(bf16[32,896]{1,0:T(8,128)(2,1)S(1)} %get-tuple-element.34), channel_id=1, source_target_pairs={{0,20},{4,16},{8,28},{12,24},{16,4},{20,0},{24,12},{28,8},{1,21},{... | collective-permute-start | bytes 172040 | tf_op jit(solution)/shard_map/ppermute | solution.py:450
  45.3 2.3 %collective-permute-start.15 = (bf16[32,896]{1,0:T(8,128)(2,1)S(1)}, bf16[32,896]{1,0:T(8,128)(2,1)S(1)}, u32[]{:S(2)}, u32[]{:S(2)}) collective-permute-start(bf16[32,896]{1,0:T(8,128)(2,1)S(1)} %get-tuple-element.35), channel_id=1, source_target_pairs={{0,28},{4,24},{8,20},{12,16},{16,12},{20,8},{24,4},{28,0},{1,29},{... | collective-permute-start | bytes 172040 | tf_op jit(solution)/shard_map/ppermute | solution.py:450
  48.7 1.2 %collective-permute-start.10 = (bf16[32,896]{1,0:T(8,128)(2,1)S(1)}, bf16[32,896]{1,0:T(8,128)(2,1)S(1)}, u32[]{:S(2)}, u32[]{:S(2)}) collective-permute-start(bf16[32,896]{1,0:T(8,128)(2,1)S(1)} %get-tuple-element.29), channel_id=1, source_target_pairs={{0,8},{4,12},{8,0},{12,4},{16,24},{20,28},{24,16},{28,20},{1,9},{5... | collective-permute-start | bytes 172040 | tf_op jit(solution)/shard_map/ppermute | solution.py:450
  49.9 3.0 %collective-permute-start.11 = (bf16[32,896]{1,0:T(8,128)(2,1)S(1)}, bf16[32,896]{1,0:T(8,128)(2,1)S(1)}, u32[]{:S(2)}, u32[]{:S(2)}) collective-permute-start(bf16[32,896]{1,0:T(8,128)(2,1)S(1)} %get-tuple-element.30), channel_id=1, source_target_pairs={{0,12},{4,8},{8,4},{12,0},{16,28},{20,24},{24,20},{28,16},{1,13},{... | collective-permute-start | bytes 172040 | tf_op jit(solution)/shard_map/ppermute | solution.py:450
  54.1 1.2 %collective-permute-done.11.refs_2_ = bf16[32,896]{1,0:T(8,128)(2,1)S(1)} collective-permute-done((bf16[32,896]{1,0:T(8,128)(2,1)S(1)}, bf16[32,896]{1,0:T(8,128)(2,1)S(1)}, u32[]{:S(2)}, u32[]{:S(2)}) %collective-permute-start.11) | collective-permute-done | bytes 57376 | tf_op jit(solution)/shard_map/ppermute | solution.py:450
  55.3 1.9 %project.2 = (bf16[64,2560]{1,0:T(8,128)(2,1)S(1)}, bf16[64,1536]{1,0:T(8,128)(2,1)S(1)}) custom-call(s32[1]{0:T(128)} %bitcast.device_ref, bf16[1536,5120]{1,0:T(8,128)(2,1)} %weight_ref.5, bf16[32,896]{1,0:T(8,128)(2,1)S(1)} %collective-permute-done.9.refs_0_, bf16[32,896]{1,0:T(8,128)(2,1)S(1)} %collective-permute-done.10.refs_1_, ...), custom_call_target="tpu_custom_call" | custom-call | flops 503316480 | bytes 7864320 | tf_op jit(solution)/shard_map/project/pallas_call | solution.py:267
  57.1 1.3 %collective-permute-start.16 = (bf16[64,2560]{1,0:T(8,128)(2,1)S(1)}, bf16[64,2560]{1,0:T(8,128)(2,1)S(1)}, u32[]{:S(2)}, u32[]{:S(2)}) collective-permute-start(bf16[64,2560]{1,0:T(8,128)(2,1)S(1)} %get-tuple-element.37), channel_id=1, source_target_pairs={{0,1},{1,0},{2,3},{3,2},{4,5},{5,4},{6,7},{7,6},{8,9},{9,8},{10,11... | collective-permute-start | bytes 983048 | tf_op jit(solution)/shard_map/ppermute | solution.py:460
  58.5 3.9 %project.3 = f32[64,2560]{1,0:T(8,128)S(1)} custom-call(s32[1]{0:T(128)} %bitcast.device_ref, bf16[1536,5120]{1,0:T(8,128)(2,1)} %weight_ref.5, bf16[64,1536]{1,0:T(8,128)(2,1)S(1)} %get-tuple-element.36.both_ref), custom_call_target="tpu_custom_call" | custom-call | flops 503316480 | bytes 7864320 | tf_op jit(solution)/shard_map/project/pallas_call | solution.py:267
  62.3 3.6 %collective-permute-done.16 = bf16[64,2560]{1,0:T(8,128)(2,1)S(1)} collective-permute-done((bf16[64,2560]{1,0:T(8,128)(2,1)S(1)}, bf16[64,2560]{1,0:T(8,128)(2,1)S(1)}, u32[]{:S(2)}, u32[]{:S(2)}) %collective-permute-start.16) | collective-permute-done | bytes 327712 | tf_op jit(solution)/shard_map/ppermute | solution.py:460
  66.0 0.7 %fusion = (bf16[32,2560]{1,0:T(8,128)(2,1)}, bf16[32,2560]{1,0:T(8,128)(2,1)}) fusion(bf16[64,2560]{1,0:T(8,128)(2,1)S(1)} %add_convert_fusion), kind=kLoop, calls=%fused_computation.1 | loop fusion | bytes 655360 | tf_op jit(solution)/shard_map/slice | solution.py:470
  (23 shorter events, 4.8 us)
Async XLA Ops:
  2.9 16.5 %collective-permute-start.1 = (bf16[3,4,64,384]{3,2,1,0:T(8,128)(2,1)S(1)}, bf16[3,4,64,384]{3,2,1,0:T(8,128)(2,1)S(1)}, u32[]{:S(2)}, u32[]{:S(2)}) collective-permute-start(bf16[3,4,64,384]{3,2,1,0:T(8,128)(2,1)S(1)} %get-tuple-element.23), channel_id=1, source_target_pairs={{0,2},{2,0},{1,3},{3,1},{4,6},{6,4},{5,7},{7,5},{8,10},{10,8},{9,1... | collective-permute-start | bytes 1769480 | tf_op jit(solution)/shard_map/ppermute | solution.py:420
  3.4 13.4 %all-to-all-start = ((bf16[8,2,16,384]{3,2,1,0:T(8,128)(2,1)}), bf16[8,2,16,384]{3,2,1,0:T(8,128)(2,1)S(1)}, u32[]{:S(2)}, u32[]{:S(2)}) async-start(bf16[8,2,16,384]{3,2,1,0:T(8,128)(2,1)} %get-tuple-element.21), calls=%async_computation | async-start | bytes 393216 | tf_op jit(solution)/shard_map/all_to_all | solution.py:404
  9.2 16.2 %collective-permute-start.5 = (bf16[4,64,384]{2,1,0:T(8,128)(2,1)S(1)}, bf16[4,64,384]{2,1,0:T(8,128)(2,1)S(1)}, u32[]{:S(2)}, u32[]{:S(2)}) collective-permute-start(bf16[4,64,384]{2,1,0:T(8,128)(2,1)S(1)} %get-tuple-element.27), channel_id=1, source_target_pairs={{0,13},{1,12},{4,9},{5,8},{8,5},{9,4},{12,1},{13,0},{2,15},{3,14},... | collective-permute-start | bytes 589832 | tf_op jit(solution)/shard_map/ppermute | solution.py:426
  16.8 10.4 %collective-permute-start = (bf16[8,2,16,384]{3,2,1,0:T(8,128)(2,1)S(1)}, bf16[8,2,16,384]{3,2,1,0:T(8,128)(2,1)S(1)}, u32[]{:S(2)}, u32[]{:S(2)}) collective-permute-start(bf16[8,2,16,384]{3,2,1,0:T(8,128)(2,1)S(1)} %all-to-all-done), channel_id=1, source_target_pairs={{0,16},{16,0},{1,17},{17,1},{2,18},{18,2},{3,19},{19,3},{4,20},{20... | collective-permute-start | bytes 589832 | tf_op jit(solution)/shard_map/ppermute | solution.py:428
  19.5 11.0 %collective-permute-start.2 = (bf16[4,128,384]{2,1,0:T(8,128)(2,1)S(1)}, bf16[4,128,384]{2,1,0:T(8,128)(2,1)S(1)}, u32[]{:S(2)}, u32[]{:S(2)}) collective-permute-start(bf16[4,128,384]{2,1,0:T(8,128)(2,1)S(1)} %get-tuple-element.24), channel_id=1, source_target_pairs={{0,4},{2,11},{1,5},{3,10},{4,0},{6,15},{5,1},{7,14},{8,12},{10,3},... | collective-permute-start | bytes 1179656 | tf_op jit(solution)/shard_map/ppermute | solution.py:423
  19.6 14.4 %collective-permute-start.3 = (bf16[4,128,384]{2,1,0:T(8,128)(2,1)S(1)}, bf16[4,128,384]{2,1,0:T(8,128)(2,1)S(1)}, u32[]{:S(2)}, u32[]{:S(2)}) collective-permute-start(bf16[4,128,384]{2,1,0:T(8,128)(2,1)S(1)} %get-tuple-element.25), channel_id=1, source_target_pairs={{0,8},{2,7},{1,9},{3,6},{4,12},{6,3},{5,13},{7,2},{8,0},{10,15},{9... | collective-permute-start | bytes 1179656 | tf_op jit(solution)/shard_map/ppermute | solution.py:423
  20.7 13.4 %collective-permute-start.4 = (bf16[4,128,384]{2,1,0:T(8,128)(2,1)S(1)}, bf16[4,128,384]{2,1,0:T(8,128)(2,1)S(1)}, u32[]{:S(2)}, u32[]{:S(2)}) collective-permute-start(bf16[4,128,384]{2,1,0:T(8,128)(2,1)S(1)} %get-tuple-element.26), channel_id=1, source_target_pairs={{0,1},{2,14},{1,0},{3,15},{4,5},{6,10},{5,4},{7,11},{8,9},{10,6},{... | collective-permute-start | bytes 1179656 | tf_op jit(solution)/shard_map/ppermute | solution.py:423
  25.3 5.2 %collective-permute-start.6 = (bf16[1,8,2,16,384]{4,3,2,1,0:T(8,128)(2,1)S(1)}, bf16[1,8,2,16,384]{4,3,2,1,0:T(8,128)(2,1)S(1)}, u32[]{:S(2)}, u32[]{:S(2)}) collective-permute-start(bf16[1,8,2,16,384]{4,3,2,1,0:T(8,128)(2,1)S(1)} %bitcast.7), channel_id=1, source_target_pairs={{0,2},{2,0},{1,3},{3,1},{4,6},{6,4},{5,7},{7,5},{8,10},{10,8},{9,1... | collective-permute-start | bytes 589832 | tf_op jit(solution)/shard_map/ppermute | solution.py:431
  27.2 3.3 %collective-permute-start.7 = (bf16[1,8,2,16,384]{4,3,2,1,0:T(8,128)(2,1)S(1)}, bf16[1,8,2,16,384]{4,3,2,1,0:T(8,128)(2,1)S(1)}, u32[]{:S(2)}, u32[]{:S(2)}) collective-permute-start(bf16[1,8,2,16,384]{4,3,2,1,0:T(8,128)(2,1)S(1)} %bitcast.10), channel_id=1, source_target_pairs={{0,2},{2,0},{1,3},{3,1},{4,6},{6,4},{5,7},{7,5},{8,10},{10,8},{9,1... | collective-permute-start | bytes 589832 | tf_op jit(solution)/shard_map/ppermute | solution.py:431
  35.6 4.4 %collective-permute-start.8 = (bf16[8,32,896]{2,1,0:T(8,128)(2,1)S(1)}, bf16[8,32,896]{2,1,0:T(8,128)(2,1)S(1)}, u32[]{:S(2)}, u32[]{:S(2)}) collective-permute-start(bf16[8,32,896]{2,1,0:T(8,128)(2,1)S(1)} %bitcast.9), channel_id=1, source_target_pairs={{0,2},{2,0},{1,3},{3,1},{4,6},{6,4},{5,7},{7,5},{8,10},{10,8},{9,1... | collective-permute-start | bytes 1376264 | tf_op jit(solution)/shard_map/ppermute | solution.py:442
  40.7 8.0 %collective-permute-start.12 = (bf16[32,896]{1,0:T(8,128)(2,1)S(1)}, bf16[32,896]{1,0:T(8,128)(2,1)S(1)}, u32[]{:S(2)}, u32[]{:S(2)}) collective-permute-start(bf16[32,896]{1,0:T(8,128)(2,1)S(1)} %get-tuple-element.32), channel_id=1, source_target_pairs={{0,16},{4,20},{8,24},{12,28},{16,0},{20,4},{24,8},{28,12},{1,17},{... | collective-permute-start | bytes 172040 | tf_op jit(solution)/shard_map/ppermute | solution.py:450
  42.6 7.4 %collective-permute-start.13 = (bf16[32,896]{1,0:T(8,128)(2,1)S(1)}, bf16[32,896]{1,0:T(8,128)(2,1)S(1)}, u32[]{:S(2)}, u32[]{:S(2)}) collective-permute-start(bf16[32,896]{1,0:T(8,128)(2,1)S(1)} %get-tuple-element.33), channel_id=1, source_target_pairs={{0,24},{4,28},{8,16},{12,20},{16,8},{20,12},{24,0},{28,4},{1,25},{... | collective-permute-start | bytes 172040 | tf_op jit(solution)/shard_map/ppermute | solution.py:450
  43.1 10.5 %collective-permute-start.14 = (bf16[32,896]{1,0:T(8,128)(2,1)S(1)}, bf16[32,896]{1,0:T(8,128)(2,1)S(1)}, u32[]{:S(2)}, u32[]{:S(2)}) collective-permute-start(bf16[32,896]{1,0:T(8,128)(2,1)S(1)} %get-tuple-element.34), channel_id=1, source_target_pairs={{0,20},{4,16},{8,28},{12,24},{16,4},{20,0},{24,12},{28,8},{1,21},{... | collective-permute-start | bytes 172040 | tf_op jit(solution)/shard_map/ppermute | solution.py:450
  45.3 8.3 %collective-permute-start.15 = (bf16[32,896]{1,0:T(8,128)(2,1)S(1)}, bf16[32,896]{1,0:T(8,128)(2,1)S(1)}, u32[]{:S(2)}, u32[]{:S(2)}) collective-permute-start(bf16[32,896]{1,0:T(8,128)(2,1)S(1)} %get-tuple-element.35), channel_id=1, source_target_pairs={{0,28},{4,24},{8,20},{12,16},{16,12},{20,8},{24,4},{28,0},{1,29},{... | collective-permute-start | bytes 172040 | tf_op jit(solution)/shard_map/ppermute | solution.py:450
  48.3 5.8 %collective-permute-start.9 = (bf16[32,896]{1,0:T(8,128)(2,1)S(1)}, bf16[32,896]{1,0:T(8,128)(2,1)S(1)}, u32[]{:S(2)}, u32[]{:S(2)}) collective-permute-start(bf16[32,896]{1,0:T(8,128)(2,1)S(1)} %get-tuple-element.28), channel_id=1, source_target_pairs={{0,4},{4,0},{8,12},{12,8},{16,20},{20,16},{24,28},{28,24},{1,5},{5... | collective-permute-start | bytes 172040 | tf_op jit(solution)/shard_map/ppermute | solution.py:450
  48.7 5.4 %collective-permute-start.10 = (bf16[32,896]{1,0:T(8,128)(2,1)S(1)}, bf16[32,896]{1,0:T(8,128)(2,1)S(1)}, u32[]{:S(2)}, u32[]{:S(2)}) collective-permute-start(bf16[32,896]{1,0:T(8,128)(2,1)S(1)} %get-tuple-element.29), channel_id=1, source_target_pairs={{0,8},{4,12},{8,0},{12,4},{16,24},{20,28},{24,16},{28,20},{1,9},{5... | collective-permute-start | bytes 172040 | tf_op jit(solution)/shard_map/ppermute | solution.py:450
  49.9 5.3 %collective-permute-start.11 = (bf16[32,896]{1,0:T(8,128)(2,1)S(1)}, bf16[32,896]{1,0:T(8,128)(2,1)S(1)}, u32[]{:S(2)}, u32[]{:S(2)}) collective-permute-start(bf16[32,896]{1,0:T(8,128)(2,1)S(1)} %get-tuple-element.30), channel_id=1, source_target_pairs={{0,12},{4,8},{8,4},{12,0},{16,28},{20,24},{24,20},{28,16},{1,13},{... | collective-permute-start | bytes 172040 | tf_op jit(solution)/shard_map/ppermute | solution.py:450
  57.1 8.7 %collective-permute-start.16 = (bf16[64,2560]{1,0:T(8,128)(2,1)S(1)}, bf16[64,2560]{1,0:T(8,128)(2,1)S(1)}, u32[]{:S(2)}, u32[]{:S(2)}) collective-permute-start(bf16[64,2560]{1,0:T(8,128)(2,1)S(1)} %get-tuple-element.37), channel_id=1, source_target_pairs={{0,1},{1,0},{2,3},{3,2},{4,5},{5,4},{6,7},{7,6},{8,9},{9,8},{10,11... | collective-permute-start | bytes 983048 | tf_op jit(solution)/shard_map/ppermute | solution.py:460

commit v7 on v6

--- a/solution.py
+++ b/solution.py
@@ -13,7 +13,7 @@
 NT = (((1,), (1,)), ((), ()))
 PART_TURNS = (4, 6, 5, 7, 1, 2, 3, 0)
 SPLIT = 4
-TURNS = (2, 4, 1)
+TURNS = (2, 1, 4)
 FAR = 7
 ATTEND_VMEM = 16 * 2**20
 PROJECT_VMEM = 20 * 2**20

time: 66.9 us -> 66.7 us (level)
  starting transfers between devices: 29.8 us -> 28.3 us
  waiting for transfers between devices: 19.5 us -> 20.9 us
    ppermute x7, waiting for transfers between devices: 2.37 us -> 3.61 us  [local(): lax.ppermute(part, ('k', 'g'), [(i, i ^ d) for i in range(count)])]
    ppermute x7, starting transfers between devices: 11.4 us -> 10.3 us  [local(): lax.ppermute(part, ('k', 'g'), [(i, i ^ d) for i in range(count)])]
  transfers between devices with their start and end apart: 18 -> 18, of which waited for: 9 -> 10; matrix products, arithmetic and copies ran while one was open for 0% -> 0% of each run, Pallas kernels for 14% -> 14%
where the time goes in v7:
time: 66.7 us; the launch traced here: 66.5 us
  starting transfers between devices  28.3 us (42%)
  waiting for transfers between devices  20.9 us (31%)
  Pallas kernels  15.8 us (24%)
  between operations  0.76 us (1%)
  local copies, waits for them, and re-layouts  0.74 us (1%)
    ppermute x7, starting transfers between devices, local(): lax.ppermute(part, ('k', 'g'), [(i, i ^ d) for i in range(count)])  10.3 us
    all_to_all x1, starting transfers between devices, within_plane(): lax.all_to_all(x, plane_axes, split_axis=0, concat_axis=0, tiled=True)  5.76 us
    pallas_call x2, Pallas kernels, project(): pl.pallas_call(kernel, out_shape=outs, in_specs=[scalar, pl.BlockSpec(mem...  5.72 us
    ppermute x1, waiting for transfers between devices, local(): lax.ppermute(far, ('g', 'head'), [(i, i ^ FAR) for i in range(group)])  4.3 us
    ppermute x3, waiting for transfers between devices, local(): lax.ppermute(piece, ('g', 'core', 'head'), across_chips(turn, g_count, he...  4.14 us
    ppermute x1, starting transfers between devices, local(): lax.ppermute(far, ('g', 'head'), [(i, i ^ FAR) for i in range(group)])  3.82 us
    all_to_all x1, waiting for transfers between devices, within_plane(): lax.all_to_all(x, plane_axes, split_axis=0, concat_axis=0, tiled=True)  3.82 us
    ppermute x7, waiting for transfers between devices, local(): lax.ppermute(part, ('k', 'g'), [(i, i ^ d) for i in range(count)])  3.61 us
  transfers between devices with their start and end apart: 18, of which 10 were waited for; matrix products, arithmetic and copies ran while one was open for 0% of the time, Pallas kernels for 14%

profile of v7, /device:TPU:0, one launch (start us, length us, event | category | flops | bytes accessed | tf_op | source)
XLA Modules:
  0.0 66.5 jit_solution(4037417523487067225)
XLA Ops:
  0.6 2.2 %pack.1 = (bf16[8,2,16,384]{3,2,1,0:T(8,128)(2,1)}, bf16[4,64,384]{2,1,0:T(8,128)(2,1)S(1)}, bf16[4,64,384]{2,1,0:T(8,128)(2,1)S(1)}, bf16[3,4,64,384]{3,2,1,0:T(8,128)(2,1)S(1)}, bf16[3,4,64,384]{3,2,1,0:T(8,128)(2,1)S(1)}) custom-call(s32[1]{0:T(128)} %bitcast.device_ref, bf16[16,3072]{1,0:T(8,128)(2,1)} %refs_0_.1, bf16[16,3072]{1,0:T(8,128)(2,1)} %refs_1_.1, ...), custom_call_target="tpu_custom_call" | custom-call | tf_op jit(solution)/shard_map/pack/pallas_call | solution.py:317
  3.4 5.8 %all-to-all-start = ((bf16[8,2,16,384]{3,2,1,0:T(8,128)(2,1)}), bf16[8,2,16,384]{3,2,1,0:T(8,128)(2,1)S(1)}, u32[]{:S(2)}, u32[]{:S(2)}) async-start(bf16[8,2,16,384]{3,2,1,0:T(8,128)(2,1)} %get-tuple-element.21), calls=%async_computation | async-start | bytes 393216 | tf_op jit(solution)/shard_map/all_to_all | solution.py:404
  9.2 3.8 %collective-permute-start.5 = (bf16[4,64,384]{2,1,0:T(8,128)(2,1)S(1)}, bf16[4,64,384]{2,1,0:T(8,128)(2,1)S(1)}, u32[]{:S(2)}, u32[]{:S(2)}) collective-permute-start(bf16[4,64,384]{2,1,0:T(8,128)(2,1)S(1)} %get-tuple-element.27), channel_id=1, source_target_pairs={{0,13},{1,12},{4,9},{5,8},{8,5},{9,4},{12,1},{13,0},{2,15},{3,14},... | collective-permute-start | bytes 589832 | tf_op jit(solution)/shard_map/ppermute | solution.py:426
  13.0 3.8 %all-to-all-done = bf16[8,2,16,384]{3,2,1,0:T(8,128)(2,1)S(1)} async-done(((bf16[8,2,16,384]{3,2,1,0:T(8,128)(2,1)}), bf16[8,2,16,384]{3,2,1,0:T(8,128)(2,1)S(1)}, u32[]{:S(2)}, u32[]{:S(2)}) %all-to-all-start) | async-done | bytes 196640 | tf_op jit(solution)/shard_map/all_to_all | solution.py:404
  16.8 2.6 %collective-permute-start = (bf16[8,2,16,384]{3,2,1,0:T(8,128)(2,1)S(1)}, bf16[8,2,16,384]{3,2,1,0:T(8,128)(2,1)S(1)}, u32[]{:S(2)}, u32[]{:S(2)}) collective-permute-start(bf16[8,2,16,384]{3,2,1,0:T(8,128)(2,1)S(1)} %all-to-all-done), channel_id=1, source_target_pairs={{0,16},{16,0},{1,17},{17,1},{2,18},{18,2},{3,19},{19,3},{4,20},{20... | collective-permute-start | bytes 589832 | tf_op jit(solution)/shard_map/ppermute | solution.py:428
  20.2 0.8 %collective-permute-start.4 = (bf16[4,128,384]{2,1,0:T(8,128)(2,1)S(1)}, bf16[4,128,384]{2,1,0:T(8,128)(2,1)S(1)}, u32[]{:S(2)}, u32[]{:S(2)}) collective-permute-start(bf16[4,128,384]{2,1,0:T(8,128)(2,1)S(1)} %get-tuple-element.26), channel_id=1, source_target_pairs={{0,8},{2,7},{1,9},{3,6},{4,12},{6,3},{5,13},{7,2},{8,0},{10,15},{9... | collective-permute-start | bytes 1179656 | tf_op jit(solution)/shard_map/ppermute | solution.py:423
  21.0 4.3 %collective-permute-done.5.refs_6_ = bf16[4,64,384]{2,1,0:T(8,128)(2,1)S(1)} collective-permute-done((bf16[4,64,384]{2,1,0:T(8,128)(2,1)S(1)}, bf16[4,64,384]{2,1,0:T(8,128)(2,1)S(1)}, u32[]{:S(2)}, u32[]{:S(2)}) %collective-permute-start.5) | collective-permute-done | bytes 196640 | tf_op jit(solution)/shard_map/ppermute | solution.py:426
  25.3 1.8 %collective-permute-done = bf16[8,2,16,384]{3,2,1,0:T(8,128)(2,1)S(1)} collective-permute-done((bf16[8,2,16,384]{3,2,1,0:T(8,128)(2,1)S(1)}, bf16[8,2,16,384]{3,2,1,0:T(8,128)(2,1)S(1)}, u32[]{:S(2)}, u32[]{:S(2)}) %collective-permute-start) | collective-permute-done | bytes 196640 | tf_op jit(solution)/shard_map/ppermute | solution.py:428
  27.2 3.3 %hold.1.after_ref.refs_8_ = bf16[1536,2560]{1,0:T(8,128)(2,1)S(1)} custom-call(s32[1]{0:T(128)} %bitcast.device_ref, bf16[1536,5120]{1,0:T(8,128)(2,1)} %weight_ref.5, bf16[4,64,384]{2,1,0:T(8,128)(2,1)S(1)} %get-tuple-element.20.after_ref.refs_2_), custom_call_target="tpu_custom_call" | custom-call | bytes 7864320 | tf_op jit(solution)/shard_map/hold/pallas_call | solution.py:383
  30.5 4.1 %collective-permute-done.3.refs_4_ = bf16[4,128,384]{2,1,0:T(8,128)(2,1)S(1)} collective-permute-done((bf16[4,128,384]{2,1,0:T(8,128)(2,1)S(1)}, bf16[4,128,384]{2,1,0:T(8,128)(2,1)S(1)}, u32[]{:S(2)}, u32[]{:S(2)}) %collective-permute-start.3) | collective-permute-done | bytes 393248 | tf_op jit(solution)/shard_map/ppermute | solution.py:423
  34.7 1.5 %attend.3 = bf16[2,4,32,896]{3,2,1,0:T(8,128)(2,1)S(1)} custom-call(s32[1]{0:T(128)} %bitcast.device_ref, bf16[1536,2560]{1,0:T(8,128)(2,1)S(1)} %hold.1.after_ref.refs_8_, bf16[1,8,2,16,384]{4,3,2,1,0:T(8,128)(2,1)S(1)} %collective-permute-done.6.refs_0_, bf16[1,8,2,16,384]{4,3,2,1,0:T(8,128)(2,1)S(1)} %collective-permute-done.7.refs_1_, ...), custom_call_target="tpu_custom_call" | custom-call | tf_op jit(solution)/shard_map/attend/pallas_call | solution.py:119
  36.2 2.4 %collective-permute-start.8 = (bf16[8,32,896]{2,1,0:T(8,128)(2,1)S(1)}, bf16[8,32,896]{2,1,0:T(8,128)(2,1)S(1)}, u32[]{:S(2)}, u32[]{:S(2)}) collective-permute-start(bf16[8,32,896]{2,1,0:T(8,128)(2,1)S(1)} %bitcast.9), channel_id=1, source_target_pairs={{0,2},{2,0},{1,3},{3,1},{4,6},{6,4},{5,7},{7,5},{8,10},{10,8},{9,1... | collective-permute-start | bytes 1376264 | tf_op jit(solution)/shard_map/ppermute | solution.py:442
  38.6 1.5 %attend.2 = bf16[2,4,32,896]{3,2,1,0:T(8,128)(2,1)S(1)} custom-call(s32[1]{0:T(128)} %bitcast.device_ref, bf16[1536,2560]{1,0:T(8,128)(2,1)S(1)} %hold.1.after_ref.refs_8_, bf16[1,8,2,16,384]{4,3,2,1,0:T(8,128)(2,1)S(1)} %bitcast.8, bf16[1,8,2,16,384]{4,3,2,1,0:T(8,128)(2,1)S(1)} %bitcast.11, bf16[4,64,384]{2,1,0:T(8,128)(2,1)S(1)} %get-tuple-element.20.after_ref.refs_2_, ...), custom_call_target="tpu_custom_call" | custom-call | tf_op jit(solution)/shard_map/attend/pallas_call | solution.py:119
  40.8 1.8 %collective-permute-start.12 = (bf16[32,896]{1,0:T(8,128)(2,1)S(1)}, bf16[32,896]{1,0:T(8,128)(2,1)S(1)}, u32[]{:S(2)}, u32[]{:S(2)}) collective-permute-start(bf16[32,896]{1,0:T(8,128)(2,1)S(1)} %get-tuple-element.32), channel_id=1, source_target_pairs={{0,16},{4,20},{8,24},{12,28},{16,0},{20,4},{24,8},{28,12},{1,17},{... | collective-permute-start | bytes 172040 | tf_op jit(solution)/shard_map/ppermute | solution.py:450
  42.6 1.2 %collective-permute-start.13 = (bf16[32,896]{1,0:T(8,128)(2,1)S(1)}, bf16[32,896]{1,0:T(8,128)(2,1)S(1)}, u32[]{:S(2)}, u32[]{:S(2)}) collective-permute-start(bf16[32,896]{1,0:T(8,128)(2,1)S(1)} %get-tuple-element.33), channel_id=1, source_target_pairs={{0,24},{4,28},{8,16},{12,20},{16,8},{20,12},{24,0},{28,4},{1,25},{... | collective-permute-start | bytes 172040 | tf_op jit(solution)/shard_map/ppermute | solution.py:450
  43.8 1.5 %collective-permute-start.14 = (bf16[32,896]{1,0:T(8,128)(2,1)S(1)}, bf16[32,896]{1,0:T(8,128)(2,1)S(1)}, u32[]{:S(2)}, u32[]{:S(2)}) collective-permute-start(bf16[32,896]{1,0:T(8,128)(2,1)S(1)} %get-tuple-element.34), channel_id=1, source_target_pairs={{0,20},{4,16},{8,28},{12,24},{16,4},{20,0},{24,12},{28,8},{1,21},{... | collective-permute-start | bytes 172040 | tf_op jit(solution)/shard_map/ppermute | solution.py:450
  45.3 2.4 %collective-permute-start.15 = (bf16[32,896]{1,0:T(8,128)(2,1)S(1)}, bf16[32,896]{1,0:T(8,128)(2,1)S(1)}, u32[]{:S(2)}, u32[]{:S(2)}) collective-permute-start(bf16[32,896]{1,0:T(8,128)(2,1)S(1)} %get-tuple-element.35), channel_id=1, source_target_pairs={{0,28},{4,24},{8,20},{12,16},{16,12},{20,8},{24,4},{28,0},{1,29},{... | collective-permute-start | bytes 172040 | tf_op jit(solution)/shard_map/ppermute | solution.py:450
  49.0 1.2 %collective-permute-done.12.refs_4_ = bf16[32,896]{1,0:T(8,128)(2,1)S(1)} collective-permute-done((bf16[32,896]{1,0:T(8,128)(2,1)S(1)}, bf16[32,896]{1,0:T(8,128)(2,1)S(1)}, u32[]{:S(2)}, u32[]{:S(2)}) %collective-permute-start.12) | collective-permute-done | bytes 57376 | tf_op jit(solution)/shard_map/ppermute | solution.py:450
  50.2 2.8 %collective-permute-start.11 = (bf16[32,896]{1,0:T(8,128)(2,1)S(1)}, bf16[32,896]{1,0:T(8,128)(2,1)S(1)}, u32[]{:S(2)}, u32[]{:S(2)}) collective-permute-start(bf16[32,896]{1,0:T(8,128)(2,1)S(1)} %get-tuple-element.30), channel_id=1, source_target_pairs={{0,12},{4,8},{8,4},{12,0},{16,28},{20,24},{24,20},{28,16},{1,13},{... | collective-permute-start | bytes 172040 | tf_op jit(solution)/shard_map/ppermute | solution.py:450
  54.7 0.8 %collective-permute-done.11.refs_2_ = bf16[32,896]{1,0:T(8,128)(2,1)S(1)} collective-permute-done((bf16[32,896]{1,0:T(8,128)(2,1)S(1)}, bf16[32,896]{1,0:T(8,128)(2,1)S(1)}, u32[]{:S(2)}, u32[]{:S(2)}) %collective-permute-start.11) | collective-permute-done | bytes 57376 | tf_op jit(solution)/shard_map/ppermute | solution.py:450
  55.4 1.9 %project.2 = (bf16[64,2560]{1,0:T(8,128)(2,1)S(1)}, bf16[64,1536]{1,0:T(8,128)(2,1)S(1)}) custom-call(s32[1]{0:T(128)} %bitcast.device_ref, bf16[1536,5120]{1,0:T(8,128)(2,1)} %weight_ref.5, bf16[32,896]{1,0:T(8,128)(2,1)S(1)} %collective-permute-done.9.refs_0_, bf16[32,896]{1,0:T(8,128)(2,1)S(1)} %collective-permute-done.10.refs_1_, ...), custom_call_target="tpu_custom_call" | custom-call | flops 503316480 | bytes 7864320 | tf_op jit(solution)/shard_map/project/pallas_call | solution.py:267
  57.3 1.3 %collective-permute-start.16 = (bf16[64,2560]{1,0:T(8,128)(2,1)S(1)}, bf16[64,2560]{1,0:T(8,128)(2,1)S(1)}, u32[]{:S(2)}, u32[]{:S(2)}) collective-permute-start(bf16[64,2560]{1,0:T(8,128)(2,1)S(1)} %get-tuple-element.37), channel_id=1, source_target_pairs={{0,1},{1,0},{2,3},{3,2},{4,5},{5,4},{6,7},{7,6},{8,9},{9,8},{10,11... | collective-permute-start | bytes 983048 | tf_op jit(solution)/shard_map/ppermute | solution.py:460
  58.7 3.8 %project.3 = f32[64,2560]{1,0:T(8,128)S(1)} custom-call(s32[1]{0:T(128)} %bitcast.device_ref, bf16[1536,5120]{1,0:T(8,128)(2,1)} %weight_ref.5, bf16[64,1536]{1,0:T(8,128)(2,1)S(1)} %get-tuple-element.36.both_ref), custom_call_target="tpu_custom_call" | custom-call | flops 503316480 | bytes 7864320 | tf_op jit(solution)/shard_map/project/pallas_call | solution.py:267
  62.5 3.1 %collective-permute-done.16 = bf16[64,2560]{1,0:T(8,128)(2,1)S(1)} collective-permute-done((bf16[64,2560]{1,0:T(8,128)(2,1)S(1)}, bf16[64,2560]{1,0:T(8,128)(2,1)S(1)}, u32[]{:S(2)}, u32[]{:S(2)}) %collective-permute-start.16) | collective-permute-done | bytes 327712 | tf_op jit(solution)/shard_map/ppermute | solution.py:460
  (23 shorter events, 5.9 us)
Async XLA Ops:
  2.9 16.5 %collective-permute-start.1 = (bf16[3,4,64,384]{3,2,1,0:T(8,128)(2,1)S(1)}, bf16[3,4,64,384]{3,2,1,0:T(8,128)(2,1)S(1)}, u32[]{:S(2)}, u32[]{:S(2)}) collective-permute-start(bf16[3,4,64,384]{3,2,1,0:T(8,128)(2,1)S(1)} %get-tuple-element.23), channel_id=1, source_target_pairs={{0,2},{2,0},{1,3},{3,1},{4,6},{6,4},{5,7},{7,5},{8,10},{10,8},{9,1... | collective-permute-start | bytes 1769480 | tf_op jit(solution)/shard_map/ppermute | solution.py:420
  3.4 13.4 %all-to-all-start = ((bf16[8,2,16,384]{3,2,1,0:T(8,128)(2,1)}), bf16[8,2,16,384]{3,2,1,0:T(8,128)(2,1)S(1)}, u32[]{:S(2)}, u32[]{:S(2)}) async-start(bf16[8,2,16,384]{3,2,1,0:T(8,128)(2,1)} %get-tuple-element.21), calls=%async_computation | async-start | bytes 393216 | tf_op jit(solution)/shard_map/all_to_all | solution.py:404
  9.2 16.2 %collective-permute-start.5 = (bf16[4,64,384]{2,1,0:T(8,128)(2,1)S(1)}, bf16[4,64,384]{2,1,0:T(8,128)(2,1)S(1)}, u32[]{:S(2)}, u32[]{:S(2)}) collective-permute-start(bf16[4,64,384]{2,1,0:T(8,128)(2,1)S(1)} %get-tuple-element.27), channel_id=1, source_target_pairs={{0,13},{1,12},{4,9},{5,8},{8,5},{9,4},{12,1},{13,0},{2,15},{3,14},... | collective-permute-start | bytes 589832 | tf_op jit(solution)/shard_map/ppermute | solution.py:426
  16.8 10.4 %collective-permute-start = (bf16[8,2,16,384]{3,2,1,0:T(8,128)(2,1)S(1)}, bf16[8,2,16,384]{3,2,1,0:T(8,128)(2,1)S(1)}, u32[]{:S(2)}, u32[]{:S(2)}) collective-permute-start(bf16[8,2,16,384]{3,2,1,0:T(8,128)(2,1)S(1)} %all-to-all-done), channel_id=1, source_target_pairs={{0,16},{16,0},{1,17},{17,1},{2,18},{18,2},{3,19},{19,3},{4,20},{20... | collective-permute-start | bytes 589832 | tf_op jit(solution)/shard_map/ppermute | solution.py:428
  19.5 11.0 %collective-permute-start.2 = (bf16[4,128,384]{2,1,0:T(8,128)(2,1)S(1)}, bf16[4,128,384]{2,1,0:T(8,128)(2,1)S(1)}, u32[]{:S(2)}, u32[]{:S(2)}) collective-permute-start(bf16[4,128,384]{2,1,0:T(8,128)(2,1)S(1)} %get-tuple-element.24), channel_id=1, source_target_pairs={{0,4},{2,11},{1,5},{3,10},{4,0},{6,15},{5,1},{7,14},{8,12},{10,3},... | collective-permute-start | bytes 1179656 | tf_op jit(solution)/shard_map/ppermute | solution.py:423
  19.6 15.1 %collective-permute-start.3 = (bf16[4,128,384]{2,1,0:T(8,128)(2,1)S(1)}, bf16[4,128,384]{2,1,0:T(8,128)(2,1)S(1)}, u32[]{:S(2)}, u32[]{:S(2)}) collective-permute-start(bf16[4,128,384]{2,1,0:T(8,128)(2,1)S(1)} %get-tuple-element.25), channel_id=1, source_target_pairs={{0,1},{2,14},{1,0},{3,15},{4,5},{6,10},{5,4},{7,11},{8,9},{10,6},{... | collective-permute-start | bytes 1179656 | tf_op jit(solution)/shard_map/ppermute | solution.py:423
  20.2 14.5 %collective-permute-start.4 = (bf16[4,128,384]{2,1,0:T(8,128)(2,1)S(1)}, bf16[4,128,384]{2,1,0:T(8,128)(2,1)S(1)}, u32[]{:S(2)}, u32[]{:S(2)}) collective-permute-start(bf16[4,128,384]{2,1,0:T(8,128)(2,1)S(1)} %get-tuple-element.26), channel_id=1, source_target_pairs={{0,8},{2,7},{1,9},{3,6},{4,12},{6,3},{5,13},{7,2},{8,0},{10,15},{9... | collective-permute-start | bytes 1179656 | tf_op jit(solution)/shard_map/ppermute | solution.py:423
  25.3 5.2 %collective-permute-start.6 = (bf16[1,8,2,16,384]{4,3,2,1,0:T(8,128)(2,1)S(1)}, bf16[1,8,2,16,384]{4,3,2,1,0:T(8,128)(2,1)S(1)}, u32[]{:S(2)}, u32[]{:S(2)}) collective-permute-start(bf16[1,8,2,16,384]{4,3,2,1,0:T(8,128)(2,1)S(1)} %bitcast.7), channel_id=1, source_target_pairs={{0,2},{2,0},{1,3},{3,1},{4,6},{6,4},{5,7},{7,5},{8,10},{10,8},{9,1... | collective-permute-start | bytes 589832 | tf_op jit(solution)/shard_map/ppermute | solution.py:431
  27.2 3.3 %collective-permute-start.7 = (bf16[1,8,2,16,384]{4,3,2,1,0:T(8,128)(2,1)S(1)}, bf16[1,8,2,16,384]{4,3,2,1,0:T(8,128)(2,1)S(1)}, u32[]{:S(2)}, u32[]{:S(2)}) collective-permute-start(bf16[1,8,2,16,384]{4,3,2,1,0:T(8,128)(2,1)S(1)} %bitcast.10), channel_id=1, source_target_pairs={{0,2},{2,0},{1,3},{3,1},{4,6},{6,4},{5,7},{7,5},{8,10},{10,8},{9,1... | collective-permute-start | bytes 589832 | tf_op jit(solution)/shard_map/ppermute | solution.py:431
  36.2 3.9 %collective-permute-start.8 = (bf16[8,32,896]{2,1,0:T(8,128)(2,1)S(1)}, bf16[8,32,896]{2,1,0:T(8,128)(2,1)S(1)}, u32[]{:S(2)}, u32[]{:S(2)}) collective-permute-start(bf16[8,32,896]{2,1,0:T(8,128)(2,1)S(1)} %bitcast.9), channel_id=1, source_target_pairs={{0,2},{2,0},{1,3},{3,1},{4,6},{6,4},{5,7},{7,5},{8,10},{10,8},{9,1... | collective-permute-start | bytes 1376264 | tf_op jit(solution)/shard_map/ppermute | solution.py:442
  40.8 9.4 %collective-permute-start.12 = (bf16[32,896]{1,0:T(8,128)(2,1)S(1)}, bf16[32,896]{1,0:T(8,128)(2,1)S(1)}, u32[]{:S(2)}, u32[]{:S(2)}) collective-permute-start(bf16[32,896]{1,0:T(8,128)(2,1)S(1)} %get-tuple-element.32), channel_id=1, source_target_pairs={{0,16},{4,20},{8,24},{12,28},{16,0},{20,4},{24,8},{28,12},{1,17},{... | collective-permute-start | bytes 172040 | tf_op jit(solution)/shard_map/ppermute | solution.py:450
  42.6 7.7 %collective-permute-start.13 = (bf16[32,896]{1,0:T(8,128)(2,1)S(1)}, bf16[32,896]{1,0:T(8,128)(2,1)S(1)}, u32[]{:S(2)}, u32[]{:S(2)}) collective-permute-start(bf16[32,896]{1,0:T(8,128)(2,1)S(1)} %get-tuple-element.33), channel_id=1, source_target_pairs={{0,24},{4,28},{8,16},{12,20},{16,8},{20,12},{24,0},{28,4},{1,25},{... | collective-permute-start | bytes 172040 | tf_op jit(solution)/shard_map/ppermute | solution.py:450
  43.8 10.0 %collective-permute-start.14 = (bf16[32,896]{1,0:T(8,128)(2,1)S(1)}, bf16[32,896]{1,0:T(8,128)(2,1)S(1)}, u32[]{:S(2)}, u32[]{:S(2)}) collective-permute-start(bf16[32,896]{1,0:T(8,128)(2,1)S(1)} %get-tuple-element.34), channel_id=1, source_target_pairs={{0,20},{4,16},{8,28},{12,24},{16,4},{20,0},{24,12},{28,8},{1,21},{... | collective-permute-start | bytes 172040 | tf_op jit(solution)/shard_map/ppermute | solution.py:450
  45.3 8.5 %collective-permute-start.15 = (bf16[32,896]{1,0:T(8,128)(2,1)S(1)}, bf16[32,896]{1,0:T(8,128)(2,1)S(1)}, u32[]{:S(2)}, u32[]{:S(2)}) collective-permute-start(bf16[32,896]{1,0:T(8,128)(2,1)S(1)} %get-tuple-element.35), channel_id=1, source_target_pairs={{0,28},{4,24},{8,20},{12,16},{16,12},{20,8},{24,4},{28,0},{1,29},{... | collective-permute-start | bytes 172040 | tf_op jit(solution)/shard_map/ppermute | solution.py:450
  48.3 6.1 %collective-permute-start.9 = (bf16[32,896]{1,0:T(8,128)(2,1)S(1)}, bf16[32,896]{1,0:T(8,128)(2,1)S(1)}, u32[]{:S(2)}, u32[]{:S(2)}) collective-permute-start(bf16[32,896]{1,0:T(8,128)(2,1)S(1)} %get-tuple-element.28), channel_id=1, source_target_pairs={{0,4},{4,0},{8,12},{12,8},{16,20},{20,16},{24,28},{28,24},{1,5},{5... | collective-permute-start | bytes 172040 | tf_op jit(solution)/shard_map/ppermute | solution.py:450
  50.2 4.4 %collective-permute-start.10 = (bf16[32,896]{1,0:T(8,128)(2,1)S(1)}, bf16[32,896]{1,0:T(8,128)(2,1)S(1)}, u32[]{:S(2)}, u32[]{:S(2)}) collective-permute-start(bf16[32,896]{1,0:T(8,128)(2,1)S(1)} %get-tuple-element.29), channel_id=1, source_target_pairs={{0,8},{4,12},{8,0},{12,4},{16,24},{20,28},{24,16},{28,20},{1,9},{5... | collective-permute-start | bytes 172040 | tf_op jit(solution)/shard_map/ppermute | solution.py:450
  50.2 5.2 %collective-permute-start.11 = (bf16[32,896]{1,0:T(8,128)(2,1)S(1)}, bf16[32,896]{1,0:T(8,128)(2,1)S(1)}, u32[]{:S(2)}, u32[]{:S(2)}) collective-permute-start(bf16[32,896]{1,0:T(8,128)(2,1)S(1)} %get-tuple-element.30), channel_id=1, source_target_pairs={{0,12},{4,8},{8,4},{12,0},{16,28},{20,24},{24,20},{28,16},{1,13},{... | collective-permute-start | bytes 172040 | tf_op jit(solution)/shard_map/ppermute | solution.py:450
  57.3 8.3 %collective-permute-start.16 = (bf16[64,2560]{1,0:T(8,128)(2,1)S(1)}, bf16[64,2560]{1,0:T(8,128)(2,1)S(1)}, u32[]{:S(2)}, u32[]{:S(2)}) collective-permute-start(bf16[64,2560]{1,0:T(8,128)(2,1)S(1)} %get-tuple-element.37), channel_id=1, source_target_pairs={{0,1},{1,0},{2,3},{3,2},{4,5},{5,4},{6,7},{7,6},{8,9},{9,8},{10,11... | collective-permute-start | bytes 983048 | tf_op jit(solution)/shard_map/ppermute | solution.py:460

commit v8 on v7

--- a/solution.py
+++ b/solution.py
@@ -211,8 +211,8 @@
         *refs, out_ref, both_ref = refs
         parts_refs, held_refs = refs[:-held_count], refs[-held_count:]
         merge(my_g, parts_refs, both_ref, heads, g_count, turns)
-        for i, held in enumerate(held_refs):
-            times(both_ref, held[...], out_ref, i)
+        for held in held_refs:
+            times(both_ref, held[:, : out_ref.shape[1]], out_ref, 0)
     else:
         *parts_refs, out_ref, both_ref, held, sems = refs
         copies = fetch(0, weight_ref, held, sems)
@@ -225,6 +225,36 @@
     out_ref[:, i * tile : (i + 1) * tile] = jnp.dot(
         both_ref[...], columns, preferred_element_type=jnp.float32
     ).astype(out_ref.dtype)
+
+
+def rest_kernel(device_ref, weight_ref, both_ref, held_ref, out_ref):
+    times(both_ref, held_ref[:, held_ref.shape[1] - out_ref.shape[1] :], out_ref, 0)
+
+
+def sum_kernel(own_ref, received_ref, *refs):
+    rows = own_ref.shape[0] // 2
+    total = (own_ref[...] + received_ref[...].astype(jnp.float32)).astype(jnp.bfloat16)
+    refs[-2][...] = total[:rows]
+    refs[-1][...] = total[rows:]
+
+
+def sum_columns(own, received, part, outs=()):
+    rows, tile = own.shape[0] // 2, received.shape[1]
+    shape = jax.ShapeDtypeStruct((rows, own.shape[1]), jnp.bfloat16)
+    return pl.pallas_call(
+        sum_kernel,
+        grid=(1,),
+        out_shape=[shape] * 2,
+        in_specs=[
+            pl.BlockSpec((2 * rows, tile), lambda n: (0, part)),
+            pl.BlockSpec((2 * rows, tile), lambda n: (0, 0)),
+        ]
+        + [pl.BlockSpec(memory_space=pl.ANY)] * len(outs),
+        out_specs=[pl.BlockSpec((rows, tile), lambda n: (0, part))] * 2,
+        input_output_aliases={2 + i: i for i in range(len(outs))},
+        compiler_params=pltpu.CompilerParams(vmem_limit_bytes=8 * 2**20),
+        name="sum_columns",
+    )(own, received, *outs)
 
 
 def second_kernel(head_axis, device_ref, weight_ref, both_ref, out_ref, held, sems):
@@ -454,13 +484,21 @@
     merged = (2 * rows, out_weight.shape[0])
     merging = functools.partial(first_kernel, heads, g_count, head_axis, part_turns, len(held))
     if head_axis == 2:
+        first = width // 2
         sent, both = project(
-            merging, device, parts, out_weight, width, jnp.bfloat16, merged, held
+            merging, device, parts, out_weight, first, jnp.bfloat16, merged, held
         )
-        received = lax.ppermute(sent, "head", swap)
+        received = [lax.ppermute(sent, "head", swap)]
+        (sent,) = project(
+            rest_kernel, device, [both], out_weight, width - first, jnp.bfloat16, None, held
+        )
+        received.append(lax.ppermute(sent, "head", swap))
         own_half = functools.partial(second_kernel, head_axis)
         (own,) = project(own_half, device, [both], out_weight, width, jnp.float32)
-        total = own + received.astype(jnp.float32)
+        outs = ()
+        for part, arrived in enumerate(received):
+            outs = sum_columns(own, arrived, part, outs)
+        return tuple(outs)
     else:
         partial, _ = project(
             merging, device, parts, out_weight, width * head_axis, jnp.float32, merged

time: 66.7 us -> 66.4 us (level)
  waiting for transfers between devices: 20.9 us -> 19.1 us
  Pallas kernels: 15.8 us -> 17.3 us
  starting transfers between devices: 28.3 us -> 29.1 us
  local copies, waits for them, and re-layouts: 0.74 us -> 0 us
    ppermute x1 -> x2, waiting for transfers between devices: 3.14 us -> 1.39 us  [the longest x1 1.07 us: local(): received.append(lax.ppermute(sent, 'head', swap))]
    pallas_call x0 -> x2, Pallas kernels: none -> 1.36 us  [sum_columns(): pl.pallas_call(sum_kernel, grid=(1,), out_shape=[shape] * 2, in_specs=[pl...]
    ppermute x1 -> x2, starting transfers between devices: 1.34 us -> 2.15 us  [the longest x1 1.34 us: local(): received = [lax.ppermute(sent, 'head', swap)]]
    slice x1 -> x0, local copies, waits for them, and re-layouts: 0.74 us -> none  [local(): return (total[:rows], total[rows:])]
    pallas_call x2 -> x3, Pallas kernels: 5.72 us -> 5.84 us  [project(): pl.pallas_call(kernel, out_shape=outs, in_specs=[scalar, pl.BlockSpec(mem...]
  transfers between devices with their start and end apart: 18 -> 19, of which waited for: 10 -> 11; matrix products, arithmetic and copies ran while one was open for 0% -> 0% of each run, Pallas kernels for 14% -> 17%
where the time goes in v8:
time: 66.4 us; the launch traced here: 66.2 us
  starting transfers between devices  29.1 us (44%)
  waiting for transfers between devices  19.1 us (29%)
  Pallas kernels  17.3 us (26%)
  between operations  0.75 us (1%)
    ppermute x7, starting transfers between devices, local(): lax.ppermute(part, ('k', 'g'), [(i, i ^ d) for i in range(count)])  10.3 us
    pallas_call x3, Pallas kernels, project(): pl.pallas_call(kernel, out_shape=outs, in_specs=[scalar, pl.BlockSpec(mem...  5.84 us
    all_to_all x1, starting transfers between devices, within_plane(): lax.all_to_all(x, plane_axes, split_axis=0, concat_axis=0, tiled=True)  5.76 us
    ppermute x1, waiting for transfers between devices, local(): lax.ppermute(far, ('g', 'head'), [(i, i ^ FAR) for i in range(group)])  4.3 us
    ppermute x3, waiting for transfers between devices, local(): lax.ppermute(piece, ('g', 'core', 'head'), across_chips(turn, g_count, he...  4.14 us
    ppermute x1, starting transfers between devices, local(): lax.ppermute(far, ('g', 'head'), [(i, i ^ FAR) for i in range(group)])  3.82 us
    all_to_all x1, waiting for transfers between devices, within_plane(): lax.all_to_all(x, plane_axes, split_axis=0, concat_axis=0, tiled=True)  3.82 us
    ppermute x7, waiting for transfers between devices, local(): lax.ppermute(part, ('k', 'g'), [(i, i ^ d) for i in range(count)])  3.62 us
  transfers between devices with their start and end apart: 19, of which 11 were waited for; matrix products, arithmetic and copies ran while one was open for 0% of the time, Pallas kernels for 17%

profile of v8, /device:TPU:0, one launch (start us, length us, event | category | flops | bytes accessed | tf_op | source)
XLA Modules:
  0.0 66.2 jit_solution(18222471853399589365)
XLA Ops:
  0.6 2.2 %pack.1 = (bf16[8,2,16,384]{3,2,1,0:T(8,128)(2,1)}, bf16[4,64,384]{2,1,0:T(8,128)(2,1)S(1)}, bf16[4,64,384]{2,1,0:T(8,128)(2,1)S(1)}, bf16[3,4,64,384]{3,2,1,0:T(8,128)(2,1)S(1)}, bf16[3,4,64,384]{3,2,1,0:T(8,128)(2,1)S(1)}) custom-call(s32[1]{0:T(128)} %bitcast.device_ref, bf16[16,3072]{1,0:T(8,128)(2,1)} %refs_0_.1, bf16[16,3072]{1,0:T(8,128)(2,1)} %refs_1_.1, ...), custom_call_target="tpu_custom_call" | custom-call | tf_op jit(solution)/shard_map/pack/pallas_call | solution.py:347
  3.4 5.8 %all-to-all-start = ((bf16[8,2,16,384]{3,2,1,0:T(8,128)(2,1)}), bf16[8,2,16,384]{3,2,1,0:T(8,128)(2,1)S(1)}, u32[]{:S(2)}, u32[]{:S(2)}) async-start(bf16[8,2,16,384]{3,2,1,0:T(8,128)(2,1)} %get-tuple-element.23), calls=%async_computation | async-start | bytes 393216 | tf_op jit(solution)/shard_map/all_to_all | solution.py:434
  9.2 3.8 %collective-permute-start.5 = (bf16[4,64,384]{2,1,0:T(8,128)(2,1)S(1)}, bf16[4,64,384]{2,1,0:T(8,128)(2,1)S(1)}, u32[]{:S(2)}, u32[]{:S(2)}) collective-permute-start(bf16[4,64,384]{2,1,0:T(8,128)(2,1)S(1)} %get-tuple-element.29), channel_id=1, source_target_pairs={{0,13},{1,12},{4,9},{5,8},{8,5},{9,4},{12,1},{13,0},{2,15},{3,14},... | collective-permute-start | bytes 589832 | tf_op jit(solution)/shard_map/ppermute | solution.py:456
  13.0 3.8 %all-to-all-done = bf16[8,2,16,384]{3,2,1,0:T(8,128)(2,1)S(1)} async-done(((bf16[8,2,16,384]{3,2,1,0:T(8,128)(2,1)}), bf16[8,2,16,384]{3,2,1,0:T(8,128)(2,1)S(1)}, u32[]{:S(2)}, u32[]{:S(2)}) %all-to-all-start) | async-done | bytes 196640 | tf_op jit(solution)/shard_map/all_to_all | solution.py:434
  16.8 2.6 %collective-permute-start = (bf16[8,2,16,384]{3,2,1,0:T(8,128)(2,1)S(1)}, bf16[8,2,16,384]{3,2,1,0:T(8,128)(2,1)S(1)}, u32[]{:S(2)}, u32[]{:S(2)}) collective-permute-start(bf16[8,2,16,384]{3,2,1,0:T(8,128)(2,1)S(1)} %all-to-all-done), channel_id=1, source_target_pairs={{0,16},{16,0},{1,17},{17,1},{2,18},{18,2},{3,19},{19,3},{4,20},{20... | collective-permute-start | bytes 589832 | tf_op jit(solution)/shard_map/ppermute | solution.py:458
  20.2 0.8 %collective-permute-start.4 = (bf16[4,128,384]{2,1,0:T(8,128)(2,1)S(1)}, bf16[4,128,384]{2,1,0:T(8,128)(2,1)S(1)}, u32[]{:S(2)}, u32[]{:S(2)}) collective-permute-start(bf16[4,128,384]{2,1,0:T(8,128)(2,1)S(1)} %get-tuple-element.28), channel_id=1, source_target_pairs={{0,8},{2,7},{1,9},{3,6},{4,12},{6,3},{5,13},{7,2},{8,0},{10,15},{9... | collective-permute-start | bytes 1179656 | tf_op jit(solution)/shard_map/ppermute | solution.py:453
  21.0 4.3 %collective-permute-done.5.refs_6_ = bf16[4,64,384]{2,1,0:T(8,128)(2,1)S(1)} collective-permute-done((bf16[4,64,384]{2,1,0:T(8,128)(2,1)S(1)}, bf16[4,64,384]{2,1,0:T(8,128)(2,1)S(1)}, u32[]{:S(2)}, u32[]{:S(2)}) %collective-permute-start.5) | collective-permute-done | bytes 196640 | tf_op jit(solution)/shard_map/ppermute | solution.py:456
  25.3 1.8 %collective-permute-done = bf16[8,2,16,384]{3,2,1,0:T(8,128)(2,1)S(1)} collective-permute-done((bf16[8,2,16,384]{3,2,1,0:T(8,128)(2,1)S(1)}, bf16[8,2,16,384]{3,2,1,0:T(8,128)(2,1)S(1)}, u32[]{:S(2)}, u32[]{:S(2)}) %collective-permute-start) | collective-permute-done | bytes 196640 | tf_op jit(solution)/shard_map/ppermute | solution.py:458
  27.2 3.3 %hold.1.after_ref.refs_8_.held_ref = bf16[1536,2560]{1,0:T(8,128)(2,1)S(1)} custom-call(s32[1]{0:T(128)} %bitcast.device_ref, bf16[1536,5120]{1,0:T(8,128)(2,1)} %weight_ref.7, bf16[4,64,384]{2,1,0:T(8,128)(2,1)S(1)} %get-tuple-element.22.after_ref.refs_2_), custom_call_target="tpu_custom_call" | custom-call | bytes 7864320 | tf_op jit(solution)/shard_map/hold/pallas_call | solution.py:413
  30.5 4.1 %collective-permute-done.3.refs_4_ = bf16[4,128,384]{2,1,0:T(8,128)(2,1)S(1)} collective-permute-done((bf16[4,128,384]{2,1,0:T(8,128)(2,1)S(1)}, bf16[4,128,384]{2,1,0:T(8,128)(2,1)S(1)}, u32[]{:S(2)}, u32[]{:S(2)}) %collective-permute-start.3) | collective-permute-done | bytes 393248 | tf_op jit(solution)/shard_map/ppermute | solution.py:453
  34.7 1.5 %attend.3 = bf16[2,4,32,896]{3,2,1,0:T(8,128)(2,1)S(1)} custom-call(s32[1]{0:T(128)} %bitcast.device_ref, bf16[1536,2560]{1,0:T(8,128)(2,1)S(1)} %hold.1.after_ref.refs_8_.held_ref, bf16[1,8,2,16,384]{4,3,2,1,0:T(8,128)(2,1)S(1)} %collective-permute-done.6.refs_0_, bf16[1,8,2,16,384]{4,3,2,1,0:T(8,128)(2,1)S(1)} %collective-permute-done.7.refs_1_, ...), custom_call_target="tpu_custom_call" | custom-call | tf_op jit(solution)/shard_map/attend/pallas_call | solution.py:119
  36.2 2.4 %collective-permute-start.8 = (bf16[8,32,896]{2,1,0:T(8,128)(2,1)S(1)}, bf16[8,32,896]{2,1,0:T(8,128)(2,1)S(1)}, u32[]{:S(2)}, u32[]{:S(2)}) collective-permute-start(bf16[8,32,896]{2,1,0:T(8,128)(2,1)S(1)} %bitcast.9), channel_id=1, source_target_pairs={{0,2},{2,0},{1,3},{3,1},{4,6},{6,4},{5,7},{7,5},{8,10},{10,8},{9,1... | collective-permute-start | bytes 1376264 | tf_op jit(solution)/shard_map/ppermute | solution.py:472
  38.6 1.5 %attend.2 = bf16[2,4,32,896]{3,2,1,0:T(8,128)(2,1)S(1)} custom-call(s32[1]{0:T(128)} %bitcast.device_ref, bf16[1536,2560]{1,0:T(8,128)(2,1)S(1)} %hold.1.after_ref.refs_8_.held_ref, bf16[1,8,2,16,384]{4,3,2,1,0:T(8,128)(2,1)S(1)} %bitcast.8, bf16[1,8,2,16,384]{4,3,2,1,0:T(8,128)(2,1)S(1)} %bitcast.11, ...), custom_call_target="tpu_custom_call" | custom-call | tf_op jit(solution)/shard_map/attend/pallas_call | solution.py:119
  40.8 1.8 %collective-permute-start.12 = (bf16[32,896]{1,0:T(8,128)(2,1)S(1)}, bf16[32,896]{1,0:T(8,128)(2,1)S(1)}, u32[]{:S(2)}, u32[]{:S(2)}) collective-permute-start(bf16[32,896]{1,0:T(8,128)(2,1)S(1)} %get-tuple-element.34), channel_id=1, source_target_pairs={{0,16},{4,20},{8,24},{12,28},{16,0},{20,4},{24,8},{28,12},{1,17},{... | collective-permute-start | bytes 172040 | tf_op jit(solution)/shard_map/ppermute | solution.py:480
  42.6 1.2 %collective-permute-start.13 = (bf16[32,896]{1,0:T(8,128)(2,1)S(1)}, bf16[32,896]{1,0:T(8,128)(2,1)S(1)}, u32[]{:S(2)}, u32[]{:S(2)}) collective-permute-start(bf16[32,896]{1,0:T(8,128)(2,1)S(1)} %get-tuple-element.35), channel_id=1, source_target_pairs={{0,24},{4,28},{8,16},{12,20},{16,8},{20,12},{24,0},{28,4},{1,25},{... | collective-permute-start | bytes 172040 | tf_op jit(solution)/shard_map/ppermute | solution.py:480
  43.8 1.5 %collective-permute-start.14 = (bf16[32,896]{1,0:T(8,128)(2,1)S(1)}, bf16[32,896]{1,0:T(8,128)(2,1)S(1)}, u32[]{:S(2)}, u32[]{:S(2)}) collective-permute-start(bf16[32,896]{1,0:T(8,128)(2,1)S(1)} %get-tuple-element.36), channel_id=1, source_target_pairs={{0,20},{4,16},{8,28},{12,24},{16,4},{20,0},{24,12},{28,8},{1,21},{... | collective-permute-start | bytes 172040 | tf_op jit(solution)/shard_map/ppermute | solution.py:480
  45.3 2.4 %collective-permute-start.15 = (bf16[32,896]{1,0:T(8,128)(2,1)S(1)}, bf16[32,896]{1,0:T(8,128)(2,1)S(1)}, u32[]{:S(2)}, u32[]{:S(2)}) collective-permute-start(bf16[32,896]{1,0:T(8,128)(2,1)S(1)} %get-tuple-element.37), channel_id=1, source_target_pairs={{0,28},{4,24},{8,20},{12,16},{16,12},{20,8},{24,4},{28,0},{1,29},{... | collective-permute-start | bytes 172040 | tf_op jit(solution)/shard_map/ppermute | solution.py:480
  49.0 1.2 %collective-permute-done.12.refs_4_ = bf16[32,896]{1,0:T(8,128)(2,1)S(1)} collective-permute-done((bf16[32,896]{1,0:T(8,128)(2,1)S(1)}, bf16[32,896]{1,0:T(8,128)(2,1)S(1)}, u32[]{:S(2)}, u32[]{:S(2)}) %collective-permute-start.12) | collective-permute-done | bytes 57376 | tf_op jit(solution)/shard_map/ppermute | solution.py:480
  50.2 2.8 %collective-permute-start.11 = (bf16[32,896]{1,0:T(8,128)(2,1)S(1)}, bf16[32,896]{1,0:T(8,128)(2,1)S(1)}, u32[]{:S(2)}, u32[]{:S(2)}) collective-permute-start(bf16[32,896]{1,0:T(8,128)(2,1)S(1)} %get-tuple-element.32), channel_id=1, source_target_pairs={{0,12},{4,8},{8,4},{12,0},{16,28},{20,24},{24,20},{28,16},{1,13},{... | collective-permute-start | bytes 172040 | tf_op jit(solution)/shard_map/ppermute | solution.py:480
  55.4 1.2 %project.3 = (bf16[64,1280]{1,0:T(8,128)(2,1)S(1)}, bf16[64,1536]{1,0:T(8,128)(2,1)S(1)}) custom-call(s32[1]{0:T(128)} %bitcast.device_ref, bf16[1536,5120]{1,0:T(8,128)(2,1)} %weight_ref.7, bf16[32,896]{1,0:T(8,128)(2,1)S(1)} %collective-permute-done.9.refs_0_, bf16[32,896]{1,0:T(8,128)(2,1)S(1)} %collective-permute-done.10.refs_1_, ...), custom_call_target="tpu_custom_call" | custom-call | flops 251658240 | bytes 3932160 | tf_op jit(solution)/shard_map/project/pallas_call | solution.py:297
  56.6 1.3 %collective-permute-start.17 = (bf16[64,1280]{1,0:T(8,128)(2,1)S(1)}, bf16[64,1280]{1,0:T(8,128)(2,1)S(1)}, u32[]{:S(2)}, u32[]{:S(2)}) collective-permute-start(bf16[64,1280]{1,0:T(8,128)(2,1)S(1)} %get-tuple-element.39), channel_id=1, source_target_pairs={{0,1},{1,0},{2,3},{3,2},{4,5},{5,4},{6,7},{7,6},{8,9},{9,8},{10,11... | collective-permute-start | bytes 491528 | tf_op jit(solution)/shard_map/ppermute | solution.py:491
  58.8 0.8 %collective-permute-start.16 = (bf16[64,1280]{1,0:T(8,128)(2,1)S(1)}, bf16[64,1280]{1,0:T(8,128)(2,1)S(1)}, u32[]{:S(2)}, u32[]{:S(2)}) collective-permute-start(bf16[64,1280]{1,0:T(8,128)(2,1)S(1)} %project.5), channel_id=1, source_target_pairs={{0,1},{1,0},{2,3},{3,2},{4,5},{5,4},{6,7},{7,6},{8,9},{9,8},{10,11... | collective-permute-start | bytes 491528 | tf_op jit(solution)/shard_map/ppermute | solution.py:495
  59.6 3.8 %project.4.own_ref = f32[64,2560]{1,0:T(8,128)S(1)} custom-call(s32[1]{0:T(128)} %bitcast.device_ref, bf16[1536,5120]{1,0:T(8,128)(2,1)} %weight_ref.7, bf16[64,1536]{1,0:T(8,128)(2,1)S(1)} %get-tuple-element.38.both_ref), custom_call_target="tpu_custom_call" | custom-call | flops 503316480 | bytes 7864320 | tf_op jit(solution)/shard_map/project/pallas_call | solution.py:297
  64.4 1.1 %collective-permute-done.16.received_ref = bf16[64,1280]{1,0:T(8,128)(2,1)S(1)} collective-permute-done((bf16[64,1280]{1,0:T(8,128)(2,1)S(1)}, bf16[64,1280]{1,0:T(8,128)(2,1)S(1)}, u32[]{:S(2)}, u32[]{:S(2)}) %collective-permute-start.16) | collective-permute-done | bytes 163872 | tf_op jit(solution)/shard_map/ppermute | solution.py:495
  (26 shorter events, 8.3 us)
Async XLA Ops:
  2.9 16.5 %collective-permute-start.1 = (bf16[3,4,64,384]{3,2,1,0:T(8,128)(2,1)S(1)}, bf16[3,4,64,384]{3,2,1,0:T(8,128)(2,1)S(1)}, u32[]{:S(2)}, u32[]{:S(2)}) collective-permute-start(bf16[3,4,64,384]{3,2,1,0:T(8,128)(2,1)S(1)} %get-tuple-element.25), channel_id=1, source_target_pairs={{0,2},{2,0},{1,3},{3,1},{4,6},{6,4},{5,7},{7,5},{8,10},{10,8},{9,1... | collective-permute-start | bytes 1769480 | tf_op jit(solution)/shard_map/ppermute | solution.py:450
  3.4 13.4 %all-to-all-start = ((bf16[8,2,16,384]{3,2,1,0:T(8,128)(2,1)}), bf16[8,2,16,384]{3,2,1,0:T(8,128)(2,1)S(1)}, u32[]{:S(2)}, u32[]{:S(2)}) async-start(bf16[8,2,16,384]{3,2,1,0:T(8,128)(2,1)} %get-tuple-element.23), calls=%async_computation | async-start | bytes 393216 | tf_op jit(solution)/shard_map/all_to_all | solution.py:434
  9.2 16.2 %collective-permute-start.5 = (bf16[4,64,384]{2,1,0:T(8,128)(2,1)S(1)}, bf16[4,64,384]{2,1,0:T(8,128)(2,1)S(1)}, u32[]{:S(2)}, u32[]{:S(2)}) collective-permute-start(bf16[4,64,384]{2,1,0:T(8,128)(2,1)S(1)} %get-tuple-element.29), channel_id=1, source_target_pairs={{0,13},{1,12},{4,9},{5,8},{8,5},{9,4},{12,1},{13,0},{2,15},{3,14},... | collective-permute-start | bytes 589832 | tf_op jit(solution)/shard_map/ppermute | solution.py:456
  16.8 10.4 %collective-permute-start = (bf16[8,2,16,384]{3,2,1,0:T(8,128)(2,1)S(1)}, bf16[8,2,16,384]{3,2,1,0:T(8,128)(2,1)S(1)}, u32[]{:S(2)}, u32[]{:S(2)}) collective-permute-start(bf16[8,2,16,384]{3,2,1,0:T(8,128)(2,1)S(1)} %all-to-all-done), channel_id=1, source_target_pairs={{0,16},{16,0},{1,17},{17,1},{2,18},{18,2},{3,19},{19,3},{4,20},{20... | collective-permute-start | bytes 589832 | tf_op jit(solution)/shard_map/ppermute | solution.py:458
  19.5 11.0 %collective-permute-start.2 = (bf16[4,128,384]{2,1,0:T(8,128)(2,1)S(1)}, bf16[4,128,384]{2,1,0:T(8,128)(2,1)S(1)}, u32[]{:S(2)}, u32[]{:S(2)}) collective-permute-start(bf16[4,128,384]{2,1,0:T(8,128)(2,1)S(1)} %get-tuple-element.26), channel_id=1, source_target_pairs={{0,4},{2,11},{1,5},{3,10},{4,0},{6,15},{5,1},{7,14},{8,12},{10,3},... | collective-permute-start | bytes 1179656 | tf_op jit(solution)/shard_map/ppermute | solution.py:453
  19.6 15.1 %collective-permute-start.3 = (bf16[4,128,384]{2,1,0:T(8,128)(2,1)S(1)}, bf16[4,128,384]{2,1,0:T(8,128)(2,1)S(1)}, u32[]{:S(2)}, u32[]{:S(2)}) collective-permute-start(bf16[4,128,384]{2,1,0:T(8,128)(2,1)S(1)} %get-tuple-element.27), channel_id=1, source_target_pairs={{0,1},{2,14},{1,0},{3,15},{4,5},{6,10},{5,4},{7,11},{8,9},{10,6},{... | collective-permute-start | bytes 1179656 | tf_op jit(solution)/shard_map/ppermute | solution.py:453
  20.2 14.5 %collective-permute-start.4 = (bf16[4,128,384]{2,1,0:T(8,128)(2,1)S(1)}, bf16[4,128,384]{2,1,0:T(8,128)(2,1)S(1)}, u32[]{:S(2)}, u32[]{:S(2)}) collective-permute-start(bf16[4,128,384]{2,1,0:T(8,128)(2,1)S(1)} %get-tuple-element.28), channel_id=1, source_target_pairs={{0,8},{2,7},{1,9},{3,6},{4,12},{6,3},{5,13},{7,2},{8,0},{10,15},{9... | collective-permute-start | bytes 1179656 | tf_op jit(solution)/shard_map/ppermute | solution.py:453
  25.3 5.2 %collective-permute-start.6 = (bf16[1,8,2,16,384]{4,3,2,1,0:T(8,128)(2,1)S(1)}, bf16[1,8,2,16,384]{4,3,2,1,0:T(8,128)(2,1)S(1)}, u32[]{:S(2)}, u32[]{:S(2)}) collective-permute-start(bf16[1,8,2,16,384]{4,3,2,1,0:T(8,128)(2,1)S(1)} %bitcast.7), channel_id=1, source_target_pairs={{0,2},{2,0},{1,3},{3,1},{4,6},{6,4},{5,7},{7,5},{8,10},{10,8},{9,1... | collective-permute-start | bytes 589832 | tf_op jit(solution)/shard_map/ppermute | solution.py:461
  27.2 3.3 %collective-permute-start.7 = (bf16[1,8,2,16,384]{4,3,2,1,0:T(8,128)(2,1)S(1)}, bf16[1,8,2,16,384]{4,3,2,1,0:T(8,128)(2,1)S(1)}, u32[]{:S(2)}, u32[]{:S(2)}) collective-permute-start(bf16[1,8,2,16,384]{4,3,2,1,0:T(8,128)(2,1)S(1)} %bitcast.10), channel_id=1, source_target_pairs={{0,2},{2,0},{1,3},{3,1},{4,6},{6,4},{5,7},{7,5},{8,10},{10,8},{9,1... | collective-permute-start | bytes 589832 | tf_op jit(solution)/shard_map/ppermute | solution.py:461
  36.2 3.9 %collective-permute-start.8 = (bf16[8,32,896]{2,1,0:T(8,128)(2,1)S(1)}, bf16[8,32,896]{2,1,0:T(8,128)(2,1)S(1)}, u32[]{:S(2)}, u32[]{:S(2)}) collective-permute-start(bf16[8,32,896]{2,1,0:T(8,128)(2,1)S(1)} %bitcast.9), channel_id=1, source_target_pairs={{0,2},{2,0},{1,3},{3,1},{4,6},{6,4},{5,7},{7,5},{8,10},{10,8},{9,1... | collective-permute-start | bytes 1376264 | tf_op jit(solution)/shard_map/ppermute | solution.py:472
  40.8 9.4 %collective-permute-start.12 = (bf16[32,896]{1,0:T(8,128)(2,1)S(1)}, bf16[32,896]{1,0:T(8,128)(2,1)S(1)}, u32[]{:S(2)}, u32[]{:S(2)}) collective-permute-start(bf16[32,896]{1,0:T(8,128)(2,1)S(1)} %get-tuple-element.34), channel_id=1, source_target_pairs={{0,16},{4,20},{8,24},{12,28},{16,0},{20,4},{24,8},{28,12},{1,17},{... | collective-permute-start | bytes 172040 | tf_op jit(solution)/shard_map/ppermute | solution.py:480
  42.6 7.7 %collective-permute-start.13 = (bf16[32,896]{1,0:T(8,128)(2,1)S(1)}, bf16[32,896]{1,0:T(8,128)(2,1)S(1)}, u32[]{:S(2)}, u32[]{:S(2)}) collective-permute-start(bf16[32,896]{1,0:T(8,128)(2,1)S(1)} %get-tuple-element.35), channel_id=1, source_target_pairs={{0,24},{4,28},{8,16},{12,20},{16,8},{20,12},{24,0},{28,4},{1,25},{... | collective-permute-start | bytes 172040 | tf_op jit(solution)/shard_map/ppermute | solution.py:480
  43.8 9.9 %collective-permute-start.14 = (bf16[32,896]{1,0:T(8,128)(2,1)S(1)}, bf16[32,896]{1,0:T(8,128)(2,1)S(1)}, u32[]{:S(2)}, u32[]{:S(2)}) collective-permute-start(bf16[32,896]{1,0:T(8,128)(2,1)S(1)} %get-tuple-element.36), channel_id=1, source_target_pairs={{0,20},{4,16},{8,28},{12,24},{16,4},{20,0},{24,12},{28,8},{1,21},{... | collective-permute-start | bytes 172040 | tf_op jit(solution)/shard_map/ppermute | solution.py:480
  45.3 8.5 %collective-permute-start.15 = (bf16[32,896]{1,0:T(8,128)(2,1)S(1)}, bf16[32,896]{1,0:T(8,128)(2,1)S(1)}, u32[]{:S(2)}, u32[]{:S(2)}) collective-permute-start(bf16[32,896]{1,0:T(8,128)(2,1)S(1)} %get-tuple-element.37), channel_id=1, source_target_pairs={{0,28},{4,24},{8,20},{12,16},{16,12},{20,8},{24,4},{28,0},{1,29},{... | collective-permute-start | bytes 172040 | tf_op jit(solution)/shard_map/ppermute | solution.py:480
  48.3 6.1 %collective-permute-start.9 = (bf16[32,896]{1,0:T(8,128)(2,1)S(1)}, bf16[32,896]{1,0:T(8,128)(2,1)S(1)}, u32[]{:S(2)}, u32[]{:S(2)}) collective-permute-start(bf16[32,896]{1,0:T(8,128)(2,1)S(1)} %get-tuple-element.30), channel_id=1, source_target_pairs={{0,4},{4,0},{8,12},{12,8},{16,20},{20,16},{24,28},{28,24},{1,5},{5... | collective-permute-start | bytes 172040 | tf_op jit(solution)/shard_map/ppermute | solution.py:480
  50.2 4.4 %collective-permute-start.10 = (bf16[32,896]{1,0:T(8,128)(2,1)S(1)}, bf16[32,896]{1,0:T(8,128)(2,1)S(1)}, u32[]{:S(2)}, u32[]{:S(2)}) collective-permute-start(bf16[32,896]{1,0:T(8,128)(2,1)S(1)} %get-tuple-element.31), channel_id=1, source_target_pairs={{0,8},{4,12},{8,0},{12,4},{16,24},{20,28},{24,16},{28,20},{1,9},{5... | collective-permute-start | bytes 172040 | tf_op jit(solution)/shard_map/ppermute | solution.py:480
  50.2 5.2 %collective-permute-start.11 = (bf16[32,896]{1,0:T(8,128)(2,1)S(1)}, bf16[32,896]{1,0:T(8,128)(2,1)S(1)}, u32[]{:S(2)}, u32[]{:S(2)}) collective-permute-start(bf16[32,896]{1,0:T(8,128)(2,1)S(1)} %get-tuple-element.32), channel_id=1, source_target_pairs={{0,12},{4,8},{8,4},{12,0},{16,28},{20,24},{24,20},{28,16},{1,13},{... | collective-permute-start | bytes 172040 | tf_op jit(solution)/shard_map/ppermute | solution.py:480
  56.6 7.1 %collective-permute-start.17 = (bf16[64,1280]{1,0:T(8,128)(2,1)S(1)}, bf16[64,1280]{1,0:T(8,128)(2,1)S(1)}, u32[]{:S(2)}, u32[]{:S(2)}) collective-permute-start(bf16[64,1280]{1,0:T(8,128)(2,1)S(1)} %get-tuple-element.39), channel_id=1, source_target_pairs={{0,1},{1,0},{2,3},{3,2},{4,5},{5,4},{6,7},{7,6},{8,9},{9,8},{10,11... | collective-permute-start | bytes 491528 | tf_op jit(solution)/shard_map/ppermute | solution.py:491
  58.8 6.7 %collective-permute-start.16 = (bf16[64,1280]{1,0:T(8,128)(2,1)S(1)}, bf16[64,1280]{1,0:T(8,128)(2,1)S(1)}, u32[]{:S(2)}, u32[]{:S(2)}) collective-permute-start(bf16[64,1280]{1,0:T(8,128)(2,1)S(1)} %project.5), channel_id=1, source_target_pairs={{0,1},{1,0},{2,3},{3,2},{4,5},{5,4},{6,7},{7,6},{8,9},{9,8},{10,11... | collective-permute-start | bytes 491528 | tf_op jit(solution)/shard_map/ppermute | solution.py:495

commit v9 on v8

--- a/solution.py
+++ b/solution.py
@@ -155,11 +155,10 @@
     return share, shift, top + jnp.log(total), mean_slope
 
 
-def merge_head(parts, share, shift, h):
+def merge_head(owns, tans, share, shift, h):
     value = tangent = 0.0
-    for part, e, s in zip(parts, share, shift):
-        own = part[:, 2 * h * DH : (2 * h + 1) * DH].astype(jnp.float32)
-        own_tan = part[:, (2 * h + 1) * DH : (2 * h + 2) * DH].astype(jnp.float32)
+    for own, own_tan, e, s in zip(owns, tans, share, shift):
+        own, own_tan = own.astype(jnp.float32), own_tan.astype(jnp.float32)
         e, s = e[:, h : h + 1], s[:, h : h + 1]
         value += e * own
         tangent += e * own_tan + s * own
@@ -167,14 +166,20 @@
 
 
 def merge(my_g, parts_refs, both_ref, heads, g_count, turns):
-    rows = parts_refs[0].shape[0]
+    rows = both_ref.shape[0] // 2
     tail = slice(2 * heads * DH, (2 * heads + 1) * DH)
     for d in range(g_count):
         g = my_g ^ d
-        parts = [parts_refs[turns.index(j)][...] for j in range(d, len(turns), g_count)]
-        share, shift, _, _ = merge_stats([part[:, tail] for part in parts], heads)
+        parts = [parts_refs[turns.index(j)] for j in range(d, len(turns), g_count)]
+        tails = [part[2 * heads * rows :].astype(jnp.float32) for part in parts]
+        tails = [jnp.concatenate([tail, pltpu.roll(tail, DH // 2, 1)]) for tail in tails]
+        share, shift, _, _ = merge_stats(tails, heads)
         for h in range(heads):
-            value, tangent = merge_head(parts, share, shift, h)
+            owns, tans = (
+                [part[i * rows : (i + 1) * rows] for part in parts]
+                for i in (2 * h, 2 * h + 1)
+            )
+            value, tangent = merge_head(owns, tans, share, shift, h)
             columns = pl.ds(pl.multiple_of((g * heads + h) * DH, DH), DH)
             both_ref[:rows, columns] = value.astype(jnp.bfloat16)
             both_ref[rows:, columns] = tangent.astype(jnp.bfloat16)
@@ -185,19 +190,28 @@
     tail = slice(2 * heads * DH, (2 * heads + 1) * DH)
     for d, out_ref in zip(turns, out_refs):
         parts = [ref[(k * g_count + g) ^ d] for ref in (home_ref, away_ref)]
+        rows = parts[0].shape[0]
         share, shift, lse, slope = merge_stats([part[:, tail] for part in parts], heads)
         for h in range(heads):
-            both = jnp.concatenate(merge_head(parts, share, shift, h), axis=1)
-            out_ref[:, 2 * h * DH : 2 * (h + 1) * DH] = both.astype(jnp.bfloat16)
-        out_ref[:, tail] = packed_stats(lse, slope, heads)
+            owns, tans = (
+                [part[:, i * DH : (i + 1) * DH] for part in parts] for i in (2 * h, 2 * h + 1)
+            )
+            for i, x in enumerate(merge_head(owns, tans, share, shift, h)):
+                first = (2 * h + i) * rows
+                out_ref[first : first + rows] = x.astype(jnp.bfloat16)
+        packed = packed_stats(lse, slope, heads).astype(jnp.float32)
+        packed = packed[: rows // 2] + pltpu.roll(packed[rows // 2 :], DH // 2, 1)
+        out_ref[2 * heads * rows :] = packed.astype(jnp.bfloat16)
 
 
 def merge_pair(device, home, away, heads, turns, g_count, head_axis):
     whole = pl.BlockSpec(memory_space=pltpu.VMEM)
     count = len(turns)
+    rows = home.shape[1]
+    size = 2 * heads * rows + rows // 2
     return pl.pallas_call(
         functools.partial(pair_kernel, heads, turns, g_count, head_axis),
-        out_shape=[jax.ShapeDtypeStruct(home.shape[1:], home.dtype)] * count,
+        out_shape=[jax.ShapeDtypeStruct((size, DH), home.dtype)] * count,
         in_specs=[pl.BlockSpec(memory_space=pltpu.SMEM), whole, whole],
         out_specs=[whole] * count,
         compiler_params=pltpu.CompilerParams(vmem_limit_bytes=ATTEND_VMEM),

time: 66.4 us -> 65.8 us (level)
  waiting for transfers between devices: 19.1 us -> 18.2 us
  transfers between devices with their start and end apart: 19 -> 19, of which waited for: 11 -> 8; matrix products, arithmetic and copies ran while one was open for 0% -> 0% of each run, Pallas kernels for 17% -> 17%
where the time goes in v9:
time: 65.8 us; the launch traced here: 65.5 us
  starting transfers between devices  29.1 us (44%)
  waiting for transfers between devices  18.2 us (28%)
  Pallas kernels  17.5 us (27%)
  between operations  0.76 us (1%)
    ppermute x7, starting transfers between devices, local(): lax.ppermute(part, ('k', 'g'), [(i, i ^ d) for i in range(count)])  10.4 us
    pallas_call x3, Pallas kernels, project(): pl.pallas_call(kernel, out_shape=outs, in_specs=[scalar, pl.BlockSpec(mem...  5.89 us
    all_to_all x1, starting transfers between devices, within_plane(): lax.all_to_all(x, plane_axes, split_axis=0, concat_axis=0, tiled=True)  5.76 us
    ppermute x1, waiting for transfers between devices, local(): lax.ppermute(far, ('g', 'head'), [(i, i ^ FAR) for i in range(group)])  4.3 us
    ppermute x3, waiting for transfers between devices, local(): lax.ppermute(piece, ('g', 'core', 'head'), across_chips(turn, g_count, he...  4.14 us
    ppermute x1, starting transfers between devices, local(): lax.ppermute(far, ('g', 'head'), [(i, i ^ FAR) for i in range(group)])  3.82 us
    all_to_all x1, waiting for transfers between devices, within_plane(): lax.all_to_all(x, plane_axes, split_axis=0, concat_axis=0, tiled=True)  3.82 us
    pallas_call x1, Pallas kernels, hold(): pl.pallas_call(functools.partial(hold_kernel, head_axis), out_shape=jax.S...  3.32 us
  transfers between devices with their start and end apart: 19, of which 8 were waited for; matrix products, arithmetic and copies ran while one was open for 0% of the time, Pallas kernels for 17%

profile of v9, /device:TPU:0, one launch (start us, length us, event | category | flops | bytes accessed | tf_op | source)
XLA Modules:
  0.0 65.5 jit_solution(7050713291294587968)
XLA Ops:
  0.6 2.2 %pack.1 = (bf16[8,2,16,384]{3,2,1,0:T(8,128)(2,1)}, bf16[4,64,384]{2,1,0:T(8,128)(2,1)S(1)}, bf16[4,64,384]{2,1,0:T(8,128)(2,1)S(1)}, bf16[3,4,64,384]{3,2,1,0:T(8,128)(2,1)S(1)}, bf16[3,4,64,384]{3,2,1,0:T(8,128)(2,1)S(1)}) custom-call(s32[1]{0:T(128)} %bitcast.device_ref, bf16[16,3072]{1,0:T(8,128)(2,1)} %refs_0_.1, bf16[16,3072]{1,0:T(8,128)(2,1)} %refs_1_.1, ...), custom_call_target="tpu_custom_call" | custom-call | tf_op jit(solution)/shard_map/pack/pallas_call | solution.py:361
  3.4 5.8 %all-to-all-start = ((bf16[8,2,16,384]{3,2,1,0:T(8,128)(2,1)}), bf16[8,2,16,384]{3,2,1,0:T(8,128)(2,1)S(1)}, u32[]{:S(2)}, u32[]{:S(2)}) async-start(bf16[8,2,16,384]{3,2,1,0:T(8,128)(2,1)} %get-tuple-element.23), calls=%async_computation | async-start | bytes 393216 | tf_op jit(solution)/shard_map/all_to_all | solution.py:448
  9.2 3.8 %collective-permute-start.5 = (bf16[4,64,384]{2,1,0:T(8,128)(2,1)S(1)}, bf16[4,64,384]{2,1,0:T(8,128)(2,1)S(1)}, u32[]{:S(2)}, u32[]{:S(2)}) collective-permute-start(bf16[4,64,384]{2,1,0:T(8,128)(2,1)S(1)} %get-tuple-element.29), channel_id=1, source_target_pairs={{0,13},{1,12},{4,9},{5,8},{8,5},{9,4},{12,1},{13,0},{2,15},{3,14},... | collective-permute-start | bytes 589832 | tf_op jit(solution)/shard_map/ppermute | solution.py:470
  13.0 3.8 %all-to-all-done = bf16[8,2,16,384]{3,2,1,0:T(8,128)(2,1)S(1)} async-done(((bf16[8,2,16,384]{3,2,1,0:T(8,128)(2,1)}), bf16[8,2,16,384]{3,2,1,0:T(8,128)(2,1)S(1)}, u32[]{:S(2)}, u32[]{:S(2)}) %all-to-all-start) | async-done | bytes 196640 | tf_op jit(solution)/shard_map/all_to_all | solution.py:448
  16.8 2.6 %collective-permute-start = (bf16[8,2,16,384]{3,2,1,0:T(8,128)(2,1)S(1)}, bf16[8,2,16,384]{3,2,1,0:T(8,128)(2,1)S(1)}, u32[]{:S(2)}, u32[]{:S(2)}) collective-permute-start(bf16[8,2,16,384]{3,2,1,0:T(8,128)(2,1)S(1)} %all-to-all-done), channel_id=1, source_target_pairs={{0,16},{16,0},{1,17},{17,1},{2,18},{18,2},{3,19},{19,3},{4,20},{20... | collective-permute-start | bytes 589832 | tf_op jit(solution)/shard_map/ppermute | solution.py:472
  21.0 4.3 %collective-permute-done.5.refs_6_ = bf16[4,64,384]{2,1,0:T(8,128)(2,1)S(1)} collective-permute-done((bf16[4,64,384]{2,1,0:T(8,128)(2,1)S(1)}, bf16[4,64,384]{2,1,0:T(8,128)(2,1)S(1)}, u32[]{:S(2)}, u32[]{:S(2)}) %collective-permute-start.5) | collective-permute-done | bytes 196640 | tf_op jit(solution)/shard_map/ppermute | solution.py:470
  25.3 1.8 %collective-permute-done = bf16[8,2,16,384]{3,2,1,0:T(8,128)(2,1)S(1)} collective-permute-done((bf16[8,2,16,384]{3,2,1,0:T(8,128)(2,1)S(1)}, bf16[8,2,16,384]{3,2,1,0:T(8,128)(2,1)S(1)}, u32[]{:S(2)}, u32[]{:S(2)}) %collective-permute-start) | collective-permute-done | bytes 196640 | tf_op jit(solution)/shard_map/ppermute | solution.py:472
  27.2 3.3 %hold.1.after_ref.refs_8_.held_ref = bf16[1536,2560]{1,0:T(8,128)(2,1)S(1)} custom-call(s32[1]{0:T(128)} %bitcast.device_ref, bf16[1536,5120]{1,0:T(8,128)(2,1)} %weight_ref.7, bf16[4,64,384]{2,1,0:T(8,128)(2,1)S(1)} %get-tuple-element.22.after_ref.refs_2_), custom_call_target="tpu_custom_call" | custom-call | bytes 7864320 | tf_op jit(solution)/shard_map/hold/pallas_call | solution.py:427
  30.5 4.1 %collective-permute-done.3.refs_4_ = bf16[4,128,384]{2,1,0:T(8,128)(2,1)S(1)} collective-permute-done((bf16[4,128,384]{2,1,0:T(8,128)(2,1)S(1)}, bf16[4,128,384]{2,1,0:T(8,128)(2,1)S(1)}, u32[]{:S(2)}, u32[]{:S(2)}) %collective-permute-start.3) | collective-permute-done | bytes 393248 | tf_op jit(solution)/shard_map/ppermute | solution.py:467
  34.7 1.5 %attend.3 = bf16[2,4,32,896]{3,2,1,0:T(8,128)(2,1)S(1)} custom-call(s32[1]{0:T(128)} %bitcast.device_ref, bf16[1536,2560]{1,0:T(8,128)(2,1)S(1)} %hold.1.after_ref.refs_8_.held_ref, bf16[1,8,2,16,384]{4,3,2,1,0:T(8,128)(2,1)S(1)} %collective-permute-done.6.refs_0_, bf16[1,8,2,16,384]{4,3,2,1,0:T(8,128)(2,1)S(1)} %collective-permute-done.7.refs_1_, ...), custom_call_target="tpu_custom_call" | custom-call | tf_op jit(solution)/shard_map/attend/pallas_call | solution.py:119
  36.2 2.4 %collective-permute-start.8 = (bf16[8,32,896]{2,1,0:T(8,128)(2,1)S(1)}, bf16[8,32,896]{2,1,0:T(8,128)(2,1)S(1)}, u32[]{:S(2)}, u32[]{:S(2)}) collective-permute-start(bf16[8,32,896]{2,1,0:T(8,128)(2,1)S(1)} %bitcast.9), channel_id=1, source_target_pairs={{0,2},{2,0},{1,3},{3,1},{4,6},{6,4},{5,7},{7,5},{8,10},{10,8},{9,1... | collective-permute-start | bytes 1376264 | tf_op jit(solution)/shard_map/ppermute | solution.py:486
  38.6 1.5 %attend.2 = bf16[2,4,32,896]{3,2,1,0:T(8,128)(2,1)S(1)} custom-call(s32[1]{0:T(128)} %bitcast.device_ref, bf16[1536,2560]{1,0:T(8,128)(2,1)S(1)} %hold.1.after_ref.refs_8_.held_ref, bf16[1,8,2,16,384]{4,3,2,1,0:T(8,128)(2,1)S(1)} %bitcast.8, bf16[1,8,2,16,384]{4,3,2,1,0:T(8,128)(2,1)S(1)} %bitcast.11, ...), custom_call_target="tpu_custom_call" | custom-call | tf_op jit(solution)/shard_map/attend/pallas_call | solution.py:119
  40.9 1.8 %collective-permute-start.12 = (bf16[208,128]{1,0:T(8,128)(2,1)S(1)}, bf16[208,128]{1,0:T(8,128)(2,1)S(1)}, u32[]{:S(2)}, u32[]{:S(2)}) collective-permute-start(bf16[208,128]{1,0:T(8,128)(2,1)S(1)} %get-tuple-element.34), channel_id=1, source_target_pairs={{0,16},{4,20},{8,24},{12,28},{16,0},{20,4},{24,8},{28,12},{1,17},{... | collective-permute-start | bytes 159752 | tf_op jit(solution)/shard_map/ppermute | solution.py:494
  42.6 1.2 %collective-permute-start.13 = (bf16[208,128]{1,0:T(8,128)(2,1)S(1)}, bf16[208,128]{1,0:T(8,128)(2,1)S(1)}, u32[]{:S(2)}, u32[]{:S(2)}) collective-permute-start(bf16[208,128]{1,0:T(8,128)(2,1)S(1)} %get-tuple-element.35), channel_id=1, source_target_pairs={{0,24},{4,28},{8,16},{12,20},{16,8},{20,12},{24,0},{28,4},{1,25},{... | collective-permute-start | bytes 159752 | tf_op jit(solution)/shard_map/ppermute | solution.py:494
  43.8 1.5 %collective-permute-start.14 = (bf16[208,128]{1,0:T(8,128)(2,1)S(1)}, bf16[208,128]{1,0:T(8,128)(2,1)S(1)}, u32[]{:S(2)}, u32[]{:S(2)}) collective-permute-start(bf16[208,128]{1,0:T(8,128)(2,1)S(1)} %get-tuple-element.36), channel_id=1, source_target_pairs={{0,20},{4,16},{8,28},{12,24},{16,4},{20,0},{24,12},{28,8},{1,21},{... | collective-permute-start | bytes 159752 | tf_op jit(solution)/shard_map/ppermute | solution.py:494
  45.3 2.4 %collective-permute-start.15 = (bf16[208,128]{1,0:T(8,128)(2,1)S(1)}, bf16[208,128]{1,0:T(8,128)(2,1)S(1)}, u32[]{:S(2)}, u32[]{:S(2)}) collective-permute-start(bf16[208,128]{1,0:T(8,128)(2,1)S(1)} %get-tuple-element.37), channel_id=1, source_target_pairs={{0,28},{4,24},{8,20},{12,16},{16,12},{20,8},{24,4},{28,0},{1,29},{... | collective-permute-start | bytes 159752 | tf_op jit(solution)/shard_map/ppermute | solution.py:494
  50.1 1.9 %collective-permute-start.11 = (bf16[208,128]{1,0:T(8,128)(2,1)S(1)}, bf16[208,128]{1,0:T(8,128)(2,1)S(1)}, u32[]{:S(2)}, u32[]{:S(2)}) collective-permute-start(bf16[208,128]{1,0:T(8,128)(2,1)S(1)} %get-tuple-element.32), channel_id=1, source_target_pairs={{0,12},{4,8},{8,4},{12,0},{16,28},{20,24},{24,20},{28,16},{1,13},{... | collective-permute-start | bytes 159752 | tf_op jit(solution)/shard_map/ppermute | solution.py:494
  52.0 1.1 %collective-permute-done.14.refs_6_ = bf16[208,128]{1,0:T(8,128)(2,1)S(1)} collective-permute-done((bf16[208,128]{1,0:T(8,128)(2,1)S(1)}, bf16[208,128]{1,0:T(8,128)(2,1)S(1)}, u32[]{:S(2)}, u32[]{:S(2)}) %collective-permute-start.14) | collective-permute-done | bytes 53280 | tf_op jit(solution)/shard_map/ppermute | solution.py:494
  54.0 1.1 %collective-permute-done.11.refs_2_ = bf16[208,128]{1,0:T(8,128)(2,1)S(1)} collective-permute-done((bf16[208,128]{1,0:T(8,128)(2,1)S(1)}, bf16[208,128]{1,0:T(8,128)(2,1)S(1)}, u32[]{:S(2)}, u32[]{:S(2)}) %collective-permute-start.11) | collective-permute-done | bytes 53280 | tf_op jit(solution)/shard_map/ppermute | solution.py:494
  55.1 1.2 %project.3 = (bf16[64,1280]{1,0:T(8,128)(2,1)S(1)}, bf16[64,1536]{1,0:T(8,128)(2,1)S(1)}) custom-call(s32[1]{0:T(128)} %bitcast.device_ref, bf16[1536,5120]{1,0:T(8,128)(2,1)} %weight_ref.7, bf16[208,128]{1,0:T(8,128)(2,1)S(1)} %collective-permute-done.9.refs_0_, bf16[208,128]{1,0:T(8,128)(2,1)S(1)} %collective-permute-done.10.refs_1_, ...), custom_call_target="tpu_custom_call" | custom-call | flops 251658240 | bytes 3932160 | tf_op jit(solution)/shard_map/project/pallas_call | solution.py:311
  56.4 1.0 %collective-permute-start.17 = (bf16[64,1280]{1,0:T(8,128)(2,1)S(1)}, bf16[64,1280]{1,0:T(8,128)(2,1)S(1)}, u32[]{:S(2)}, u32[]{:S(2)}) collective-permute-start(bf16[64,1280]{1,0:T(8,128)(2,1)S(1)} %get-tuple-element.39), channel_id=1, source_target_pairs={{0,1},{1,0},{2,3},{3,2},{4,5},{5,4},{6,7},{7,6},{8,9},{9,8},{10,11... | collective-permute-start | bytes 491528 | tf_op jit(solution)/shard_map/ppermute | solution.py:505
  58.2 1.1 %collective-permute-start.16 = (bf16[64,1280]{1,0:T(8,128)(2,1)S(1)}, bf16[64,1280]{1,0:T(8,128)(2,1)S(1)}, u32[]{:S(2)}, u32[]{:S(2)}) collective-permute-start(bf16[64,1280]{1,0:T(8,128)(2,1)S(1)} %project.5), channel_id=1, source_target_pairs={{0,1},{1,0},{2,3},{3,2},{4,5},{5,4},{6,7},{7,6},{8,9},{9,8},{10,11... | collective-permute-start | bytes 491528 | tf_op jit(solution)/shard_map/ppermute | solution.py:509
  59.3 3.8 %project.4.own_ref = f32[64,2560]{1,0:T(8,128)S(1)} custom-call(s32[1]{0:T(128)} %bitcast.device_ref, bf16[1536,5120]{1,0:T(8,128)(2,1)} %weight_ref.7, bf16[64,1536]{1,0:T(8,128)(2,1)S(1)} %get-tuple-element.38.both_ref), custom_call_target="tpu_custom_call" | custom-call | flops 503316480 | bytes 7864320 | tf_op jit(solution)/shard_map/project/pallas_call | solution.py:311
  63.9 1.0 %collective-permute-done.16.received_ref = bf16[64,1280]{1,0:T(8,128)(2,1)S(1)} collective-permute-done((bf16[64,1280]{1,0:T(8,128)(2,1)S(1)}, bf16[64,1280]{1,0:T(8,128)(2,1)S(1)}, u32[]{:S(2)}, u32[]{:S(2)}) %collective-permute-start.16) | collective-permute-done | bytes 163872 | tf_op jit(solution)/shard_map/ppermute | solution.py:509
  (26 shorter events, 8.3 us)
Async XLA Ops:
  2.9 16.5 %collective-permute-start.1 = (bf16[3,4,64,384]{3,2,1,0:T(8,128)(2,1)S(1)}, bf16[3,4,64,384]{3,2,1,0:T(8,128)(2,1)S(1)}, u32[]{:S(2)}, u32[]{:S(2)}) collective-permute-start(bf16[3,4,64,384]{3,2,1,0:T(8,128)(2,1)S(1)} %get-tuple-element.25), channel_id=1, source_target_pairs={{0,2},{2,0},{1,3},{3,1},{4,6},{6,4},{5,7},{7,5},{8,10},{10,8},{9,1... | collective-permute-start | bytes 1769480 | tf_op jit(solution)/shard_map/ppermute | solution.py:464
  3.4 13.4 %all-to-all-start = ((bf16[8,2,16,384]{3,2,1,0:T(8,128)(2,1)}), bf16[8,2,16,384]{3,2,1,0:T(8,128)(2,1)S(1)}, u32[]{:S(2)}, u32[]{:S(2)}) async-start(bf16[8,2,16,384]{3,2,1,0:T(8,128)(2,1)} %get-tuple-element.23), calls=%async_computation | async-start | bytes 393216 | tf_op jit(solution)/shard_map/all_to_all | solution.py:448
  9.2 16.2 %collective-permute-start.5 = (bf16[4,64,384]{2,1,0:T(8,128)(2,1)S(1)}, bf16[4,64,384]{2,1,0:T(8,128)(2,1)S(1)}, u32[]{:S(2)}, u32[]{:S(2)}) collective-permute-start(bf16[4,64,384]{2,1,0:T(8,128)(2,1)S(1)} %get-tuple-element.29), channel_id=1, source_target_pairs={{0,13},{1,12},{4,9},{5,8},{8,5},{9,4},{12,1},{13,0},{2,15},{3,14},... | collective-permute-start | bytes 589832 | tf_op jit(solution)/shard_map/ppermute | solution.py:470
  16.8 10.4 %collective-permute-start = (bf16[8,2,16,384]{3,2,1,0:T(8,128)(2,1)S(1)}, bf16[8,2,16,384]{3,2,1,0:T(8,128)(2,1)S(1)}, u32[]{:S(2)}, u32[]{:S(2)}) collective-permute-start(bf16[8,2,16,384]{3,2,1,0:T(8,128)(2,1)S(1)} %all-to-all-done), channel_id=1, source_target_pairs={{0,16},{16,0},{1,17},{17,1},{2,18},{18,2},{3,19},{19,3},{4,20},{20... | collective-permute-start | bytes 589832 | tf_op jit(solution)/shard_map/ppermute | solution.py:472
  19.5 11.0 %collective-permute-start.2 = (bf16[4,128,384]{2,1,0:T(8,128)(2,1)S(1)}, bf16[4,128,384]{2,1,0:T(8,128)(2,1)S(1)}, u32[]{:S(2)}, u32[]{:S(2)}) collective-permute-start(bf16[4,128,384]{2,1,0:T(8,128)(2,1)S(1)} %get-tuple-element.26), channel_id=1, source_target_pairs={{0,4},{2,11},{1,5},{3,10},{4,0},{6,15},{5,1},{7,14},{8,12},{10,3},... | collective-permute-start | bytes 1179656 | tf_op jit(solution)/shard_map/ppermute | solution.py:467
  19.6 15.1 %collective-permute-start.3 = (bf16[4,128,384]{2,1,0:T(8,128)(2,1)S(1)}, bf16[4,128,384]{2,1,0:T(8,128)(2,1)S(1)}, u32[]{:S(2)}, u32[]{:S(2)}) collective-permute-start(bf16[4,128,384]{2,1,0:T(8,128)(2,1)S(1)} %get-tuple-element.27), channel_id=1, source_target_pairs={{0,1},{2,14},{1,0},{3,15},{4,5},{6,10},{5,4},{7,11},{8,9},{10,6},{... | collective-permute-start | bytes 1179656 | tf_op jit(solution)/shard_map/ppermute | solution.py:467
  20.2 14.5 %collective-permute-start.4 = (bf16[4,128,384]{2,1,0:T(8,128)(2,1)S(1)}, bf16[4,128,384]{2,1,0:T(8,128)(2,1)S(1)}, u32[]{:S(2)}, u32[]{:S(2)}) collective-permute-start(bf16[4,128,384]{2,1,0:T(8,128)(2,1)S(1)} %get-tuple-element.28), channel_id=1, source_target_pairs={{0,8},{2,7},{1,9},{3,6},{4,12},{6,3},{5,13},{7,2},{8,0},{10,15},{9... | collective-permute-start | bytes 1179656 | tf_op jit(solution)/shard_map/ppermute | solution.py:467
  25.3 5.2 %collective-permute-start.6 = (bf16[1,8,2,16,384]{4,3,2,1,0:T(8,128)(2,1)S(1)}, bf16[1,8,2,16,384]{4,3,2,1,0:T(8,128)(2,1)S(1)}, u32[]{:S(2)}, u32[]{:S(2)}) collective-permute-start(bf16[1,8,2,16,384]{4,3,2,1,0:T(8,128)(2,1)S(1)} %bitcast.7), channel_id=1, source_target_pairs={{0,2},{2,0},{1,3},{3,1},{4,6},{6,4},{5,7},{7,5},{8,10},{10,8},{9,1... | collective-permute-start | bytes 589832 | tf_op jit(solution)/shard_map/ppermute | solution.py:475
  27.2 3.3 %collective-permute-start.7 = (bf16[1,8,2,16,384]{4,3,2,1,0:T(8,128)(2,1)S(1)}, bf16[1,8,2,16,384]{4,3,2,1,0:T(8,128)(2,1)S(1)}, u32[]{:S(2)}, u32[]{:S(2)}) collective-permute-start(bf16[1,8,2,16,384]{4,3,2,1,0:T(8,128)(2,1)S(1)} %bitcast.10), channel_id=1, source_target_pairs={{0,2},{2,0},{1,3},{3,1},{4,6},{6,4},{5,7},{7,5},{8,10},{10,8},{9,1... | collective-permute-start | bytes 589832 | tf_op jit(solution)/shard_map/ppermute | solution.py:475
  36.2 3.9 %collective-permute-start.8 = (bf16[8,32,896]{2,1,0:T(8,128)(2,1)S(1)}, bf16[8,32,896]{2,1,0:T(8,128)(2,1)S(1)}, u32[]{:S(2)}, u32[]{:S(2)}) collective-permute-start(bf16[8,32,896]{2,1,0:T(8,128)(2,1)S(1)} %bitcast.9), channel_id=1, source_target_pairs={{0,2},{2,0},{1,3},{3,1},{4,6},{6,4},{5,7},{7,5},{8,10},{10,8},{9,1... | collective-permute-start | bytes 1376264 | tf_op jit(solution)/shard_map/ppermute | solution.py:486
  40.9 8.3 %collective-permute-start.12 = (bf16[208,128]{1,0:T(8,128)(2,1)S(1)}, bf16[208,128]{1,0:T(8,128)(2,1)S(1)}, u32[]{:S(2)}, u32[]{:S(2)}) collective-permute-start(bf16[208,128]{1,0:T(8,128)(2,1)S(1)} %get-tuple-element.34), channel_id=1, source_target_pairs={{0,16},{4,20},{8,24},{12,28},{16,0},{20,4},{24,8},{28,12},{1,17},{... | collective-permute-start | bytes 159752 | tf_op jit(solution)/shard_map/ppermute | solution.py:494
  42.6 7.4 %collective-permute-start.13 = (bf16[208,128]{1,0:T(8,128)(2,1)S(1)}, bf16[208,128]{1,0:T(8,128)(2,1)S(1)}, u32[]{:S(2)}, u32[]{:S(2)}) collective-permute-start(bf16[208,128]{1,0:T(8,128)(2,1)S(1)} %get-tuple-element.35), channel_id=1, source_target_pairs={{0,24},{4,28},{8,16},{12,20},{16,8},{20,12},{24,0},{28,4},{1,25},{... | collective-permute-start | bytes 159752 | tf_op jit(solution)/shard_map/ppermute | solution.py:494
  43.8 9.3 %collective-permute-start.14 = (bf16[208,128]{1,0:T(8,128)(2,1)S(1)}, bf16[208,128]{1,0:T(8,128)(2,1)S(1)}, u32[]{:S(2)}, u32[]{:S(2)}) collective-permute-start(bf16[208,128]{1,0:T(8,128)(2,1)S(1)} %get-tuple-element.36), channel_id=1, source_target_pairs={{0,20},{4,16},{8,28},{12,24},{16,4},{20,0},{24,12},{28,8},{1,21},{... | collective-permute-start | bytes 159752 | tf_op jit(solution)/shard_map/ppermute | solution.py:494
  45.3 7.8 %collective-permute-start.15 = (bf16[208,128]{1,0:T(8,128)(2,1)S(1)}, bf16[208,128]{1,0:T(8,128)(2,1)S(1)}, u32[]{:S(2)}, u32[]{:S(2)}) collective-permute-start(bf16[208,128]{1,0:T(8,128)(2,1)S(1)} %get-tuple-element.37), channel_id=1, source_target_pairs={{0,28},{4,24},{8,20},{12,16},{16,12},{20,8},{24,4},{28,0},{1,29},{... | collective-permute-start | bytes 159752 | tf_op jit(solution)/shard_map/ppermute | solution.py:494
  48.5 5.5 %collective-permute-start.9 = (bf16[208,128]{1,0:T(8,128)(2,1)S(1)}, bf16[208,128]{1,0:T(8,128)(2,1)S(1)}, u32[]{:S(2)}, u32[]{:S(2)}) collective-permute-start(bf16[208,128]{1,0:T(8,128)(2,1)S(1)} %get-tuple-element.30), channel_id=1, source_target_pairs={{0,4},{4,0},{8,12},{12,8},{16,20},{20,16},{24,28},{28,24},{1,5},{5... | collective-permute-start | bytes 159752 | tf_op jit(solution)/shard_map/ppermute | solution.py:494
  49.2 4.8 %collective-permute-start.10 = (bf16[208,128]{1,0:T(8,128)(2,1)S(1)}, bf16[208,128]{1,0:T(8,128)(2,1)S(1)}, u32[]{:S(2)}, u32[]{:S(2)}) collective-permute-start(bf16[208,128]{1,0:T(8,128)(2,1)S(1)} %get-tuple-element.31), channel_id=1, source_target_pairs={{0,8},{4,12},{8,0},{12,4},{16,24},{20,28},{24,16},{28,20},{1,9},{5... | collective-permute-start | bytes 159752 | tf_op jit(solution)/shard_map/ppermute | solution.py:494
  50.1 5.0 %collective-permute-start.11 = (bf16[208,128]{1,0:T(8,128)(2,1)S(1)}, bf16[208,128]{1,0:T(8,128)(2,1)S(1)}, u32[]{:S(2)}, u32[]{:S(2)}) collective-permute-start(bf16[208,128]{1,0:T(8,128)(2,1)S(1)} %get-tuple-element.32), channel_id=1, source_target_pairs={{0,12},{4,8},{8,4},{12,0},{16,28},{20,24},{24,20},{28,16},{1,13},{... | collective-permute-start | bytes 159752 | tf_op jit(solution)/shard_map/ppermute | solution.py:494
  56.4 6.8 %collective-permute-start.17 = (bf16[64,1280]{1,0:T(8,128)(2,1)S(1)}, bf16[64,1280]{1,0:T(8,128)(2,1)S(1)}, u32[]{:S(2)}, u32[]{:S(2)}) collective-permute-start(bf16[64,1280]{1,0:T(8,128)(2,1)S(1)} %get-tuple-element.39), channel_id=1, source_target_pairs={{0,1},{1,0},{2,3},{3,2},{4,5},{5,4},{6,7},{7,6},{8,9},{9,8},{10,11... | collective-permute-start | bytes 491528 | tf_op jit(solution)/shard_map/ppermute | solution.py:505
  58.2 6.7 %collective-permute-start.16 = (bf16[64,1280]{1,0:T(8,128)(2,1)S(1)}, bf16[64,1280]{1,0:T(8,128)(2,1)S(1)}, u32[]{:S(2)}, u32[]{:S(2)}) collective-permute-start(bf16[64,1280]{1,0:T(8,128)(2,1)S(1)} %project.5), channel_id=1, source_target_pairs={{0,1},{1,0},{2,3},{3,2},{4,5},{5,4},{6,7},{7,6},{8,9},{9,8},{10,11... | collective-permute-start | bytes 491528 | tf_op jit(solution)/shard_map/ppermute | solution.py:509

commit v10 on v9

--- a/solution.py
+++ b/solution.py
@@ -11,7 +11,7 @@
 H = 24
 DH = 128
 NT = (((1,), (1,)), ((), ()))
-PART_TURNS = (4, 6, 5, 7, 1, 2, 3, 0)
+PART_TURNS = (4, 5, 6, 7, 2, 1, 3, 0)
 SPLIT = 4
 TURNS = (2, 1, 4)
 FAR = 7

time: 65.8 us -> 66.3 us (level)
    ppermute x1, starting transfers between devices: 1.01 us -> 2.05 us  [local(): received = [lax.ppermute(sent, 'head', swap)]]
    ppermute x1, starting transfers between devices: 1.15 us -> 0.1 us  [local(): received.append(lax.ppermute(sent, 'head', swap))]
  transfers between devices with their start and end apart: 19 -> 19, of which waited for: 8 -> 10; matrix products, arithmetic and copies ran while one was open for 0% -> 0% of each run, Pallas kernels for 17% -> 17%
where the time goes in v10:
time: 66.3 us; the launch traced here: 66 us
  starting transfers between devices  29.3 us (44%)
  waiting for transfers between devices  18.5 us (28%)
  Pallas kernels  17.5 us (26%)
  between operations  0.77 us (1%)
    ppermute x7, starting transfers between devices, local(): lax.ppermute(part, ('k', 'g'), [(i, i ^ d) for i in range(count)])  10.5 us
    pallas_call x3, Pallas kernels, project(): pl.pallas_call(kernel, out_shape=outs, in_specs=[scalar, pl.BlockSpec(mem...  5.89 us
    all_to_all x1, starting transfers between devices, within_plane(): lax.all_to_all(x, plane_axes, split_axis=0, concat_axis=0, tiled=True)  5.76 us
    ppermute x1, waiting for transfers between devices, local(): lax.ppermute(far, ('g', 'head'), [(i, i ^ FAR) for i in range(group)])  4.3 us
    ppermute x3, waiting for transfers between devices, local(): lax.ppermute(piece, ('g', 'core', 'head'), across_chips(turn, g_count, he...  4.14 us
    ppermute x1, starting transfers between devices, local(): lax.ppermute(far, ('g', 'head'), [(i, i ^ FAR) for i in range(group)])  3.82 us
    all_to_all x1, waiting for transfers between devices, within_plane(): lax.all_to_all(x, plane_axes, split_axis=0, concat_axis=0, tiled=True)  3.82 us
    ppermute x7, waiting for transfers between devices, local(): lax.ppermute(part, ('k', 'g'), [(i, i ^ d) for i in range(count)])  3.67 us
  transfers between devices with their start and end apart: 19, of which 10 were waited for; matrix products, arithmetic and copies ran while one was open for 0% of the time, Pallas kernels for 17%

profile of v10, /device:TPU:0, one launch (start us, length us, event | category | flops | bytes accessed | tf_op | source)
XLA Modules:
  0.0 66.0 jit_solution(1703560617909699888)
XLA Ops:
  0.6 2.2 %pack.1 = (bf16[8,2,16,384]{3,2,1,0:T(8,128)(2,1)}, bf16[4,64,384]{2,1,0:T(8,128)(2,1)S(1)}, bf16[4,64,384]{2,1,0:T(8,128)(2,1)S(1)}, bf16[3,4,64,384]{3,2,1,0:T(8,128)(2,1)S(1)}, bf16[3,4,64,384]{3,2,1,0:T(8,128)(2,1)S(1)}) custom-call(s32[1]{0:T(128)} %bitcast.device_ref, bf16[16,3072]{1,0:T(8,128)(2,1)} %refs_0_.1, bf16[16,3072]{1,0:T(8,128)(2,1)} %refs_1_.1, ...), custom_call_target="tpu_custom_call" | custom-call | tf_op jit(solution)/shard_map/pack/pallas_call | solution.py:361
  3.4 5.8 %all-to-all-start = ((bf16[8,2,16,384]{3,2,1,0:T(8,128)(2,1)}), bf16[8,2,16,384]{3,2,1,0:T(8,128)(2,1)S(1)}, u32[]{:S(2)}, u32[]{:S(2)}) async-start(bf16[8,2,16,384]{3,2,1,0:T(8,128)(2,1)} %get-tuple-element.23), calls=%async_computation | async-start | bytes 393216 | tf_op jit(solution)/shard_map/all_to_all | solution.py:448
  9.2 3.8 %collective-permute-start.5 = (bf16[4,64,384]{2,1,0:T(8,128)(2,1)S(1)}, bf16[4,64,384]{2,1,0:T(8,128)(2,1)S(1)}, u32[]{:S(2)}, u32[]{:S(2)}) collective-permute-start(bf16[4,64,384]{2,1,0:T(8,128)(2,1)S(1)} %get-tuple-element.29), channel_id=1, source_target_pairs={{0,13},{1,12},{4,9},{5,8},{8,5},{9,4},{12,1},{13,0},{2,15},{3,14},... | collective-permute-start | bytes 589832 | tf_op jit(solution)/shard_map/ppermute | solution.py:470
  13.0 3.8 %all-to-all-done = bf16[8,2,16,384]{3,2,1,0:T(8,128)(2,1)S(1)} async-done(((bf16[8,2,16,384]{3,2,1,0:T(8,128)(2,1)}), bf16[8,2,16,384]{3,2,1,0:T(8,128)(2,1)S(1)}, u32[]{:S(2)}, u32[]{:S(2)}) %all-to-all-start) | async-done | bytes 196640 | tf_op jit(solution)/shard_map/all_to_all | solution.py:448
  16.8 2.6 %collective-permute-start = (bf16[8,2,16,384]{3,2,1,0:T(8,128)(2,1)S(1)}, bf16[8,2,16,384]{3,2,1,0:T(8,128)(2,1)S(1)}, u32[]{:S(2)}, u32[]{:S(2)}) collective-permute-start(bf16[8,2,16,384]{3,2,1,0:T(8,128)(2,1)S(1)} %all-to-all-done), channel_id=1, source_target_pairs={{0,16},{16,0},{1,17},{17,1},{2,18},{18,2},{3,19},{19,3},{4,20},{20... | collective-permute-start | bytes 589832 | tf_op jit(solution)/shard_map/ppermute | solution.py:472
  20.2 0.8 %collective-permute-start.4 = (bf16[4,128,384]{2,1,0:T(8,128)(2,1)S(1)}, bf16[4,128,384]{2,1,0:T(8,128)(2,1)S(1)}, u32[]{:S(2)}, u32[]{:S(2)}) collective-permute-start(bf16[4,128,384]{2,1,0:T(8,128)(2,1)S(1)} %get-tuple-element.28), channel_id=1, source_target_pairs={{0,8},{2,7},{1,9},{3,6},{4,12},{6,3},{5,13},{7,2},{8,0},{10,15},{9... | collective-permute-start | bytes 1179656 | tf_op jit(solution)/shard_map/ppermute | solution.py:467
  21.0 4.3 %collective-permute-done.5.refs_6_ = bf16[4,64,384]{2,1,0:T(8,128)(2,1)S(1)} collective-permute-done((bf16[4,64,384]{2,1,0:T(8,128)(2,1)S(1)}, bf16[4,64,384]{2,1,0:T(8,128)(2,1)S(1)}, u32[]{:S(2)}, u32[]{:S(2)}) %collective-permute-start.5) | collective-permute-done | bytes 196640 | tf_op jit(solution)/shard_map/ppermute | solution.py:470
  25.3 1.8 %collective-permute-done = bf16[8,2,16,384]{3,2,1,0:T(8,128)(2,1)S(1)} collective-permute-done((bf16[8,2,16,384]{3,2,1,0:T(8,128)(2,1)S(1)}, bf16[8,2,16,384]{3,2,1,0:T(8,128)(2,1)S(1)}, u32[]{:S(2)}, u32[]{:S(2)}) %collective-permute-start) | collective-permute-done | bytes 196640 | tf_op jit(solution)/shard_map/ppermute | solution.py:472
  27.2 3.3 %hold.1.after_ref.refs_8_.held_ref = bf16[1536,2560]{1,0:T(8,128)(2,1)S(1)} custom-call(s32[1]{0:T(128)} %bitcast.device_ref, bf16[1536,5120]{1,0:T(8,128)(2,1)} %weight_ref.7, bf16[4,64,384]{2,1,0:T(8,128)(2,1)S(1)} %get-tuple-element.22.after_ref.refs_2_), custom_call_target="tpu_custom_call" | custom-call | bytes 7864320 | tf_op jit(solution)/shard_map/hold/pallas_call | solution.py:427
  30.5 4.1 %collective-permute-done.3.refs_4_ = bf16[4,128,384]{2,1,0:T(8,128)(2,1)S(1)} collective-permute-done((bf16[4,128,384]{2,1,0:T(8,128)(2,1)S(1)}, bf16[4,128,384]{2,1,0:T(8,128)(2,1)S(1)}, u32[]{:S(2)}, u32[]{:S(2)}) %collective-permute-start.3) | collective-permute-done | bytes 393248 | tf_op jit(solution)/shard_map/ppermute | solution.py:467
  34.7 1.5 %attend.3 = bf16[2,4,32,896]{3,2,1,0:T(8,128)(2,1)S(1)} custom-call(s32[1]{0:T(128)} %bitcast.device_ref, bf16[1536,2560]{1,0:T(8,128)(2,1)S(1)} %hold.1.after_ref.refs_8_.held_ref, bf16[1,8,2,16,384]{4,3,2,1,0:T(8,128)(2,1)S(1)} %collective-permute-done.6.refs_0_, bf16[1,8,2,16,384]{4,3,2,1,0:T(8,128)(2,1)S(1)} %collective-permute-done.7.refs_1_, ...), custom_call_target="tpu_custom_call" | custom-call | tf_op jit(solution)/shard_map/attend/pallas_call | solution.py:119
  36.2 2.4 %collective-permute-start.8 = (bf16[8,32,896]{2,1,0:T(8,128)(2,1)S(1)}, bf16[8,32,896]{2,1,0:T(8,128)(2,1)S(1)}, u32[]{:S(2)}, u32[]{:S(2)}) collective-permute-start(bf16[8,32,896]{2,1,0:T(8,128)(2,1)S(1)} %bitcast.9), channel_id=1, source_target_pairs={{0,2},{2,0},{1,3},{3,1},{4,6},{6,4},{5,7},{7,5},{8,10},{10,8},{9,1... | collective-permute-start | bytes 1376264 | tf_op jit(solution)/shard_map/ppermute | solution.py:486
  38.6 1.5 %attend.2 = bf16[2,4,32,896]{3,2,1,0:T(8,128)(2,1)S(1)} custom-call(s32[1]{0:T(128)} %bitcast.device_ref, bf16[1536,2560]{1,0:T(8,128)(2,1)S(1)} %hold.1.after_ref.refs_8_.held_ref, bf16[1,8,2,16,384]{4,3,2,1,0:T(8,128)(2,1)S(1)} %bitcast.8, bf16[1,8,2,16,384]{4,3,2,1,0:T(8,128)(2,1)S(1)} %bitcast.11, ...), custom_call_target="tpu_custom_call" | custom-call | tf_op jit(solution)/shard_map/attend/pallas_call | solution.py:119
  40.1 0.8 %merge_pair.3 = (bf16[208,128]{1,0:T(8,128)(2,1)S(1)}, bf16[208,128]{1,0:T(8,128)(2,1)S(1)}, bf16[208,128]{1,0:T(8,128)(2,1)S(1)}, bf16[208,128]{1,0:T(8,128)(2,1)S(1)}) custom-call(s32[1]{0:T(128)} %bitcast.device_ref, bf16[8,32,896]{2,1,0:T(8,128)(2,1)S(1)} %bitcast.5, bf16[8,32,896]{2,1,0:T(8,128)(2,1)S(1)} %collective-permute-done.8.away_ref), custom_call_target="tpu_custom_call" | custom-call | tf_op jit(solution)/shard_map/merge_pair/pallas_call | solution.py:212
  40.9 1.8 %collective-permute-start.12 = (bf16[208,128]{1,0:T(8,128)(2,1)S(1)}, bf16[208,128]{1,0:T(8,128)(2,1)S(1)}, u32[]{:S(2)}, u32[]{:S(2)}) collective-permute-start(bf16[208,128]{1,0:T(8,128)(2,1)S(1)} %get-tuple-element.34), channel_id=1, source_target_pairs={{0,16},{4,20},{8,24},{12,28},{16,0},{20,4},{24,8},{28,12},{1,17},{... | collective-permute-start | bytes 159752 | tf_op jit(solution)/shard_map/ppermute | solution.py:494
  42.6 1.3 %collective-permute-start.13 = (bf16[208,128]{1,0:T(8,128)(2,1)S(1)}, bf16[208,128]{1,0:T(8,128)(2,1)S(1)}, u32[]{:S(2)}, u32[]{:S(2)}) collective-permute-start(bf16[208,128]{1,0:T(8,128)(2,1)S(1)} %get-tuple-element.35), channel_id=1, source_target_pairs={{0,20},{4,16},{8,28},{12,24},{16,4},{20,0},{24,12},{28,8},{1,21},{... | collective-permute-start | bytes 159752 | tf_op jit(solution)/shard_map/ppermute | solution.py:494
  43.9 2.3 %collective-permute-start.14 = (bf16[208,128]{1,0:T(8,128)(2,1)S(1)}, bf16[208,128]{1,0:T(8,128)(2,1)S(1)}, u32[]{:S(2)}, u32[]{:S(2)}) collective-permute-start(bf16[208,128]{1,0:T(8,128)(2,1)S(1)} %get-tuple-element.36), channel_id=1, source_target_pairs={{0,24},{4,28},{8,16},{12,20},{16,8},{20,12},{24,0},{28,4},{1,25},{... | collective-permute-start | bytes 159752 | tf_op jit(solution)/shard_map/ppermute | solution.py:494
  46.2 2.4 %collective-permute-start.15 = (bf16[208,128]{1,0:T(8,128)(2,1)S(1)}, bf16[208,128]{1,0:T(8,128)(2,1)S(1)}, u32[]{:S(2)}, u32[]{:S(2)}) collective-permute-start(bf16[208,128]{1,0:T(8,128)(2,1)S(1)} %get-tuple-element.37), channel_id=1, source_target_pairs={{0,28},{4,24},{8,20},{12,16},{16,12},{20,8},{24,4},{28,0},{1,29},{... | collective-permute-start | bytes 159752 | tf_op jit(solution)/shard_map/ppermute | solution.py:494
  50.8 2.1 %collective-permute-start.11 = (bf16[208,128]{1,0:T(8,128)(2,1)S(1)}, bf16[208,128]{1,0:T(8,128)(2,1)S(1)}, u32[]{:S(2)}, u32[]{:S(2)}) collective-permute-start(bf16[208,128]{1,0:T(8,128)(2,1)S(1)} %get-tuple-element.32), channel_id=1, source_target_pairs={{0,12},{4,8},{8,4},{12,0},{16,28},{20,24},{24,20},{28,16},{1,13},{... | collective-permute-start | bytes 159752 | tf_op jit(solution)/shard_map/ppermute | solution.py:494
  54.3 1.6 %collective-permute-done.11.refs_2_ = bf16[208,128]{1,0:T(8,128)(2,1)S(1)} collective-permute-done((bf16[208,128]{1,0:T(8,128)(2,1)S(1)}, bf16[208,128]{1,0:T(8,128)(2,1)S(1)}, u32[]{:S(2)}, u32[]{:S(2)}) %collective-permute-start.11) | collective-permute-done | bytes 53280 | tf_op jit(solution)/shard_map/ppermute | solution.py:494
  55.9 1.2 %project.3 = (bf16[64,1280]{1,0:T(8,128)(2,1)S(1)}, bf16[64,1536]{1,0:T(8,128)(2,1)S(1)}) custom-call(s32[1]{0:T(128)} %bitcast.device_ref, bf16[1536,5120]{1,0:T(8,128)(2,1)} %weight_ref.7, bf16[208,128]{1,0:T(8,128)(2,1)S(1)} %collective-permute-done.9.refs_0_, bf16[208,128]{1,0:T(8,128)(2,1)S(1)} %collective-permute-done.10.refs_1_, ...), custom_call_target="tpu_custom_call" | custom-call | flops 251658240 | bytes 3932160 | tf_op jit(solution)/shard_map/project/pallas_call | solution.py:311
  57.1 2.1 %collective-permute-start.17 = (bf16[64,1280]{1,0:T(8,128)(2,1)S(1)}, bf16[64,1280]{1,0:T(8,128)(2,1)S(1)}, u32[]{:S(2)}, u32[]{:S(2)}) collective-permute-start(bf16[64,1280]{1,0:T(8,128)(2,1)S(1)} %get-tuple-element.39), channel_id=1, source_target_pairs={{0,1},{1,0},{2,3},{3,2},{4,5},{5,4},{6,7},{7,6},{8,9},{9,8},{10,11... | collective-permute-start | bytes 491528 | tf_op jit(solution)/shard_map/ppermute | solution.py:505
  59.2 0.8 %project.5 = bf16[64,1280]{1,0:T(8,128)(2,1)S(1)} custom-call(s32[1]{0:T(128)} %bitcast.device_ref, bf16[1536,5120]{1,0:T(8,128)(2,1)} %weight_ref.7, bf16[64,1536]{1,0:T(8,128)(2,1)S(1)} %get-tuple-element.38.both_ref, bf16[1536,2560]{1,0:T(8,128)(2,1)S(1)} %hold.1.after_ref.refs_8_.held_ref), custom_call_target="tpu_custom_call" | custom-call | flops 251658240 | bytes 3932160 | tf_op jit(solution)/shard_map/project/pallas_call | solution.py:311
  60.1 3.8 %project.4.own_ref = f32[64,2560]{1,0:T(8,128)S(1)} custom-call(s32[1]{0:T(128)} %bitcast.device_ref, bf16[1536,5120]{1,0:T(8,128)(2,1)} %weight_ref.7, bf16[64,1536]{1,0:T(8,128)(2,1)S(1)} %get-tuple-element.38.both_ref), custom_call_target="tpu_custom_call" | custom-call | flops 503316480 | bytes 7864320 | tf_op jit(solution)/shard_map/project/pallas_call | solution.py:311
  (26 shorter events, 7.2 us)
Async XLA Ops:
  2.9 16.5 %collective-permute-start.1 = (bf16[3,4,64,384]{3,2,1,0:T(8,128)(2,1)S(1)}, bf16[3,4,64,384]{3,2,1,0:T(8,128)(2,1)S(1)}, u32[]{:S(2)}, u32[]{:S(2)}) collective-permute-start(bf16[3,4,64,384]{3,2,1,0:T(8,128)(2,1)S(1)} %get-tuple-element.25), channel_id=1, source_target_pairs={{0,2},{2,0},{1,3},{3,1},{4,6},{6,4},{5,7},{7,5},{8,10},{10,8},{9,1... | collective-permute-start | bytes 1769480 | tf_op jit(solution)/shard_map/ppermute | solution.py:464
  3.4 13.4 %all-to-all-start = ((bf16[8,2,16,384]{3,2,1,0:T(8,128)(2,1)}), bf16[8,2,16,384]{3,2,1,0:T(8,128)(2,1)S(1)}, u32[]{:S(2)}, u32[]{:S(2)}) async-start(bf16[8,2,16,384]{3,2,1,0:T(8,128)(2,1)} %get-tuple-element.23), calls=%async_computation | async-start | bytes 393216 | tf_op jit(solution)/shard_map/all_to_all | solution.py:448
  9.2 16.2 %collective-permute-start.5 = (bf16[4,64,384]{2,1,0:T(8,128)(2,1)S(1)}, bf16[4,64,384]{2,1,0:T(8,128)(2,1)S(1)}, u32[]{:S(2)}, u32[]{:S(2)}) collective-permute-start(bf16[4,64,384]{2,1,0:T(8,128)(2,1)S(1)} %get-tuple-element.29), channel_id=1, source_target_pairs={{0,13},{1,12},{4,9},{5,8},{8,5},{9,4},{12,1},{13,0},{2,15},{3,14},... | collective-permute-start | bytes 589832 | tf_op jit(solution)/shard_map/ppermute | solution.py:470
  16.8 10.4 %collective-permute-start = (bf16[8,2,16,384]{3,2,1,0:T(8,128)(2,1)S(1)}, bf16[8,2,16,384]{3,2,1,0:T(8,128)(2,1)S(1)}, u32[]{:S(2)}, u32[]{:S(2)}) collective-permute-start(bf16[8,2,16,384]{3,2,1,0:T(8,128)(2,1)S(1)} %all-to-all-done), channel_id=1, source_target_pairs={{0,16},{16,0},{1,17},{17,1},{2,18},{18,2},{3,19},{19,3},{4,20},{20... | collective-permute-start | bytes 589832 | tf_op jit(solution)/shard_map/ppermute | solution.py:472
  19.5 11.0 %collective-permute-start.2 = (bf16[4,128,384]{2,1,0:T(8,128)(2,1)S(1)}, bf16[4,128,384]{2,1,0:T(8,128)(2,1)S(1)}, u32[]{:S(2)}, u32[]{:S(2)}) collective-permute-start(bf16[4,128,384]{2,1,0:T(8,128)(2,1)S(1)} %get-tuple-element.26), channel_id=1, source_target_pairs={{0,4},{2,11},{1,5},{3,10},{4,0},{6,15},{5,1},{7,14},{8,12},{10,3},... | collective-permute-start | bytes 1179656 | tf_op jit(solution)/shard_map/ppermute | solution.py:467
  19.6 15.1 %collective-permute-start.3 = (bf16[4,128,384]{2,1,0:T(8,128)(2,1)S(1)}, bf16[4,128,384]{2,1,0:T(8,128)(2,1)S(1)}, u32[]{:S(2)}, u32[]{:S(2)}) collective-permute-start(bf16[4,128,384]{2,1,0:T(8,128)(2,1)S(1)} %get-tuple-element.27), channel_id=1, source_target_pairs={{0,1},{2,14},{1,0},{3,15},{4,5},{6,10},{5,4},{7,11},{8,9},{10,6},{... | collective-permute-start | bytes 1179656 | tf_op jit(solution)/shard_map/ppermute | solution.py:467
  20.2 14.5 %collective-permute-start.4 = (bf16[4,128,384]{2,1,0:T(8,128)(2,1)S(1)}, bf16[4,128,384]{2,1,0:T(8,128)(2,1)S(1)}, u32[]{:S(2)}, u32[]{:S(2)}) collective-permute-start(bf16[4,128,384]{2,1,0:T(8,128)(2,1)S(1)} %get-tuple-element.28), channel_id=1, source_target_pairs={{0,8},{2,7},{1,9},{3,6},{4,12},{6,3},{5,13},{7,2},{8,0},{10,15},{9... | collective-permute-start | bytes 1179656 | tf_op jit(solution)/shard_map/ppermute | solution.py:467
  25.3 5.2 %collective-permute-start.6 = (bf16[1,8,2,16,384]{4,3,2,1,0:T(8,128)(2,1)S(1)}, bf16[1,8,2,16,384]{4,3,2,1,0:T(8,128)(2,1)S(1)}, u32[]{:S(2)}, u32[]{:S(2)}) collective-permute-start(bf16[1,8,2,16,384]{4,3,2,1,0:T(8,128)(2,1)S(1)} %bitcast.7), channel_id=1, source_target_pairs={{0,2},{2,0},{1,3},{3,1},{4,6},{6,4},{5,7},{7,5},{8,10},{10,8},{9,1... | collective-permute-start | bytes 589832 | tf_op jit(solution)/shard_map/ppermute | solution.py:475
  27.2 3.3 %collective-permute-start.7 = (bf16[1,8,2,16,384]{4,3,2,1,0:T(8,128)(2,1)S(1)}, bf16[1,8,2,16,384]{4,3,2,1,0:T(8,128)(2,1)S(1)}, u32[]{:S(2)}, u32[]{:S(2)}) collective-permute-start(bf16[1,8,2,16,384]{4,3,2,1,0:T(8,128)(2,1)S(1)} %bitcast.10), channel_id=1, source_target_pairs={{0,2},{2,0},{1,3},{3,1},{4,6},{6,4},{5,7},{7,5},{8,10},{10,8},{9,1... | collective-permute-start | bytes 589832 | tf_op jit(solution)/shard_map/ppermute | solution.py:475
  36.2 3.9 %collective-permute-start.8 = (bf16[8,32,896]{2,1,0:T(8,128)(2,1)S(1)}, bf16[8,32,896]{2,1,0:T(8,128)(2,1)S(1)}, u32[]{:S(2)}, u32[]{:S(2)}) collective-permute-start(bf16[8,32,896]{2,1,0:T(8,128)(2,1)S(1)} %bitcast.9), channel_id=1, source_target_pairs={{0,2},{2,0},{1,3},{3,1},{4,6},{6,4},{5,7},{7,5},{8,10},{10,8},{9,1... | collective-permute-start | bytes 1376264 | tf_op jit(solution)/shard_map/ppermute | solution.py:486
  40.9 8.6 %collective-permute-start.12 = (bf16[208,128]{1,0:T(8,128)(2,1)S(1)}, bf16[208,128]{1,0:T(8,128)(2,1)S(1)}, u32[]{:S(2)}, u32[]{:S(2)}) collective-permute-start(bf16[208,128]{1,0:T(8,128)(2,1)S(1)} %get-tuple-element.34), channel_id=1, source_target_pairs={{0,16},{4,20},{8,24},{12,28},{16,0},{20,4},{24,8},{28,12},{1,17},{... | collective-permute-start | bytes 159752 | tf_op jit(solution)/shard_map/ppermute | solution.py:494
  42.6 8.2 %collective-permute-start.13 = (bf16[208,128]{1,0:T(8,128)(2,1)S(1)}, bf16[208,128]{1,0:T(8,128)(2,1)S(1)}, u32[]{:S(2)}, u32[]{:S(2)}) collective-permute-start(bf16[208,128]{1,0:T(8,128)(2,1)S(1)} %get-tuple-element.35), channel_id=1, source_target_pairs={{0,20},{4,16},{8,28},{12,24},{16,4},{20,0},{24,12},{28,8},{1,21},{... | collective-permute-start | bytes 159752 | tf_op jit(solution)/shard_map/ppermute | solution.py:494
  43.9 9.0 %collective-permute-start.14 = (bf16[208,128]{1,0:T(8,128)(2,1)S(1)}, bf16[208,128]{1,0:T(8,128)(2,1)S(1)}, u32[]{:S(2)}, u32[]{:S(2)}) collective-permute-start(bf16[208,128]{1,0:T(8,128)(2,1)S(1)} %get-tuple-element.36), channel_id=1, source_target_pairs={{0,24},{4,28},{8,16},{12,20},{16,8},{20,12},{24,0},{28,4},{1,25},{... | collective-permute-start | bytes 159752 | tf_op jit(solution)/shard_map/ppermute | solution.py:494
  46.2 6.9 %collective-permute-start.15 = (bf16[208,128]{1,0:T(8,128)(2,1)S(1)}, bf16[208,128]{1,0:T(8,128)(2,1)S(1)}, u32[]{:S(2)}, u32[]{:S(2)}) collective-permute-start(bf16[208,128]{1,0:T(8,128)(2,1)S(1)} %get-tuple-element.37), channel_id=1, source_target_pairs={{0,28},{4,24},{8,20},{12,16},{16,12},{20,8},{24,4},{28,0},{1,29},{... | collective-permute-start | bytes 159752 | tf_op jit(solution)/shard_map/ppermute | solution.py:494
  49.4 4.2 %collective-permute-start.9 = (bf16[208,128]{1,0:T(8,128)(2,1)S(1)}, bf16[208,128]{1,0:T(8,128)(2,1)S(1)}, u32[]{:S(2)}, u32[]{:S(2)}) collective-permute-start(bf16[208,128]{1,0:T(8,128)(2,1)S(1)} %get-tuple-element.30), channel_id=1, source_target_pairs={{0,8},{4,12},{8,0},{12,4},{16,24},{20,28},{24,16},{28,20},{1,9},{5... | collective-permute-start | bytes 159752 | tf_op jit(solution)/shard_map/ppermute | solution.py:494
  49.4 4.8 %collective-permute-start.10 = (bf16[208,128]{1,0:T(8,128)(2,1)S(1)}, bf16[208,128]{1,0:T(8,128)(2,1)S(1)}, u32[]{:S(2)}, u32[]{:S(2)}) collective-permute-start(bf16[208,128]{1,0:T(8,128)(2,1)S(1)} %get-tuple-element.31), channel_id=1, source_target_pairs={{0,4},{4,0},{8,12},{12,8},{16,20},{20,16},{24,28},{28,24},{1,5},{5... | collective-permute-start | bytes 159752 | tf_op jit(solution)/shard_map/ppermute | solution.py:494
  50.8 5.0 %collective-permute-start.11 = (bf16[208,128]{1,0:T(8,128)(2,1)S(1)}, bf16[208,128]{1,0:T(8,128)(2,1)S(1)}, u32[]{:S(2)}, u32[]{:S(2)}) collective-permute-start(bf16[208,128]{1,0:T(8,128)(2,1)S(1)} %get-tuple-element.32), channel_id=1, source_target_pairs={{0,12},{4,8},{8,4},{12,0},{16,28},{20,24},{24,20},{28,16},{1,13},{... | collective-permute-start | bytes 159752 | tf_op jit(solution)/shard_map/ppermute | solution.py:494
  57.1 6.8 %collective-permute-start.17 = (bf16[64,1280]{1,0:T(8,128)(2,1)S(1)}, bf16[64,1280]{1,0:T(8,128)(2,1)S(1)}, u32[]{:S(2)}, u32[]{:S(2)}) collective-permute-start(bf16[64,1280]{1,0:T(8,128)(2,1)S(1)} %get-tuple-element.39), channel_id=1, source_target_pairs={{0,1},{1,0},{2,3},{3,2},{4,5},{5,4},{6,7},{7,6},{8,9},{9,8},{10,11... | collective-permute-start | bytes 491528 | tf_op jit(solution)/shard_map/ppermute | solution.py:505
  60.0 5.4 %collective-permute-start.16 = (bf16[64,1280]{1,0:T(8,128)(2,1)S(1)}, bf16[64,1280]{1,0:T(8,128)(2,1)S(1)}, u32[]{:S(2)}, u32[]{:S(2)}) collective-permute-start(bf16[64,1280]{1,0:T(8,128)(2,1)S(1)} %project.5), channel_id=1, source_target_pairs={{0,1},{1,0},{2,3},{3,2},{4,5},{5,4},{6,7},{7,6},{8,9},{9,8},{10,11... | collective-permute-start | bytes 491528 | tf_op jit(solution)/shard_map/ppermute | solution.py:509
